TPU v7x, 32 devices: a whole 2x2x4 slice. The times are simulated.
32 devices in a mesh: groups: 2 (over x), ctx: 16 (over z, y, core).
Axes of the slice: x: 2, y: 2, z: 4, core: 2. Of those that a mesh axis runs over, the one named last changes fastest.
Arguments:
- index_queries: bfloat16 [64, 32, 128], P(('groups', 'ctx')), parts along dimension 0, may hold values from -0.5 to 0.5
- index_weights: bfloat16 [64, 32], P(('groups', 'ctx')), parts along dimension 0, may hold values from -1 to 1
- index_keys: bfloat16 [16384, 128], P(('groups', 'ctx')), parts along dimension 0, may hold values from -4 to 4
- key_scales: bfloat16 [16384], P(('groups', 'ctx')), parts along dimension 0, may hold values from 0.25 to 4
- q_latent: bfloat16 [64, 128, 576], P(('groups', 'ctx')), parts along dimension 0, may hold values from -6 to 6
- latents: bfloat16 [16384, 576], P(('groups', 'ctx')), parts along dimension 0, may hold values from -4 to 4
- wanted: int32 [32, 16, 4], P(('groups', 'ctx')), parts along dimension 0, may hold values from -1 to 7, as said below
- selected: int32 [64, 2048], P(('groups', 'ctx')), parts along dimension 0, may hold values from 0 to 4095, as said below
Outputs:
- index_scores: float32 [64, 8192], P(('groups', 'ctx')), parts along dimension 0
- attended: bfloat16 [64, 128, 512], P(('groups', 'ctx')), parts along dimension 0
There are 2 independent parts, one for each index of `groups`. A program takes and returns all parts, laid end to end along the dimension named above; each array names one. Nothing has to cross between parts.
Inputs may be any that keep to these rules, and one draw needn't show every extreme that they name: For each device r and owner o, the first n entries of wanted[r, o, :] are distinct block numbers of that owner, with n from 1 to 4, and the remaining entries are -1; in every draw some owner is asked for 4 blocks by every device. `selected`: the 2048 entries of a row are distinct, and each names a slot row whose block entry in wanted is not -1.
All inputs are finite; a program needn't handle non-finite values.
Results may differ from a plain program's by a relative error of at most 0.0046.
Values may be sent and summed in bfloat16 or wider, within the bound.
No kernel may reach another device: no remote copies, remote signals or barrier semaphores. Data moves between devices by JAX's collectives and lax.ppermute only.
A program may use at most 128 MiB of HBM per device.

v0:
```python
import math

import jax
import jax.numpy as jnp
from jax import lax
from jax.sharding import PartitionSpec as P

KVR = 512
BLOCK = 64


softmax_scale = 192.0 ** (-0.5)


def score_block(queries, head_weights, key_rows, scale_rows):
    raw = jnp.einsum("tjd,sd->tjs", queries, key_rows, preferred_element_type=jnp.float32)
    lifted = jax.nn.relu(raw * scale_rows.astype(jnp.float32)[None, None, :])
    return jnp.einsum(
        "tj,tjs->ts", head_weights.astype(jnp.float32), lifted, precision=lax.Precision.HIGHEST
    )


def local(
    index_queries, index_weights, index_keys, key_scales, q_latent, latents, wanted, selected
):
    rows_here = index_queries.shape[0]
    key_rows = lax.all_gather(index_keys, "ctx", axis=0, tiled=True)
    scale_rows = lax.all_gather(key_scales, "ctx", axis=0, tiled=True)
    row_count = key_rows.shape[0]
    block_size = math.gcd(row_count, 2048)

    def one_block(operands):
        return score_block(index_queries, index_weights, operands[0], operands[1])

    blocks = lax.map(
        one_block,
        (
            key_rows.reshape(row_count // block_size, block_size, key_rows.shape[1]),
            scale_rows.reshape(row_count // block_size, block_size),
        ),
    )
    columns = jnp.moveaxis(blocks, 0, 1).reshape(rows_here, row_count)
    requests = wanted[0]
    row_width = latents.shape[1]
    block_table = latents.reshape(latents.shape[0] // BLOCK, BLOCK, row_width)

    def lookup(asked):
        return jnp.take(block_table, jnp.clip(asked, 0, None), axis=0)

    def serve_slot(asked):
        return lax.all_to_all(lookup(asked), "ctx", split_axis=0, concat_axis=0, tiled=True)

    gathered_slots = [
        serve_slot(
            lax.all_to_all(
                requests[:, slot : slot + 1], "ctx", split_axis=0, concat_axis=0, tiled=True
            )
        )
        for slot in range(requests.shape[1])
    ]
    fetched = jnp.concatenate(gathered_slots, axis=1)
    buffer_rows = fetched.reshape(-1, row_width)
    slot_total = buffer_rows.shape[0]
    value_rows = buffer_rows[:, :KVR]

    def attend(operands):
        query_row, chosen = operands
        chosen_mask = jnp.zeros((slot_total,), jnp.bool_).at[chosen].set(True)
        logits = (
            lax.dot_general(
                query_row, buffer_rows, (((1,), (1,)), ((), ())), preferred_element_type=jnp.float32
            )
            * softmax_scale
        )
        logits = jnp.where(chosen_mask[None, :], logits, -jnp.inf)
        highest = jnp.max(logits, axis=1, keepdims=True)
        expo = jnp.exp(logits - highest)
        weights_low = (expo / jnp.sum(expo, axis=1, keepdims=True)).astype(jnp.bfloat16)
        return jnp.dot(weights_low, value_rows, preferred_element_type=jnp.float32).astype(
            jnp.bfloat16
        )

    attended = lax.map(attend, (q_latent, selected))
    return (columns, attended)


def solution(mesh):
    return jax.shard_map(
        local,
        mesh=mesh,
        in_specs=(
            P(("groups", "ctx"), None, None),
            P(("groups", "ctx"), None),
            P(("groups", "ctx"), None),
            P(("groups", "ctx")),
            P(("groups", "ctx"), None, None),
            P(("groups", "ctx"), None),
            P(("groups", "ctx"), None, None),
            P(("groups", "ctx"), None),
        ),
        out_specs=(P(("groups", "ctx"), None), P(("groups", "ctx"), None, None)),
        check_vma=False,
    )
```

profile of v0, /device:TPU:0, one launch (start us, length us, event | category | flops | bytes accessed | tf_op | source)
XLA Modules:
  0.0 255.5 jit_solution(11994839722847719275)
XLA Ops:
  7.2 0.8 slice_bitcast_fusion.3
  8.0 0.7 copy.27
  8.7 7.4 %all-to-all-start = ((s32[16,1,1]{2,1,0:T(1,128)}), s32[16,1,1]{2,1,0:T(1,128)S(1)}, u32[]{:S(2)}, u32[]{:S(2)}) async-start(s32[16,1,1]{2,1,0:T(1,128)} %copy.27), calls=%async_computation | async-start | bytes 16384 | tf_op jit(solution)/shard_map/all_to_all | solution.py:55
  16.1 1.4 copy.28
  17.4 0.7 copy.30
  18.1 0.7 copy.32
  18.8 0.7 copy.34
  19.5 3.0 %all-to-all-done = s32[16,1,1]{2,1,0:T(1,128)S(1)} async-done(((s32[16,1,1]{2,1,0:T(1,128)}), s32[16,1,1]{2,1,0:T(1,128)S(1)}, u32[]{:S(2)}, u32[]{:S(2)}) %all-to-all-start) | async-done | bytes 96 | tf_op jit(solution)/shard_map/all_to_all | solution.py:55
  22.5 3.5 %all-to-all-start.2 = ((s32[16,1,1]{2,1,0:T(1,128)}), s32[16,1,1]{2,1,0:T(1,128)S(1)}, u32[]{:S(2)}, u32[]{:S(2)}) async-start(s32[16,1,1]{2,1,0:T(1,128)} %copy.30), calls=%async_computation.2 | async-start | bytes 16384 | tf_op jit(solution)/shard_map/all_to_all | solution.py:55
  26.0 0.4 maximum_reduce_fusion.3
  26.4 6.0 %all-to-all-done.2 = s32[16,1,1]{2,1,0:T(1,128)S(1)} async-done(((s32[16,1,1]{2,1,0:T(1,128)}), s32[16,1,1]{2,1,0:T(1,128)S(1)}, u32[]{:S(2)}, u32[]{:S(2)}) %all-to-all-start.2) | async-done | bytes 96 | tf_op jit(solution)/shard_map/all_to_all | solution.py:55
  32.3 3.5 %all-to-all-start.4 = ((s32[16,1,1]{2,1,0:T(1,128)}), s32[16,1,1]{2,1,0:T(1,128)S(1)}, u32[]{:S(2)}, u32[]{:S(2)}) async-start(s32[16,1,1]{2,1,0:T(1,128)} %copy.32), calls=%async_computation.4 | async-start | bytes 16384 | tf_op jit(solution)/shard_map/all_to_all | solution.py:55
  35.8 0.8 gather_fusion
  36.6 5.5 %all-to-all-done.4 = s32[16,1,1]{2,1,0:T(1,128)S(1)} async-done(((s32[16,1,1]{2,1,0:T(1,128)}), s32[16,1,1]{2,1,0:T(1,128)S(1)}, u32[]{:S(2)}, u32[]{:S(2)}) %all-to-all-start.4) | async-done | bytes 96 | tf_op jit(solution)/shard_map/all_to_all | solution.py:55
  42.1 3.5 %all-to-all-start.6 = ((s32[16,1,1]{2,1,0:T(1,128)}), s32[16,1,1]{2,1,0:T(1,128)S(1)}, u32[]{:S(2)}, u32[]{:S(2)}) async-start(s32[16,1,1]{2,1,0:T(1,128)} %copy.34), calls=%async_computation.6 | async-start | bytes 16384 | tf_op jit(solution)/shard_map/all_to_all | solution.py:55
  45.6 1.3 fusion.20
  46.9 5.0 %all-to-all-done.6 = s32[16,1,1]{2,1,0:T(1,128)S(1)} async-done(((s32[16,1,1]{2,1,0:T(1,128)}), s32[16,1,1]{2,1,0:T(1,128)S(1)}, u32[]{:S(2)}, u32[]{:S(2)}) %all-to-all-start.6) | async-done | bytes 96 | tf_op jit(solution)/shard_map/all_to_all | solution.py:55
  51.9 3.7 %all-to-all-start.1 = ((bf16[16,1,64,576]{3,2,1,0:T(8,128)(2,1)}), bf16[16,1,64,576]{3,2,1,0:T(8,128)(2,1)S(1)}, u32[]{:S(2)}, u32[]{:S(2)}) async-start(bf16[16,1,64,576]{3,2,1,0:T(8,128)(2,1)} %fusion.20), calls=%async_computation.1 | async-start | bytes 2621440 | tf_op jit(solution)/shard_map/all_to_all | solution.py:51
  55.6 0.4 maximum_reduce_fusion.2
  56.0 0.8 gather_fusion.1
  56.8 1.3 fusion.19
  58.1 24.9 %all-to-all-done.1 = bf16[16,1,64,576]{3,2,1,0:T(8,128)(2,1)S(1)} async-done(((bf16[16,1,64,576]{3,2,1,0:T(8,128)(2,1)}), bf16[16,1,64,576]{3,2,1,0:T(8,128)(2,1)S(1)}, u32[]{:S(2)}, u32[]{:S(2)}) %all-to-all-start.1) | async-done | bytes 1179680 | tf_op jit(solution)/shard_map/all_to_all | solution.py:51
  82.9 8.0 %all-to-all-start.3 = ((bf16[16,1,64,576]{3,2,1,0:T(8,128)(2,1)}), bf16[16,1,64,576]{3,2,1,0:T(8,128)(2,1)S(1)}, u32[]{:S(2)}, u32[]{:S(2)}) async-start(bf16[16,1,64,576]{3,2,1,0:T(8,128)(2,1)} %fusion.19), calls=%async_computation.3 | async-start | bytes 2621440 | tf_op jit(solution)/shard_map/all_to_all | solution.py:51
  90.9 0.4 maximum_reduce_fusion.1
  91.3 1.8 gather_fusion.2
  93.1 2.6 %fusion.18 = bf16[16,1,64,576]{3,2,1,0:T(8,128)(2,1)} fusion(bf16[16,64,576]{2,1,0:T(8,128)(2,1)} %gather_fusion.2, pred[16]{0:T(512)(128)(4,1)S(1)} %and_bitcast_fusion.1), kind=kLoop, calls=%fused_computation.34 | loop fusion | flops 589824 | bytes 2359312 | tf_op jit(solution)/shard_map/jit(_take)/select_n | solution.py:48
  95.7 22.7 %all-to-all-done.3 = bf16[16,1,64,576]{3,2,1,0:T(8,128)(2,1)S(1)} async-done(((bf16[16,1,64,576]{3,2,1,0:T(8,128)(2,1)}), bf16[16,1,64,576]{3,2,1,0:T(8,128)(2,1)S(1)}, u32[]{:S(2)}, u32[]{:S(2)}) %all-to-all-start.3) | async-done | bytes 1179680 | tf_op jit(solution)/shard_map/all_to_all | solution.py:51
  118.3 8.1 %all-to-all-start.5 = ((bf16[16,1,64,576]{3,2,1,0:T(8,128)(2,1)}), bf16[16,1,64,576]{3,2,1,0:T(8,128)(2,1)}, u32[]{:S(2)}, u32[]{:S(2)}) async-start(bf16[16,1,64,576]{3,2,1,0:T(8,128)(2,1)} %fusion.18), calls=%async_computation.5 | async-start | bytes 2621440 | tf_op jit(solution)/shard_map/all_to_all | solution.py:51
  126.4 0.4 maximum_reduce_fusion
  126.8 1.8 gather_fusion.3
  128.6 2.6 %fusion.17 = bf16[16,1,64,576]{3,2,1,0:T(8,128)(2,1)} fusion(bf16[16,64,576]{2,1,0:T(8,128)(2,1)} %gather_fusion.3, pred[16]{0:T(512)(128)(4,1)S(1)} %and_bitcast_fusion), kind=kLoop, calls=%fused_computation.32 | loop fusion | flops 589824 | bytes 2359312 | tf_op jit(solution)/shard_map/jit(_take)/select_n | solution.py:48
  131.2 22.7 %all-to-all-done.5 = bf16[16,1,64,576]{3,2,1,0:T(8,128)(2,1)} async-done(((bf16[16,1,64,576]{3,2,1,0:T(8,128)(2,1)}), bf16[16,1,64,576]{3,2,1,0:T(8,128)(2,1)}, u32[]{:S(2)}, u32[]{:S(2)}) %all-to-all-start.5) | async-done | bytes 1179680 | tf_op jit(solution)/shard_map/all_to_all | solution.py:51
  153.9 8.1 %all-to-all-start.7 = ((bf16[16,1,64,576]{3,2,1,0:T(8,128)(2,1)}), bf16[16,1,64,576]{3,2,1,0:T(8,128)(2,1)}, u32[]{:S(2)}, u32[]{:S(2)}) async-start(bf16[16,1,64,576]{3,2,1,0:T(8,128)(2,1)} %fusion.17), calls=%async_computation.7 | async-start | bytes 2621440 | tf_op jit(solution)/shard_map/all_to_all | solution.py:51
  161.9 0.0 all-gather.3.cloned.1.call-start
  162.0 0.7 all-gather.3.cloned.1.call-update
  162.7 39.8 %all-gather = bf16[16,1,512]{2,1,0:T(2,128)(2,1)S(1)} all-gather(bf16[1,1,512]{2,1,0:T(2,128)(2,1)S(1)} %reshape.188), channel_id=1, replica_groups=mesh['groups'=2,'ctx'=16] {'ctx'}, dimensions={0}, use_global_device_ids=true | all-gather | bytes 17408 | tf_op jit(solution)/shard_map/all_gather | solution.py:28
  202.5 0.1 reduce
  202.6 2.3 pad_maximum_fusion
  205.0 2.6 %slice.28 = bf16[4096,512]{1,0:T(8,128)(2,1)} slice(bf16[4096,576]{1,0:T(8,128)(2,1)S(1)} %bitcast.132), slice={[0:4096], [0:512]} | slice | bytes 8388608 | tf_op jit(solution)/shard_map/slice | solution.py:64
  207.6 1.1 copy-done
  208.7 30.1 %while.21 = (s32[]{:T(128)}, bf16[2,128,512]{2,1,0:T(8,128)(2,1)S(1)}, s32[2,2048]{1,0:T(2,128)S(1)}, bf16[2,128,576]{1,2,0:T(8,128)(2,1)S(1)}, bf16[4096,576]{1...) while((s32[]{:T(128)}, bf16[2,128,512]{2,1,0:T(8,128)(2,1)S(1)}, ...), condition=%wide.region_6.8_spmd, body=%wide.region_2.7_spmd.sunk | while | flops 1145116416 | bytes 32289412 | solution.py:83
  208.7 9.1 %scatter_custom_fusion.5 = pred[4096]{0:T(1024)(128)(4,1)S(1)} fusion(s32[2048]{0:T(1024)S(1)} %bitcast.140, pred[2048]{0:T(1024)(128)(4,1)S(1)} %broadcast.208, pred[]{:T(512)} %constant.28.clone.1..sunk), kind=kCustom, calls=%fused_computation.27.clone.1 | custom fusion | bytes 4097 | tf_op jit(solution)/shard_map/while/body/eval_jaxpr/scatter | solution.py:68
  217.9 4.6 %fusion.51 = (f32[128]{0:T(128)S(1)}, f32[128,4096]{1,0:T(8,128)S(1)}) fusion(bf16[4096,576]{1,0:T(8,128)(2,1)} %get-tuple-element.220, bf16[2,128,576]{1,2,0:T(8,128)(2,1)S(1)} %get-tuple-element.219, s32[]{:T(128)} %get-tuple-element.207, pred[4096]{0:T(1024)(128)(4,1)S(1)} %scatter_custom_fusion.5), kind=kOutput, calls=%fused_computation.63.clone.1 | convolution fusion | flops 605552512 | bytes 6967812 | tf_op jit(solution)/shard_map/while/body/eval_jaxpr/dot_general | solution.py:70
  222.5 0.4 fusion.52
  222.9 0.8 fusion.53
  223.8 9.1 %scatter_custom_fusion.5 = pred[4096]{0:T(1024)(128)(4,1)S(1)} fusion(s32[2048]{0:T(1024)S(1)} %bitcast.140, pred[2048]{0:T(1024)(128)(4,1)S(1)} %broadcast.208, pred[]{:T(512)} %constant.28.clone.1..sunk), kind=kCustom, calls=%fused_computation.27.clone.1 | custom fusion | bytes 4097 | tf_op jit(solution)/shard_map/while/body/eval_jaxpr/scatter | solution.py:68
  232.9 4.6 %fusion.51 = (f32[128]{0:T(128)S(1)}, f32[128,4096]{1,0:T(8,128)S(1)}) fusion(bf16[4096,576]{1,0:T(8,128)(2,1)} %get-tuple-element.220, bf16[2,128,576]{1,2,0:T(8,128)(2,1)S(1)} %get-tuple-element.219, s32[]{:T(128)} %get-tuple-element.207, pred[4096]{0:T(1024)(128)(4,1)S(1)} %scatter_custom_fusion.5), kind=kOutput, calls=%fused_computation.63.clone.1 | convolution fusion | flops 605552512 | bytes 6967812 | tf_op jit(solution)/shard_map/while/body/eval_jaxpr/dot_general | solution.py:70
  237.5 0.4 fusion.52
  238.0 0.8 fusion.53
  238.8 0.0 all-gather.3.cloned.1.call-done
  238.9 0.6 copy-done.7
  239.5 9.2 %while.20 = (s32[]{:T(128)}, f32[4,2,2048]{2,1,0:T(2,128)}, bf16[4,2048,128]{2,1,0:T(8,128)(2,1)}, bf16[2,32,128]{2,1,0:T(8,128)(2,1)S(1)}, bf16[4,2048]{1,0:T(4...) while((s32[]{:T(128)}, f32[4,2,2048]{2,1,0:T(2,128)}, bf16[4,2048,128]{2,1,0:T(8,128)(2,1)}, ...), condition=%wide.region_1.2_spmd, body=%wide.region_0.1_spmd.sunk | while | flops 35391488 | bytes 1660113 | solution.py:35
  239.5 1.3 fusion.46
  240.9 0.3 fusion.47
  241.2 0.6 bitcast_dynamic-update-slice_fusion.2
  241.8 1.3 fusion.46
  243.2 0.3 fusion.47
  243.5 0.6 bitcast_dynamic-update-slice_fusion.2
  244.1 1.4 fusion.46
  245.5 0.3 fusion.47
  245.8 0.6 bitcast_dynamic-update-slice_fusion.2
  246.4 1.3 fusion.46
  247.8 0.3 fusion.47
  248.1 0.6 bitcast_dynamic-update-slice_fusion.2
  (41 shorter events, 0.2 us)
Async XLA Ops:
  8.7 13.8 %all-to-all-start = ((s32[16,1,1]{2,1,0:T(1,128)}), s32[16,1,1]{2,1,0:T(1,128)S(1)}, u32[]{:S(2)}, u32[]{:S(2)}) async-start(s32[16,1,1]{2,1,0:T(1,128)} %copy.27), calls=%async_computation | async-start | bytes 16384 | tf_op jit(solution)/shard_map/all_to_all | solution.py:55
  22.5 9.9 %all-to-all-start.2 = ((s32[16,1,1]{2,1,0:T(1,128)}), s32[16,1,1]{2,1,0:T(1,128)S(1)}, u32[]{:S(2)}, u32[]{:S(2)}) async-start(s32[16,1,1]{2,1,0:T(1,128)} %copy.30), calls=%async_computation.2 | async-start | bytes 16384 | tf_op jit(solution)/shard_map/all_to_all | solution.py:55
  32.3 9.8 %all-to-all-start.4 = ((s32[16,1,1]{2,1,0:T(1,128)}), s32[16,1,1]{2,1,0:T(1,128)S(1)}, u32[]{:S(2)}, u32[]{:S(2)}) async-start(s32[16,1,1]{2,1,0:T(1,128)} %copy.32), calls=%async_computation.4 | async-start | bytes 16384 | tf_op jit(solution)/shard_map/all_to_all | solution.py:55
  42.1 9.8 %all-to-all-start.6 = ((s32[16,1,1]{2,1,0:T(1,128)}), s32[16,1,1]{2,1,0:T(1,128)S(1)}, u32[]{:S(2)}, u32[]{:S(2)}) async-start(s32[16,1,1]{2,1,0:T(1,128)} %copy.34), calls=%async_computation.6 | async-start | bytes 16384 | tf_op jit(solution)/shard_map/all_to_all | solution.py:55
  51.9 31.1 %all-to-all-start.1 = ((bf16[16,1,64,576]{3,2,1,0:T(8,128)(2,1)}), bf16[16,1,64,576]{3,2,1,0:T(8,128)(2,1)S(1)}, u32[]{:S(2)}, u32[]{:S(2)}) async-start(bf16[16,1,64,576]{3,2,1,0:T(8,128)(2,1)} %fusion.20), calls=%async_computation.1 | async-start | bytes 2621440 | tf_op jit(solution)/shard_map/all_to_all | solution.py:51
  82.9 35.4 %all-to-all-start.3 = ((bf16[16,1,64,576]{3,2,1,0:T(8,128)(2,1)}), bf16[16,1,64,576]{3,2,1,0:T(8,128)(2,1)S(1)}, u32[]{:S(2)}, u32[]{:S(2)}) async-start(bf16[16,1,64,576]{3,2,1,0:T(8,128)(2,1)} %fusion.19), calls=%async_computation.3 | async-start | bytes 2621440 | tf_op jit(solution)/shard_map/all_to_all | solution.py:51
  118.3 35.5 %all-to-all-start.5 = ((bf16[16,1,64,576]{3,2,1,0:T(8,128)(2,1)}), bf16[16,1,64,576]{3,2,1,0:T(8,128)(2,1)}, u32[]{:S(2)}, u32[]{:S(2)}) async-start(bf16[16,1,64,576]{3,2,1,0:T(8,128)(2,1)} %fusion.18), calls=%async_computation.5 | async-start | bytes 2621440 | tf_op jit(solution)/shard_map/all_to_all | solution.py:51
  131.2 31.5 %copy-start.6 = (bf16[512]{0:T(512)(128)(2,1)S(1)}, bf16[512]{0:T(512)(128)(2,1)}, u32[]{:S(2)}) copy-start(bf16[512]{0:T(512)(128)(2,1)} %param.17) | copy-start | bytes 3076
  153.9 48.8 %all-to-all-start.7 = ((bf16[16,1,64,576]{3,2,1,0:T(8,128)(2,1)}), bf16[16,1,64,576]{3,2,1,0:T(8,128)(2,1)}, u32[]{:S(2)}, u32[]{:S(2)}) async-start(bf16[16,1,64,576]{3,2,1,0:T(8,128)(2,1)} %fusion.17), calls=%async_computation.7 | async-start | bytes 2621440 | tf_op jit(solution)/shard_map/all_to_all | solution.py:51
  161.9 76.9 %all-gather.3.cloned.1.call-start = ((), (), s32[]{:S(2)}) async-start(), calls=%async_computation.8 | async-start | bytes 2228224 | tf_op jit(solution)/shard_map/all_gather | solution.py:27
  205.0 3.7 %copy-start = (bf16[16,4,64,576]{3,2,1,0:T(8,128)(2,1)}, bf16[16,4,64,576]{3,2,1,0:T(8,128)(2,1)S(1)}, u32[]{:S(2)}) copy-start(bf16[16,4,64,576]{3,2,1,0:T(8,128)(2,1)S(1)} %pad_maximum_fusion) | copy-start | bytes 14155780
  205.0 3.7 %copy-start.2 = (bf16[2,128,576]{1,2,0:T(8,128)(2,1)S(1)}, bf16[2,128,576]{1,2,0:T(8,128)(2,1)}, u32[]{:S(2)}) copy-start(bf16[2,128,576]{1,2,0:T(8,128)(2,1)} %param.18) | copy-start | bytes 884740
  205.0 3.7 %copy-start.4 = (s32[2,2048]{1,0:T(2,128)S(1)}, s32[2,2048]{1,0:T(2,128)}, u32[]{:S(2)}) copy-start(s32[2,2048]{1,0:T(2,128)} %param.21) | copy-start | bytes 49156
  208.7 30.2 %copy-start.3 = (bf16[2,32,128]{2,1,0:T(8,128)(2,1)S(1)}, bf16[2,32,128]{2,1,0:T(8,128)(2,1)}, u32[]{:S(2)}) copy-start(bf16[2,32,128]{2,1,0:T(8,128)(2,1)} %param.14) | copy-start | bytes 49156
  208.7 30.2 %copy-start.5 = (bf16[2,32]{1,0:T(2,128)(2,1)S(1)}, bf16[2,32]{1,0:T(2,128)(2,1)}, u32[]{:S(2)}) copy-start(bf16[2,32]{1,0:T(2,128)(2,1)} %param.15) | copy-start | bytes 388
  217.9 5.1 %copy-start.1 = (bf16[4096,512]{1,0:T(8,128)(2,1)S(1)}, bf16[4096,512]{1,0:T(8,128)(2,1)}, u32[]{:S(2)}) copy-start(bf16[4096,512]{1,0:T(8,128)(2,1)} %get-tuple-element.221) | copy-start | bytes 12582916 | tf_op jit(solution)/shard_map/while
  232.9 5.1 %copy-start.1 = (bf16[4096,512]{1,0:T(8,128)(2,1)S(1)}, bf16[4096,512]{1,0:T(8,128)(2,1)}, u32[]{:S(2)}) copy-start(bf16[4096,512]{1,0:T(8,128)(2,1)} %get-tuple-element.221) | copy-start | bytes 12582916 | tf_op jit(solution)/shard_map/while
  238.8 0.7 copy-start.7
Sparse Core Ops, SparseCore 0:
  164.9 49.6 all-gather.2
where the time goes:
time: 260 us; the launch traced here: 256 us
  waiting for transfers between devices  90.4 us (35%)
  starting transfers between devices  45.6 us (18%)
  blocking collectives  39.8 us (15%)
  local copies, waits for them, and re-layouts  35.1 us (14%)
  matrix products  17.4 us (7%)
  between operations  14.3 us (6%)
  other arithmetic  12.7 us (5%)
    all_to_all x4, waiting for transfers between devices, serve_slot(): lax.all_to_all(lookup(asked), 'ctx', split_axis=0, concat_axis=0, tiled=T...  70.2 us
    all_gather x1, blocking collectives, local(): scale_rows = lax.all_gather(key_scales, 'ctx', axis=0, tiled=True)  39.8 us
    all_to_all x4, starting transfers between devices, serve_slot(): lax.all_to_all(lookup(asked), 'ctx', split_axis=0, concat_axis=0, tiled=T...  27.8 us
    all_to_all x4, waiting for transfers between devices, local(): lax.all_to_all(requests[:, slot:slot + 1], 'ctx', split_axis=0, concat_ax...  19.5 us
    scatter x2, local copies, waits for them, and re-layouts, attend(): chosen_mask = jnp.zeros((slot_total,), jnp.bool_).at[chosen].set(True)  18.3 us
    all_to_all x4, starting transfers between devices, local(): lax.all_to_all(requests[:, slot:slot + 1], 'ctx', split_axis=0, concat_ax...  17.8 us
    dot_general x2, matrix products, attend(): lax.dot_general(query_row, buffer_rows, (((1,), (1,)), ((), ())), preferr...  9.18 us
    select_n x4, other arithmetic, lookup(): return jnp.take(block_table, jnp.clip(asked, 0, None), axis=0)  7.71 us
  transfers between devices with their start and end apart: 9, of which 7 were waited for; matrix products, arithmetic and copies ran while one was open for 21% of the time, Pallas kernels for 0%

commit v1 on v0

v1 whole, which is shorter than its diff:
```python
import functools

import jax
import jax.numpy as jnp
from jax import lax
from jax.experimental import pallas as pl
from jax.experimental.pallas import tpu as pltpu
from jax.sharding import PartitionSpec as P

BLOCK = 64
LANES = 512
KVR = 512
ROPE = 64
HEADS = 128
IH = 32
IDX = 128
TOK = 512
NEG = -1e30
LOG2E = 1.4426950408889634
TO_LOG2 = 192.0 ** (-0.5) * LOG2E

KV_ROPE = TOK
KV_KEYS = KV_ROPE + ROPE
KV_SCALE = KV_KEYS + IDX
KV_ROWS = KV_SCALE + 16

Q_LAT = 2 * HEADS
Q_ROPE = Q_LAT
Q_IDX = Q_ROPE + 32
Q_W = Q_IDX + 16
Q_BIAS = Q_W + 16

BF = jnp.bfloat16
F32 = jnp.float32
VMEM = pl.BlockSpec(memory_space=pltpu.VMEM)


def nn(a, b):
    return lax.dot_general(a, b, (((1,), (0,)), ((), ())), preferred_element_type=F32)


def nt(a, b):
    return lax.dot_general(a, b, (((1,), (1,)), ((), ())), preferred_element_type=F32)


def iota(shape, dim):
    return lax.broadcasted_iota(jnp.int32, shape, dim)


def onehot(cond):
    return jnp.where(cond, 1.0, 0.0).astype(BF)


def eye(n):
    return onehot(iota((n, n), 0) == iota((n, n), 1))


def pack_kv_kernel(lat_ref, keys_ref, scale_ref, out_ref):
    out_ref[0:TOK, :] = lat_ref[:, 0:KVR]
    out_ref[KV_ROPE:KV_KEYS, :] = nt(eye(ROPE), lat_ref[:, KVR : KVR + ROPE]).astype(BF)
    out_ref[KV_KEYS:KV_SCALE, :] = nt(eye(IDX), keys_ref[...]).astype(BF)
    out_ref[KV_SCALE:KV_ROWS, :] = jnp.broadcast_to(scale_ref[...], (16, TOK))


def pack_q_kernel(half_size, q_ref, iq_ref, w_ref, sel_ref, want_ref, wire_ref, own_ref, bias):
    me = lax.axis_index("ctx")
    half = me // half_size
    n = 2 * half_size
    slots = want_ref.shape[2]
    topk = sel_ref.shape[1]
    for t in range(2):
        wire_ref[t * HEADS : (t + 1) * HEADS, :] = q_ref[t, :, 0:KVR]
    place = [
        onehot(iota((ROPE, 2 * ROPE), 0) + t * ROPE == iota((ROPE, 2 * ROPE), 1)) for t in range(2)
    ]
    ropes = nn(q_ref[0, :, KVR : KVR + ROPE], place[0]) + nn(q_ref[1, :, KVR : KVR + ROPE], place[1])
    ropes = ropes.astype(BF)
    for b in range(4):
        wire_ref[Q_ROPE : Q_ROPE + 32, b * 128 : (b + 1) * 128] = ropes[b * 32 : (b + 1) * 32, :]
        wire_ref[Q_IDX : Q_IDX + 16, b * 128 : (b + 1) * 128] = iq_ref[
            b // 2, (b % 2) * 16 : (b % 2) * 16 + 16, :
        ]
    wire_ref[Q_W : Q_W + 16, :] = jnp.zeros((16, LANES), BF)
    wire_ref[Q_W : Q_W + 2, 0:IH] = w_ref[...]
    lane_block = iota((n, LANES), 1) // BLOCK
    spread = onehot(iota((BLOCK, LANES), 1) % BLOCK == iota((BLOCK, LANES), 0))
    for t in range(2):
        sel = sel_ref[t : t + 1, :]
        slot = sel // BLOCK
        inner = onehot(sel % BLOCK == iota((BLOCK, topk), 0))
        total = jnp.zeros((n, LANES), F32)
        for b in range(slots):
            picked = onehot(slot == iota((n, topk), 0) * slots + b)
            count = nt(picked, inner)
            wide = nn(count.astype(BF), spread)
            total = total + jnp.where(lane_block == want_ref[0, :, b : b + 1], wide, 0.0)
        bias[t] = jnp.where(total > 0.5, 0.0, NEG)
    mine = half * half_size
    other = (1 - half) * half_size
    for t in range(2):
        own_ref[t * half_size : (t + 1) * half_size, :] = bias[
            t, pl.ds(pl.multiple_of(mine, half_size), half_size), :
        ].astype(BF)
        wire_ref[Q_BIAS + t * half_size : Q_BIAS + (t + 1) * half_size, :] = bias[
            t, pl.ds(pl.multiple_of(other, half_size), half_size), :
        ].astype(BF)


def split3(x):
    hi = x.astype(BF)
    rest = x - hi.astype(F32)
    mid = rest.astype(BF)
    return hi, mid, (rest - mid.astype(F32)).astype(BF)


def attend_kernel(half_size, masks, first, mode, *refs):
    count = len(masks)
    refs = list(refs)
    q_ref, bias_ref = refs[:2]
    pieces = refs[2 : 2 + count]
    pos = 2 + count
    if not first:
        acc_in, m_in, l_in, sc_in = refs[pos : pos + 4]
        pos += 4
    if mode == "state":
        acc_out, m_out, l_out, sc_out = refs[pos : pos + 4]
        pos += 4
    elif mode == "wire":
        wire_out = refs[pos]
        pos += 1
    else:
        o_out, lse_out, sc_out = refs[pos : pos + 3]
        pos += 3
    bias, logits, sc = refs[pos : pos + 3]

    me = lax.axis_index("ctx")
    core = me % 2
    rows = 2 * half_size
    bias_base = Q_BIAS if bias_ref.shape[0] > rows else 0
    bias[...] = bias_ref[bias_base : bias_base + rows, :].astype(F32)
    if not first:
        sc[...] = sc_in[...]
    elif len(masks) < half_size:
        sc[...] = jnp.zeros_like(sc)

    q_lat = q_ref[0:Q_LAT, :]
    ropes = jnp.concatenate(
        [q_ref[Q_ROPE : Q_ROPE + 32, b * 128 : (b + 1) * 128] for b in range(4)], axis=0
    )
    place = [
        onehot(iota((ROPE, 2 * ROPE), 0) + t * ROPE == iota((ROPE, 2 * ROPE), 1)) for t in range(2)
    ]
    q_rope = jnp.concatenate([nt(ropes, place[t]) for t in range(2)], axis=0).astype(BF)
    iq = jnp.concatenate(
        [q_ref[Q_IDX : Q_IDX + 16, b * 128 : (b + 1) * 128] for b in range(4)], axis=0
    )
    w_cols = nt(eye(IH), q_ref[Q_W : Q_W + 16, 0:IH])

    m_prev = None if first else m_in[:, 0:1]
    m_new = m_prev
    for p in range(count):
        kv = pieces[p]
        src = lax.bitwise_xor(me, jnp.where(core == 0, masks[p][0], masks[p][1]))
        src = src % half_size
        s = nt(q_lat, kv[0:TOK, :]) + nn(q_rope, kv[KV_ROPE:KV_KEYS, :])
        s = s * TO_LOG2
        for t in range(2):
            part = s[t * HEADS : (t + 1) * HEADS, :] + bias[pl.ds(t * half_size + src, 1), :]
            logits[t * HEADS : (t + 1) * HEADS, p * TOK : (p + 1) * TOK] = part
        raw = nn(iq, kv[KV_KEYS:KV_SCALE, :])
        scale = kv[KV_SCALE : KV_SCALE + 16, :].astype(F32)[0:1, :]
        lifted = jnp.maximum(raw, 0.0)
        for t in range(2):
            weighted = lifted[t * IH : (t + 1) * IH, :] * w_cols[:, t : t + 1]
            sc[pl.ds(t * half_size + src, 1), :] = jnp.sum(weighted, axis=0, keepdims=True) * scale
    top = jnp.max(logits[...], axis=1, keepdims=True)
    m_new = top if first else jnp.maximum(m_prev, top)

    total = None
    acc = None
    for p in range(count):
        e = jnp.exp2(logits[:, p * TOK : (p + 1) * TOK] - m_new)
        part = jnp.sum(e, axis=1, keepdims=True)
        total = part if total is None else total + part
        out = nn(e.astype(BF), pieces[p][0:TOK, :])
        acc = out if acc is None else acc + out
    if not first:
        alpha = jnp.exp2(m_prev - m_new)
        total = total + l_in[:, 0:1] * alpha
        acc = acc + acc_in[...] * alpha
    if mode == "state":
        acc_out[...] = acc
        m_out[...] = jnp.broadcast_to(m_new, m_out.shape)
        l_out[...] = jnp.broadcast_to(total, l_out.shape)
        sc_out[...] = sc[...]
        return
    norm = acc / total
    lse = m_new + jnp.log(total) * LOG2E
    if mode == "own":
        o_out[...] = norm
        lse_out[...] = jnp.broadcast_to(lse, lse_out.shape)
        sc_out[...] = sc[...]
        return
    wire_out[0:Q_LAT, :] = norm.astype(BF)
    diag = iota((Q_LAT, Q_LAT), 0) == iota((Q_LAT, Q_LAT), 1)
    row = jnp.sum(jnp.where(diag, lse, 0.0), axis=0, keepdims=True)
    hi, mid, lo = [x.astype(F32) for x in split3(row)]
    which = iota((16, Q_LAT), 0)
    left = jnp.where(which == 0, hi, jnp.where(which == 1, lo, 0.0))
    right = jnp.where(which == 0, mid, 0.0)
    wire_out[Q_LAT : Q_LAT + 16, 0:Q_LAT] = left.astype(BF)
    wire_out[Q_LAT : Q_LAT + 16, Q_LAT : 2 * Q_LAT] = right.astype(BF)
    hi, mid, lo = split3(sc[...])
    wire_out[Q_LAT + 16 : Q_LAT + 16 + rows, :] = hi
    wire_out[Q_LAT + 16 + rows : Q_LAT + 16 + 2 * rows, :] = mid


def final_kernel(half_size, o_ref, lse_ref, sc_ref, wire_ref, scores_ref, out_ref):
    me = lax.axis_index("ctx")
    half = me // half_size
    rows = 2 * half_size
    stats = wire_ref[Q_LAT : Q_LAT + 16, :].astype(F32)
    row = stats[0:1, 0:Q_LAT] + stats[0:1, Q_LAT : 2 * Q_LAT] + stats[1:2, 0:Q_LAT]
    diag = iota((Q_LAT, Q_LAT), 0) == iota((Q_LAT, Q_LAT), 1)
    lse_r = jnp.sum(jnp.where(diag, row, 0.0), axis=1, keepdims=True)
    lse_o = lse_ref[:, 0:1]
    top = jnp.maximum(lse_r, lse_o)
    e_r = jnp.exp2(lse_r - top)
    e_o = jnp.exp2(lse_o - top)
    inv = 1.0 / (e_r + e_o)
    out = o_ref[...] * (e_o * inv) + wire_ref[0:Q_LAT, :].astype(F32) * (e_r * inv)
    for t in range(2):
        out_ref[t] = out[t * HEADS : (t + 1) * HEADS, :].astype(BF)
    base = Q_LAT + 16
    sc_r = wire_ref[base : base + rows, :].astype(F32) + wire_ref[
        base + rows : base + 2 * rows, :
    ].astype(F32)
    sc_o = sc_ref[...]
    for t in range(2):
        for d in range(half_size):
            line = t * half_size + d
            at = pl.multiple_of((half * half_size + d) * TOK, TOK)
            scores_ref[t : t + 1, pl.ds(at, TOK)] = sc_o[line : line + 1, :]
            at = pl.multiple_of(((1 - half) * half_size + d) * TOK, TOK)
            scores_ref[t : t + 1, pl.ds(at, TOK)] = sc_r[line : line + 1, :]


def call(kernel, out_shape, name, flops, *args, scratch=(), aliases=None):
    moved = sum(a.size * a.dtype.itemsize for a in args)
    return pl.pallas_call(
        kernel,
        out_shape=out_shape,
        in_specs=[VMEM] * len(args),
        out_specs=jax.tree.map(lambda _: VMEM, out_shape),
        scratch_shapes=list(scratch),
        input_output_aliases=aliases or {},
        name=name,
        cost_estimate=pl.CostEstimate(flops=int(flops), bytes_accessed=moved, transcendentals=0),
        compiler_params=pltpu.CompilerParams(vmem_limit_bytes=48 << 20),
    )(*args)


def shape(dims, dtype):
    return jax.ShapeDtypeStruct(dims, dtype)


def attend(half_size, q_wire, bias, group, state, mode, name):
    masks = tuple(mask for _, mask in group)
    args = [q_wire, bias] + [piece for piece, _ in group]
    aliases = {}
    rows = 2 * half_size
    state_shape = (
        shape((Q_LAT, KVR), F32),
        shape((Q_LAT, 128), F32),
        shape((Q_LAT, 128), F32),
        shape((rows, LANES), F32),
    )
    if state is not None:
        args += list(state)
    if mode == "state":
        outs = state_shape
    elif mode == "wire":
        outs = shape((Q_LAT + 16 + 2 * rows, LANES), BF)
    else:
        outs = (state_shape[0], state_shape[1], state_shape[3])
    scratch = [
        pltpu.VMEM((rows, LANES), F32),
        pltpu.VMEM((Q_LAT, TOK * len(group)), F32),
        pltpu.VMEM((rows, LANES), F32),
    ]
    flops = 2 * Q_LAT * TOK * len(group) * (2 * KVR + ROPE)
    return call(
        functools.partial(attend_kernel, half_size, masks, state is None, mode),
        outs,
        name,
        flops,
        *args,
        scratch=scratch,
        aliases=aliases,
    )


def local(n, index_queries, index_weights, index_keys, key_scales, q_latent, latents, wanted, selected):
    half_size = n // 2
    bits = n.bit_length() - 1
    top = 1 << (bits - 1)

    def permute(x, move):
        return lax.ppermute(x, "ctx", [(i, move(i)) for i in range(n)])

    def swap(x):
        return permute(x, lambda i: i ^ 1)

    kv = call(
        pack_kv_kernel,
        shape((KV_ROWS, LANES), BF),
        "pack_kv",
        2 * TOK * TOK * 192,
        latents,
        index_keys,
        key_scales.reshape(1, TOK),
    )
    r1 = permute(kv, lambda i: i ^ 2 if i % 2 == 0 else i ^ 4)
    r2 = permute(kv, lambda i: i ^ 4 if i % 2 == 0 else i ^ 2)
    r3 = permute(r1, lambda i: i ^ 4 if i % 2 == 0 else i ^ 2)
    held = [(kv, (0, 0)), (r1, (2, 4)), (r2, (4, 2)), (r3, (6, 6))]
    for bit in range(3, bits - 1):
        step = 1 << bit
        held = held + [
            (permute(piece, lambda i: i ^ step), (a ^ step, b ^ step)) for piece, (a, b) in held
        ]

    rows = 2 * half_size
    q_wire, bias_own = call(
        functools.partial(pack_q_kernel, half_size),
        (shape((Q_BIAS + rows, LANES), BF), shape((rows, LANES), BF)),
        "pack_q",
        2 * 2 * n * 2048 * 64 * 4,
        q_latent,
        index_queries,
        index_weights,
        selected,
        wanted,
        scratch=[pltpu.VMEM((2, n, LANES), F32)],
    )
    q_far = permute(q_wire, lambda i: i ^ top)

    pairs = []
    for piece, (a, b) in held:
        pairs.append([(piece, (a, b)), (swap(piece), (1 ^ b, 1 ^ a))])
    groups = [pairs[0] + pairs[1] + pairs[2], pairs[3]]
    for at in range(4, len(pairs), 3):
        groups.append(sum(pairs[at : at + 3], []))

    def run(q, bias, last, name):
        state = None
        for k, group in enumerate(groups):
            mode = last if k == len(groups) - 1 else "state"
            state = attend(half_size, q, bias, group, state, mode, f"{name}_{k}")
        return state

    wire = run(q_far, q_far, "wire", "attend_far")
    o_far = permute(wire, lambda i: i ^ top)
    o_own, lse_own, scores_own = run(q_wire, bias_own, "own", "attend_own")
    scores, attended = call(
        functools.partial(final_kernel, half_size),
        (shape((2, n * TOK), F32), shape((2, HEADS, KVR), BF)),
        "combine",
        Q_LAT * KVR * 4,
        o_own,
        lse_own,
        scores_own,
        o_far,
    )
    return scores, attended


def solution(mesh):
    spec = P(("groups", "ctx"))
    return jax.shard_map(
        functools.partial(local, mesh.shape["ctx"]),
        mesh=mesh,
        in_specs=(spec,) * 8,
        out_specs=(spec, spec),
        check_vma=False,
    )
```

time: 260 us -> 81.6 us (0.31); the launches traced: 256 us -> 81.4 us
  blocking collectives: 39.8 us -> 0 us
  waiting for transfers between devices: 90.4 us -> 51.2 us
  starting transfers between devices: 45.6 us -> 10.4 us
  local copies, waits for them, and re-layouts: 35.1 us -> 3.24 us
  matrix products: 17.4 us -> 0 us
  Pallas kernels: 0 us -> 15.8 us
  between operations: 14.3 us -> 0.77 us
  other arithmetic: 12.7 us -> 0 us
    all_to_all x8 -> x0, waiting for transfers between devices: 89.7 us -> none  [the longest x4 70.2 us: serve_slot(): lax.all_to_all(lookup(asked), 'ctx', split_axis=0, concat_axis=0, tiled=T...]
    ppermute x0 -> x9, waiting for transfers between devices: none -> 51.2 us  [permute(): return lax.ppermute(x, 'ctx', [(i, move(i)) for i in range(n)])]
    all_to_all x8 -> x0, starting transfers between devices: 45.6 us -> none  [the longest x4 27.8 us: serve_slot(): lax.all_to_all(lookup(asked), 'ctx', split_axis=0, concat_axis=0, tiled=T...]
    all_gather x1 -> x0, blocking collectives: 39.8 us -> none  [local(): scale_rows = lax.all_gather(key_scales, 'ctx', axis=0, tiled=True)]
    scatter x2 -> x0, local copies, waits for them, and re-layouts: 18.3 us -> none  [attend(): chosen_mask = jnp.zeros((slot_total,), jnp.bool_).at[chosen].set(True)]
    dot_general x12 -> x0, matrix products: 17.4 us -> none  [the longest x2 9.18 us: attend(): lax.dot_general(query_row, buffer_rows, (((1,), (1,)), ((), ())), preferr...]
    pallas_call x0 -> x7, Pallas kernels: none -> 15.8 us  [call(): pl.pallas_call(kernel, out_shape=out_shape, in_specs=[VMEM] * len(args),...]
    ppermute x0 -> x9, starting transfers between devices: none -> 10.4 us  [permute(): return lax.ppermute(x, 'ctx', [(i, move(i)) for i in range(n)])]
  transfers between devices with their start and end apart: 9 -> 9, of which waited for: 7 -> 4; matrix products, arithmetic and copies ran while one was open for 21% -> 2% of each run, Pallas kernels for 0% -> 16%
where the time goes in v1:
time: 81.6 us; the launch traced here: 81.4 us
  waiting for transfers between devices  51.2 us (63%)
  Pallas kernels  15.8 us (19%)
  starting transfers between devices  10.4 us (13%)
  local copies, waits for them, and re-layouts  3.24 us (4%)
    ppermute x9, waiting for transfers between devices, permute(): return lax.ppermute(x, 'ctx', [(i, move(i)) for i in range(n)])  51.2 us
    pallas_call x7, Pallas kernels, call(): pl.pallas_call(kernel, out_shape=out_shape, in_specs=[VMEM] * len(args),...  15.8 us
    ppermute x9, starting transfers between devices, permute(): return lax.ppermute(x, 'ctx', [(i, move(i)) for i in range(n)])  10.4 us
    unnamed x15, local copies, waits for them, and re-layouts  3.24 us
  transfers between devices with their start and end apart: 9, of which 4 were waited for; matrix products, arithmetic and copies ran while one was open for 2% of the time, Pallas kernels for 16%

profile of v1, /device:TPU:0, one launch (start us, length us, event | category | flops | bytes accessed | tf_op | source)
XLA Modules:
  0.0 81.4 jit_solution(17641089591747245650)
XLA Ops:
  0.6 0.0 copy-start.5
  0.6 0.0 copy-start
  0.7 1.4 %copy.12.lat_ref = bf16[512,576]{1,0:T(8,128)(2,1)S(1)} copy(bf16[512,576]{0,1:T(8,128)(2,1)} %param.13) | data formatting | bytes 1179648 | tf_op args[5]
  2.0 0.0 copy-done.5
  2.1 0.0 copy-done
  2.1 0.3 pack_kv.1.refs_2_
  2.4 0.0 copy-start.4
  2.4 3.0 %collective-permute-start = (bf16[720,512]{1,0:T(8,128)(2,1)S(1)}, bf16[720,512]{1,0:T(8,128)(2,1)S(1)}, u32[]{:S(2)}, u32[]{:S(2)}) collective-permute-start(bf16[720,512]{1,0:T(8,128)(2,1)S(1)} %pack_kv.1.refs_2_), channel_id=1, source_target_pairs={{0,2},{1,5},{2,0},{3,7},{4,6},{5,1},{6,4},{7,3},{8,10},{9,13},{10,... | collective-permute-start | bytes 2211848 | tf_op jit(solution)/shard_map/ppermute | solution.py:309
  5.4 1.6 %collective-permute-start.5 = (bf16[720,512]{1,0:T(8,128)(2,1)S(1)}, bf16[720,512]{1,0:T(8,128)(2,1)}, u32[]{:S(2)}, u32[]{:S(2)}) collective-permute-start(bf16[720,512]{1,0:T(8,128)(2,1)S(1)} %pack_kv.1.refs_2_), channel_id=1, source_target_pairs={{0,4},{1,3},{2,6},{3,1},{4,0},{5,7},{6,2},{7,5},{8,12},{9,11},{10,... | collective-permute-start | bytes 2211848 | tf_op jit(solution)/shard_map/ppermute | solution.py:309
  7.0 15.2 %collective-permute-done.refs_4_ = bf16[720,512]{1,0:T(8,128)(2,1)S(1)} collective-permute-done((bf16[720,512]{1,0:T(8,128)(2,1)S(1)}, bf16[720,512]{1,0:T(8,128)(2,1)S(1)}, u32[]{:S(2)}, u32[]{:S(2)}) %collective-permute-start) | collective-permute-done | bytes 737312 | tf_op jit(solution)/shard_map/ppermute | solution.py:309
  22.1 1.6 %collective-permute-start.1 = (bf16[720,512]{1,0:T(8,128)(2,1)S(1)}, bf16[720,512]{1,0:T(8,128)(2,1)S(1)}, u32[]{:S(2)}, u32[]{:S(2)}) collective-permute-start(bf16[720,512]{1,0:T(8,128)(2,1)S(1)} %collective-permute-done.refs_4_), channel_id=1, source_target_pairs={{0,4},{1,3},{2,6},{3,1},{4,0},{5,7},{6,2},{7,5},{8,12},{9,11},{10,... | collective-permute-start | bytes 2211848 | tf_op jit(solution)/shard_map/ppermute | solution.py:309
  23.8 0.0 collective-permute-start.3
  23.8 0.5 collective-permute-start.4
  24.3 0.0 collective-permute-done.5.refs_6_
  24.3 0.0 collective-permute-start.6
  24.3 9.3 %collective-permute-done.1.refs_2_ = bf16[720,512]{1,0:T(8,128)(2,1)S(1)} collective-permute-done((bf16[720,512]{1,0:T(8,128)(2,1)S(1)}, bf16[720,512]{1,0:T(8,128)(2,1)S(1)}, u32[]{:S(2)}, u32[]{:S(2)}) %collective-permute-start.1) | collective-permute-done | bytes 737312 | tf_op jit(solution)/shard_map/ppermute | solution.py:309
  33.6 0.0 collective-permute-start.2
  33.6 0.0 copy-start.1
  33.6 0.0 copy-start.2
  33.6 1.2 %copy.10.q_ref = bf16[2,128,576]{2,1,0:T(8,128)(2,1)S(1)} copy(bf16[2,128,576]{1,2,0:T(8,128)(2,1)} %param.12) | data formatting | bytes 589824 | tf_op args[4]
  34.8 0.0 copy-done.4
  34.8 0.0 copy-start.3
  34.8 0.1 copy.11.want_ref
  34.9 0.0 copy-done.1
  34.9 0.0 copy-done.2
  34.9 0.6 copy-done.3
  35.4 2.2 %pack_q.1 = (bf16[336,512]{1,0:T(8,128)(2,1)S(1)}, bf16[16,512]{1,0:T(8,128)(2,1)S(1)}) custom-call(bf16[2,128,576]{2,1,0:T(8,128)(2,1)S(1)} %copy.10.q_ref, bf16[2,32,128]{2,1,0:T(8,128)(2,1)S(1)} %copy-done.1, bf16[2,32]{1,0:T(2,128)(2,1)S(1)} %copy-done.3, s32[2,2048]{1,0:T(2,128)S(1)} %copy-done.2, s32[1,16,4]{2,1,0:T(8,128)S(1)} %copy.11.want_ref), custom_call_target="tpu_custom_call" | custom-call | flops 33554432 | bytes 328064 | tf_op jit(solution)/shard_map/pack_q/pallas_call | solution.py:250
  37.7 3.6 %collective-permute-start.7 = (bf16[336,512]{1,0:T(8,128)(2,1)S(1)}, bf16[336,512]{1,0:T(8,128)(2,1)S(1)}, u32[]{:S(2)}, u32[]{:S(2)}) collective-permute-start(bf16[336,512]{1,0:T(8,128)(2,1)S(1)} %get-tuple-element.15.refs_0_), channel_id=1, source_target_pairs={{0,8},{1,9},{2,10},{3,11},{4,12},{5,13},{6,14},{7,15},{8,0},{9,1},... | collective-permute-start | bytes 1032200 | tf_op jit(solution)/shard_map/ppermute | solution.py:309
  41.3 16.1 %collective-permute-done.7.refs_0_.refs_1_ = bf16[336,512]{1,0:T(8,128)(2,1)S(1)} collective-permute-done((bf16[336,512]{1,0:T(8,128)(2,1)S(1)}, bf16[336,512]{1,0:T(8,128)(2,1)S(1)}, u32[]{:S(2)}, u32[]{:S(2)}) %collective-permute-start.7) | collective-permute-done | bytes 344096 | tf_op jit(solution)/shard_map/ppermute | solution.py:309
  57.4 0.0 collective-permute-done.3.refs_3_
  57.4 0.0 collective-permute-done.4.refs_5_
  57.4 0.0 collective-permute-done.6.refs_7_
  57.4 4.8 %attend_far_0.1 = (f32[256,512]{1,0:T(8,128)S(1)}, f32[256,128]{1,0:T(8,128)S(1)}, f32[256,128]{1,0:T(8,128)S(1)}, f32[16,512]{1,0:T(8,128)S(1)}) custom-call(bf16[336,512]{1,0:T(8,128)(2,1)S(1)} %collective-permute-done.7.refs_0_.refs_1_, bf16[336,512]{1,0:T(8,128)(2,1)S(1)} %collective-permute-done.7.refs_0_.refs_1_, bf16[720,512]{1,0:T(8,128)(2,1)S(1)} %pack_kv.1.refs_2_, ...), custom_call_target="tpu_custom_call" | custom-call | flops 1711276032 | bytes 5111808 | tf_op jit(solution)/shard_map/attend_far_0/pallas_call | solution.py:250
  62.2 0.0 collective-permute-done.2.refs_3_
  62.2 1.4 %attend_far_1.1 = bf16[304,512]{1,0:T(8,128)(2,1)S(1)} custom-call(bf16[336,512]{1,0:T(8,128)(2,1)S(1)} %collective-permute-done.7.refs_0_.refs_1_, bf16[336,512]{1,0:T(8,128)(2,1)S(1)} %collective-permute-done.7.refs_0_.refs_1_, bf16[720,512]{1,0:T(8,128)(2,1)S(1)} %collective-permute-done.1.refs_2_, bf16[720,512]{1,0:T(8,128)(2,1)S(1)} %collective-permute-done.2.refs_3_, ...), custom_call_target="tpu_custom_call" | custom-call | flops 570425344 | bytes 2981888 | tf_op jit(solution)/shard_map/attend_far_1/pallas_call | solution.py:250
  63.6 0.1 collective-permute-start.8
  63.6 4.8 %attend_own_0.1 = (f32[256,512]{1,0:T(8,128)S(1)}, f32[256,128]{1,0:T(8,128)S(1)}, f32[256,128]{1,0:T(8,128)S(1)}, f32[16,512]{1,0:T(8,128)S(1)}) custom-call(bf16[336,512]{1,0:T(8,128)(2,1)S(1)} %get-tuple-element.15.refs_0_, bf16[16,512]{1,0:T(8,128)(2,1)S(1)} %get-tuple-element.16.refs_1_, bf16[720,512]{1,0:T(8,128)(2,1)S(1)} %pack_kv.1.refs_2_, ...), custom_call_target="tpu_custom_call" | custom-call | flops 1711276032 | bytes 4784128 | tf_op jit(solution)/shard_map/attend_own_0/pallas_call | solution.py:250
  68.4 1.4 %attend_own_1.1 = (f32[256,512]{1,0:T(8,128)S(1)}, f32[256,128]{1,0:T(8,128)S(1)}, f32[16,512]{1,0:T(8,128)S(1)}) custom-call(bf16[336,512]{1,0:T(8,128)(2,1)S(1)} %get-tuple-element.15.refs_0_, bf16[16,512]{1,0:T(8,128)(2,1)S(1)} %get-tuple-element.16.refs_1_, bf16[720,512]{1,0:T(8,128)(2,1)S(1)} %collective-permute-done.1.refs_2_, ...), custom_call_target="tpu_custom_call" | custom-call | flops 570425344 | bytes 2654208 | tf_op jit(solution)/shard_map/attend_own_1/pallas_call | solution.py:250
  69.8 10.6 %collective-permute-done.8.wire_ref = bf16[304,512]{1,0:T(8,128)(2,1)S(1)} collective-permute-done((bf16[304,512]{1,0:T(8,128)(2,1)S(1)}, bf16[304,512]{1,0:T(8,128)(2,1)S(1)}, u32[]{:S(2)}, u32[]{:S(2)}) %collective-permute-start.8) | collective-permute-done | bytes 311328 | tf_op jit(solution)/shard_map/ppermute | solution.py:309
  80.4 1.0 %combine.1 = (f32[2,8192]{1,0:T(2,128)}, bf16[2,128,512]{2,1,0:T(8,128)(2,1)}) custom-call(f32[256,512]{1,0:T(8,128)S(1)} %get-tuple-element.21.o_ref, f32[256,128]{1,0:T(8,128)S(1)} %get-tuple-element.22.lse_ref, f32[16,512]{1,0:T(8,128)S(1)} %get-tuple-element.23.sc_ref, bf16[304,512]{1,0:T(8,128)(2,1)S(1)} %collective-permute-done.8.wire_ref), custom_call_target="tpu_custom_call" | custom-call | flops 524288 | bytes 999424 | tf_op jit(solution)/shard_map/combine/pallas_call | solution.py:250
  (1 shorter events, 0.0 us)
Async XLA Ops:
  0.6 1.4 %copy-start.5 = (bf16[512]{0:T(512)(128)(2,1)S(1)}, bf16[512]{0:T(512)(128)(2,1)}, u32[]{:S(2)}) copy-start(bf16[512]{0:T(512)(128)(2,1)} %param.11) | copy-start | bytes 3076
  0.6 1.4 %copy-start = (bf16[512,128]{1,0:T(8,128)(2,1)S(1)}, bf16[512,128]{1,0:T(8,128)(2,1)}, u32[]{:S(2)}) copy-start(bf16[512,128]{1,0:T(8,128)(2,1)} %keys_ref.1) | copy-start | bytes 393220
  2.4 32.4 %copy-start.4 = (s32[1,16,4]{1,2,0:T(4,128)S(1)}, s32[1,16,4]{1,2,0:T(4,128)}, u32[]{:S(2)}) copy-start(s32[1,16,4]{1,2,0:T(4,128)} %param.14) | copy-start | bytes 772
  2.4 19.8 %collective-permute-start = (bf16[720,512]{1,0:T(8,128)(2,1)S(1)}, bf16[720,512]{1,0:T(8,128)(2,1)S(1)}, u32[]{:S(2)}, u32[]{:S(2)}) collective-permute-start(bf16[720,512]{1,0:T(8,128)(2,1)S(1)} %pack_kv.1.refs_2_), channel_id=1, source_target_pairs={{0,2},{1,5},{2,0},{3,7},{4,6},{5,1},{6,4},{7,3},{8,10},{9,13},{10,... | collective-permute-start | bytes 2211848 | tf_op jit(solution)/shard_map/ppermute | solution.py:309
  5.4 18.9 %collective-permute-start.5 = (bf16[720,512]{1,0:T(8,128)(2,1)S(1)}, bf16[720,512]{1,0:T(8,128)(2,1)}, u32[]{:S(2)}, u32[]{:S(2)}) collective-permute-start(bf16[720,512]{1,0:T(8,128)(2,1)S(1)} %pack_kv.1.refs_2_), channel_id=1, source_target_pairs={{0,4},{1,3},{2,6},{3,1},{4,0},{5,7},{6,2},{7,5},{8,12},{9,11},{10,... | collective-permute-start | bytes 2211848 | tf_op jit(solution)/shard_map/ppermute | solution.py:309
  22.1 11.5 %collective-permute-start.1 = (bf16[720,512]{1,0:T(8,128)(2,1)S(1)}, bf16[720,512]{1,0:T(8,128)(2,1)S(1)}, u32[]{:S(2)}, u32[]{:S(2)}) collective-permute-start(bf16[720,512]{1,0:T(8,128)(2,1)S(1)} %collective-permute-done.refs_4_), channel_id=1, source_target_pairs={{0,4},{1,3},{2,6},{3,1},{4,0},{5,7},{6,2},{7,5},{8,12},{9,11},{10,... | collective-permute-start | bytes 2211848 | tf_op jit(solution)/shard_map/ppermute | solution.py:309
  23.8 33.6 %collective-permute-start.3 = (bf16[720,512]{1,0:T(8,128)(2,1)S(1)}, bf16[720,512]{1,0:T(8,128)(2,1)}, u32[]{:S(2)}, u32[]{:S(2)}) collective-permute-start(bf16[720,512]{1,0:T(8,128)(2,1)S(1)} %pack_kv.1.refs_2_), channel_id=1, source_target_pairs={{0,1},{1,0},{2,3},{3,2},{4,5},{5,4},{6,7},{7,6},{8,9},{9,8},{10,11... | collective-permute-start | bytes 2211848 | tf_op jit(solution)/shard_map/ppermute | solution.py:309
  23.8 33.6 %collective-permute-start.4 = (bf16[720,512]{1,0:T(8,128)(2,1)S(1)}, bf16[720,512]{1,0:T(8,128)(2,1)}, u32[]{:S(2)}, u32[]{:S(2)}) collective-permute-start(bf16[720,512]{1,0:T(8,128)(2,1)S(1)} %collective-permute-done.refs_4_), channel_id=1, source_target_pairs={{0,1},{1,0},{2,3},{3,2},{4,5},{5,4},{6,7},{7,6},{8,9},{9,8},{10,11... | collective-permute-start | bytes 2211848 | tf_op jit(solution)/shard_map/ppermute | solution.py:309
  24.3 33.1 %collective-permute-start.6 = (bf16[720,512]{1,0:T(8,128)(2,1)}, bf16[720,512]{1,0:T(8,128)(2,1)}, u32[]{:S(2)}, u32[]{:S(2)}) collective-permute-start(bf16[720,512]{1,0:T(8,128)(2,1)} %collective-permute-done.5.refs_6_), channel_id=1, source_target_pairs={{0,1},{1,0},{2,3},{3,2},{4,5},{5,4},{6,7},{7,6},{8,9},{9,8},{10,11... | collective-permute-start | bytes 2211848 | tf_op jit(solution)/shard_map/ppermute | solution.py:309
  33.6 28.6 %collective-permute-start.2 = (bf16[720,512]{1,0:T(8,128)(2,1)S(1)}, bf16[720,512]{1,0:T(8,128)(2,1)S(1)}, u32[]{:S(2)}, u32[]{:S(2)}) collective-permute-start(bf16[720,512]{1,0:T(8,128)(2,1)S(1)} %collective-permute-done.1.refs_2_), channel_id=1, source_target_pairs={{0,1},{1,0},{2,3},{3,2},{4,5},{5,4},{6,7},{7,6},{8,9},{9,8},{10,11... | collective-permute-start | bytes 2211848 | tf_op jit(solution)/shard_map/ppermute | solution.py:309
  33.6 1.3 %copy-start.1 = (bf16[2,32,128]{2,1,0:T(8,128)(2,1)S(1)}, bf16[2,32,128]{2,1,0:T(8,128)(2,1)}, u32[]{:S(2)}) copy-start(bf16[2,32,128]{2,1,0:T(8,128)(2,1)} %iq_ref.1) | copy-start | bytes 49156
  33.6 1.3 %copy-start.2 = (s32[2,2048]{1,0:T(2,128)S(1)}, s32[2,2048]{1,0:T(2,128)}, u32[]{:S(2)}) copy-start(s32[2,2048]{1,0:T(2,128)} %sel_ref.1) | copy-start | bytes 49156
  34.8 0.7 copy-start.3
  37.7 19.7 %collective-permute-start.7 = (bf16[336,512]{1,0:T(8,128)(2,1)S(1)}, bf16[336,512]{1,0:T(8,128)(2,1)S(1)}, u32[]{:S(2)}, u32[]{:S(2)}) collective-permute-start(bf16[336,512]{1,0:T(8,128)(2,1)S(1)} %get-tuple-element.15.refs_0_), channel_id=1, source_target_pairs={{0,8},{1,9},{2,10},{3,11},{4,12},{5,13},{6,14},{7,15},{8,0},{9,1},... | collective-permute-start | bytes 1032200 | tf_op jit(solution)/shard_map/ppermute | solution.py:309
  63.6 16.8 %collective-permute-start.8 = (bf16[304,512]{1,0:T(8,128)(2,1)S(1)}, bf16[304,512]{1,0:T(8,128)(2,1)S(1)}, u32[]{:S(2)}, u32[]{:S(2)}) collective-permute-start(bf16[304,512]{1,0:T(8,128)(2,1)S(1)} %attend_far_1.1), channel_id=1, source_target_pairs={{0,8},{1,9},{2,10},{3,11},{4,12},{5,13},{6,14},{7,15},{8,0},{9,1},... | collective-permute-start | bytes 933896 | tf_op jit(solution)/shard_map/ppermute | solution.py:309

commit v2 on v1

v2 whole, which is shorter than its diff:
```python
import functools

import jax
import jax.numpy as jnp
from jax import lax
from jax.experimental import pallas as pl
from jax.experimental.pallas import tpu as pltpu
from jax.sharding import PartitionSpec as P

BLOCK = 64
LANES = 512
KVR = 512
ROPE = 64
HEADS = 128
IH = 32
IDX = 128
TOK = 512
NEG = -1e30
LOG2E = 1.4426950408889634
TO_LOG2 = 192.0 ** (-0.5) * LOG2E

WIDTH = KVR + ROPE
ROWS = 2 * HEADS
CHUNKS = TOK // 128

I_W = 2 * IH
I_ROWS = I_W + 16
K_ROWS = TOK + 16

Q_IDX = 2 * WIDTH
Q_BIAS = Q_IDX + I_ROWS

BF = jnp.bfloat16
F32 = jnp.float32
VMEM = pl.BlockSpec(memory_space=pltpu.VMEM)
HBM = pl.BlockSpec(memory_space=pltpu.HBM)


def nn(a, b):
    return lax.dot_general(a, b, (((1,), (0,)), ((), ())), preferred_element_type=F32)


def nt(a, b):
    return lax.dot_general(a, b, (((1,), (1,)), ((), ())), preferred_element_type=F32)


def iota(shape, dim):
    return lax.broadcasted_iota(jnp.int32, shape, dim)


def onehot(cond):
    return jnp.where(cond, 1.0, 0.0).astype(BF)


def eye(n):
    return onehot(iota((n, n), 0) == iota((n, n), 1))


def pack_kernel(
    half_size, q_in, iq_in, w_in, keys_in, scale_in, sel_in, want_in, lat_in,
    wire_ref, own_ref, k_ref, lat_ref, w_ref, scale_ref, sel_ref, want_ref, bias, sems,
):
    moves = [
        (sel_in, sel_ref),
        (want_in, want_ref),
        (w_in, w_ref),
        (scale_in, scale_ref),
        (q_in, wire_ref.at[0:Q_IDX]),
        (iq_in, wire_ref.at[Q_IDX : Q_IDX + I_W]),
        (keys_in, k_ref.at[0:TOK]),
        (lat_in, lat_ref),
    ]
    copies = [
        pltpu.make_async_copy(src, dst, sems.at[k]) for k, (src, dst) in enumerate(moves)
    ]
    for copy in copies:
        copy.start()
    wire_ref[Q_IDX + I_W : Q_BIAS, :] = jnp.zeros((16, IDX), BF)
    k_ref[TOK:K_ROWS, :] = jnp.zeros((16, IDX), BF)
    for copy in copies[:4]:
        copy.wait()
    wire_ref[Q_IDX + I_W : Q_IDX + I_W + 2, 0:IH] = w_ref[...]
    k_ref[TOK : TOK + CHUNKS, :] = scale_ref[...]
    me = lax.axis_index("ctx")
    half = me // half_size
    n = 2 * half_size
    slots = want_ref.shape[0]
    topk = sel_ref.shape[1]
    asked = nt(eye(n), want_ref[...].astype(F32).astype(BF))
    lane_block = (iota((n, LANES), 1) // BLOCK).astype(F32)
    spread = onehot(iota((BLOCK, LANES), 1) % BLOCK == iota((BLOCK, LANES), 0))
    line = iota((slots * n, topk), 0)
    slot_of_line = (line % n) * slots + line // n
    for t in range(2):
        sel = sel_ref[t : t + 1, :]
        inner = onehot(sel % BLOCK == iota((BLOCK, topk), 0))
        count = nt(onehot(sel // BLOCK == slot_of_line), inner)
        wide = nn(count.astype(BF), spread)
        total = jnp.zeros((n, LANES), F32)
        for b in range(slots):
            total = total + jnp.where(
                lane_block == asked[:, b : b + 1], wide[b * n : (b + 1) * n, :], 0.0
            )
        bias[t] = jnp.where(total > 0.5, 0.0, NEG)
    mine = pl.multiple_of(half * half_size, half_size)
    other = pl.multiple_of((1 - half) * half_size, half_size)
    rows = 2 * half_size
    for c in range(CHUNKS):
        lanes = slice(c * 128, (c + 1) * 128)
        own_ref[c * rows : (c + 1) * rows, :] = jnp.concatenate(
            [bias[t, pl.ds(mine, half_size), lanes] for t in range(2)], axis=0
        ).astype(BF)
        wire_ref[Q_BIAS + c * rows : Q_BIAS + (c + 1) * rows, :] = jnp.concatenate(
            [bias[t, pl.ds(other, half_size), lanes] for t in range(2)], axis=0
        ).astype(BF)
    for copy in copies[4:]:
        copy.wait()


def unpack_kernel(half_size, own_ref, wire_ref, bias_ref, q_ref, out_ref, *more):
    for t in range(2):
        rows = nt(eye(HEADS), wire_ref[t * WIDTH : (t + 1) * WIDTH, :])
        q_ref[t * HEADS : (t + 1) * HEADS, :] = rows.astype(BF)
    rows = 2 * half_size
    base = bias_ref.shape[0] - CHUNKS * rows
    for c in range(CHUNKS):
        out_ref[:, c * 128 : (c + 1) * 128] = bias_ref[
            base + c * rows : base + (c + 1) * rows, :
        ].astype(F32)
    if more:
        (pair_ref,) = more
        pair_ref[0:I_ROWS, :] = own_ref[Q_IDX:Q_BIAS, :]
        pair_ref[I_ROWS : 2 * I_ROWS, :] = wire_ref[Q_IDX:Q_BIAS, :]


def split3(x):
    hi = x.astype(BF)
    rest = x - hi.astype(F32)
    mid = rest.astype(BF)
    return hi, mid, (rest - mid.astype(F32)).astype(BF)


def attend_kernel(half_size, masks, first, mode, *refs):
    count = len(masks)
    refs = list(refs)
    q_ref, bias_ref = refs[:2]
    pieces = refs[2 : 2 + count]
    pos = 2 + count
    if not first:
        acc_in, m_in, l_in = refs[pos : pos + 3]
        pos += 3
    outs = refs[pos:-1]
    logits = refs[-1]

    me = lax.axis_index("ctx")
    core = me % 2
    q = q_ref[...]
    m_prev = None if first else m_in[:, 0:1]
    m_new = m_prev
    for p in range(count):
        kv = pieces[p]
        src = lax.bitwise_xor(me, jnp.where(core == 0, masks[p][0], masks[p][1]))
        src = src % half_size
        s = nn(q, kv[0:WIDTH, :]) * TO_LOG2
        for t in range(2):
            part = s[t * HEADS : (t + 1) * HEADS, :] + bias_ref[pl.ds(t * half_size + src, 1), :]
            logits[t * HEADS : (t + 1) * HEADS, p * TOK : (p + 1) * TOK] = part
    top = jnp.max(logits[...], axis=1, keepdims=True)
    m_new = top if first else jnp.maximum(m_prev, top)

    total = None
    acc = None
    for p in range(count):
        e = jnp.exp2(logits[:, p * TOK : (p + 1) * TOK] - m_new)
        part = jnp.sum(e, axis=1, keepdims=True)
        total = part if total is None else total + part
        out = nt(e.astype(BF), pieces[p][0:KVR, :])
        acc = out if acc is None else acc + out
    if not first:
        alpha = jnp.exp2(m_prev - m_new)
        total = total + l_in[:, 0:1] * alpha
        acc = acc + acc_in[...] * alpha
    if mode == "state":
        acc_out, m_out, l_out = outs
        acc_out[...] = acc
        m_out[...] = jnp.broadcast_to(m_new, m_out.shape)
        l_out[...] = jnp.broadcast_to(total, l_out.shape)
        return
    norm = acc / total
    lse = m_new + jnp.log(total) * LOG2E
    if mode == "own":
        o_out, lse_out = outs
        o_out[...] = norm
        lse_out[...] = jnp.broadcast_to(lse, lse_out.shape)
        return
    (wire_out,) = outs
    wire_out[0:ROWS, :] = norm.astype(BF)
    diag = iota((ROWS, ROWS), 0) == iota((ROWS, ROWS), 1)
    row = jnp.sum(jnp.where(diag, lse, 0.0), axis=0, keepdims=True)
    hi, mid, lo = [x.astype(F32) for x in split3(row)]
    which = iota((16, ROWS), 0)
    left = jnp.where(which == 0, hi, jnp.where(which == 1, lo, 0.0))
    right = jnp.where(which == 0, mid, 0.0)
    wire_out[ROWS : ROWS + 16, 0:ROWS] = left.astype(BF)
    wire_out[ROWS : ROWS + 16, ROWS : 2 * ROWS] = right.astype(BF)


def score_kernel(count, *refs):
    pairs, keys, outs = refs[:count], refs[count : count + 4], refs[count + 4 :]
    me = lax.axis_index("ctx")
    unit = eye(IH)
    for pair, out in zip(pairs, outs):
        starts = (0, I_ROWS)
        both = jnp.concatenate([pair[k : k + I_W, :] for k in starts], axis=0)
        w_cols = [nt(unit, pair[k + I_W : k + I_ROWS, 0:IH]) for k in starts]
        for p in range(4):
            raw = jnp.maximum(nt(both, keys[p][0:TOK, :]), 0.0)
            scales = keys[p][TOK:K_ROWS, :].astype(F32)
            scale = jnp.concatenate([scales[c : c + 1, :] for c in range(CHUNKS)], axis=1)
            at = pl.multiple_of(lax.bitwise_and(lax.bitwise_xor(me, p), 3) * TOK, TOK)
            for side in range(2):
                for t in range(2):
                    row = side * 2 + t
                    weighted = raw[row * IH : (row + 1) * IH, :] * w_cols[side][:, t : t + 1]
                    line = jnp.sum(weighted, axis=0, keepdims=True) * scale
                    out[row : row + 1, pl.ds(at, TOK)] = line


def order_kernel(half_size, masks, *refs):
    me = lax.axis_index("ctx")
    own_ref, far_ref = refs[-2:]
    span = 4 * TOK
    for ref, mask in zip(refs, masks):
        at = lax.bitwise_and(lax.bitwise_xor(me, mask), half_size - 1) // 4 * span
        at = pl.multiple_of(at, span)
        own_ref[:, pl.ds(at, span)] = ref[0:2, :]
        far_ref[:, pl.ds(at, span)] = ref[2:4, :]


def halves_kernel(half_size, own_ref, far_ref, out_ref):
    half = lax.axis_index("ctx") // half_size
    width = half_size * TOK
    out_ref[:, pl.ds(pl.multiple_of(half * width, width), width)] = own_ref[...]
    out_ref[:, pl.ds(pl.multiple_of((1 - half) * width, width), width)] = far_ref[...]


def final_kernel(o_ref, lse_ref, wire_ref, out_ref):
    stats = wire_ref[ROWS : ROWS + 16, :].astype(F32)
    row = stats[0:1, 0:ROWS] + stats[0:1, ROWS : 2 * ROWS] + stats[1:2, 0:ROWS]
    diag = iota((ROWS, ROWS), 0) == iota((ROWS, ROWS), 1)
    lse_r = jnp.sum(jnp.where(diag, row, 0.0), axis=1, keepdims=True)
    lse_o = lse_ref[:, 0:1]
    top = jnp.maximum(lse_r, lse_o)
    e_r = jnp.exp2(lse_r - top)
    e_o = jnp.exp2(lse_o - top)
    inv = 1.0 / (e_r + e_o)
    out = o_ref[...] * (e_o * inv) + wire_ref[0:ROWS, :].astype(F32) * (e_r * inv)
    for t in range(2):
        out_ref[t] = out[t * HEADS : (t + 1) * HEADS, :].astype(BF)


def call(kernel, out_shape, name, flops, *args, scratch=(), specs=None, limit=48 << 20):
    moved = sum(a.size * a.dtype.itemsize for a in args)
    return pl.pallas_call(
        kernel,
        out_shape=out_shape,
        in_specs=specs or [VMEM] * len(args),
        out_specs=jax.tree.map(lambda _: VMEM, out_shape),
        scratch_shapes=list(scratch),
        name=name,
        cost_estimate=pl.CostEstimate(flops=int(flops), bytes_accessed=moved, transcendentals=0),
        compiler_params=pltpu.CompilerParams(vmem_limit_bytes=limit),
    )(*args)


def shape(dims, dtype):
    return jax.ShapeDtypeStruct(dims, dtype)


def attend(half_size, q, bias, group, state, mode, name):
    masks = tuple(mask for _, mask in group)
    args = [q, bias] + [piece for piece, _ in group]
    state_shape = (shape((ROWS, KVR), F32), shape((ROWS, 128), F32), shape((ROWS, 128), F32))
    if state is not None:
        args += list(state)
    if mode == "state":
        outs = state_shape
    elif mode == "wire":
        outs = shape((ROWS + 16, LANES), BF)
    else:
        outs = state_shape[:2]
    scratch = [pltpu.VMEM((ROWS, TOK * len(group)), F32)]
    flops = 2 * ROWS * TOK * len(group) * (2 * KVR + ROPE)
    return call(
        functools.partial(attend_kernel, half_size, masks, state is None, mode),
        outs,
        name,
        flops,
        *args,
        scratch=scratch,
    )


def local(n, index_queries, index_weights, index_keys, key_scales, q_latent, latents, wanted, selected):
    half_size = n // 2
    bits = n.bit_length() - 1
    top = 1 << (bits - 1)

    def permute(x, move):
        return lax.ppermute(x, "ctx", [(i, move(i)) for i in range(n)])

    def swap(x):
        return permute(x, lambda i: i ^ 1)

    def first(i):
        return i ^ 2 if i % 2 == 0 else i ^ 4

    def second(i):
        return i ^ 4 if i % 2 == 0 else i ^ 2

    kv = latents.T
    r1 = permute(kv, first)

    rows = 2 * half_size
    q_wire, bias_own, k_wire, kv_here = call(
        functools.partial(pack_kernel, half_size),
        (
            shape((Q_BIAS + CHUNKS * rows, 128), BF),
            shape((CHUNKS * rows, 128), BF),
            shape((K_ROWS, IDX), BF),
            shape((WIDTH, TOK), BF),
        ),
        "pack",
        2 * 2 * n * 4 * 2048 * 64,
        jnp.swapaxes(q_latent, 1, 2).reshape(2 * WIDTH, HEADS),
        index_queries.reshape(2 * IH, IDX),
        index_weights,
        index_keys,
        key_scales.reshape(CHUNKS, 128),
        selected,
        wanted[0].T,
        kv,
        specs=[HBM] * 8,
        limit=None,
        scratch=[
            pltpu.VMEM((2, IH), BF),
            pltpu.VMEM((CHUNKS, 128), BF),
            pltpu.VMEM(selected.shape, jnp.int32),
            pltpu.VMEM((wanted.shape[2], n), jnp.int32),
            pltpu.VMEM((2, n, LANES), F32),
            pltpu.SemaphoreType.DMA((8,)),
        ],
    )
    q_far = permute(q_wire, lambda i: i ^ top)
    r2 = permute(kv, second)
    q_far, r2 = lax.optimization_barrier((q_far, r2))
    r3 = permute(r1, second)
    held = [(kv_here, (0, 0)), (r1, (2, 4)), (r2, (4, 2)), (r3, (6, 6))]
    for bit in range(3, bits - 1):
        step = 1 << bit
        held = held + [
            (permute(piece, lambda i: i ^ step), (a ^ step, b ^ step)) for piece, (a, b) in held
        ]

    k_next = permute(k_wire, lambda i: i ^ 2)
    keys = [k_wire, swap(k_wire), k_next, swap(k_next)]

    def unpack(wire, bias, name, flops, more=()):
        return call(
            functools.partial(unpack_kernel, half_size),
            (shape((ROWS, WIDTH), BF), shape((rows, TOK), F32), *more),
            name,
            flops,
            q_wire,
            wire,
            bias,
        )

    q_far, *keys = lax.optimization_barrier((q_far, *keys))
    q_there, bias_there, i_pair = unpack(
        q_far, q_far, "unpack_far", 3 * 1.15e9, [shape((2 * I_ROWS, IDX), BF)]
    )
    i_pairs = [i_pair]
    for bit in range(2, bits - 1):
        step = 1 << bit
        i_pairs = i_pairs + [permute(x, lambda i: i ^ step) for x in i_pairs]
    q_here, bias_here = unpack(q_wire, bias_own, "unpack_own", 0)

    def pair(item):
        piece, (a, b) = item
        return [item, (swap(piece), (1 ^ b, 1 ^ a))]

    def run(q, bias, groups, last, name, state=None):
        for k, group in enumerate(groups):
            mode = last if k == len(groups) - 1 else "state"
            state = attend(half_size, q, bias, group, state, mode, f"{name}_{k}")
        return state

    near = [pair(item) for item in held[:3]]
    (own0, own1), (r1a, r1b), (r2a, r2b) = near
    far = attend(half_size, q_there, bias_there, [own0, own1, r1a, r2a], None, "state", "far_early")
    far, r3, *i_pairs = lax.optimization_barrier((far, r3, *i_pairs))
    held[3] = (r3, held[3][1])
    late = [pair(item) for item in held[3:]]
    rest = sum(late[1:], [])
    groups = [[r1b, r2b, late[0][0]], [late[0][1]]]
    groups += [rest[at : at + 6] for at in range(0, len(rest), 6)]
    wire = run(q_there, bias_there, groups, "wire", "far_late", far)
    o_far = permute(wire, lambda i: i ^ top)

    parts = call(
        functools.partial(score_kernel, len(i_pairs)),
        tuple(shape((4, 4 * TOK), F32) for _ in i_pairs),
        "index_scores",
        2 * len(i_pairs) * 4 * IH * 4 * TOK * IDX,
        *i_pairs,
        *keys,
    )
    parts = [[(part, 0)] for part in parts]
    for bit in reversed(range(2, bits - 1)):
        step = 1 << bit
        count = len(parts) // 2
        parts = [
            parts[j] + [(permute(x, lambda i: i ^ step), mask ^ step) for x, mask in parts[j + count]]
            for j in range(count)
        ]
    ranges = parts[0]
    scores_own, scores_far = call(
        functools.partial(order_kernel, half_size, tuple(mask for _, mask in ranges)),
        (shape((2, half_size * TOK), F32), shape((2, half_size * TOK), F32)),
        "order_scores",
        0,
        *[x for x, _ in ranges],
    )
    scores_far = permute(scores_far, lambda i: i ^ top)
    late = [sum(near + late[:1], [])] + groups[2:]
    o_own, lse_own = run(q_here, bias_here, late, "own", "own_late")
    attended = call(
        final_kernel,
        shape((2, HEADS, KVR), BF),
        "combine",
        10 * 1.15e9,
        o_own,
        lse_own,
        o_far,
    )
    attended, scores_far = lax.optimization_barrier((attended, scores_far))
    scores = call(
        functools.partial(halves_kernel, half_size),
        shape((2, n * TOK), F32),
        "join_scores",
        0,
        scores_own,
        scores_far,
    )
    return scores, attended


def solution(mesh):
    spec = P(("groups", "ctx"))
    return jax.shard_map(
        functools.partial(local, mesh.shape["ctx"]),
        mesh=mesh,
        in_specs=(spec,) * 8,
        out_specs=(spec, spec),
        check_vma=False,
    )
```

time: 81.6 us -> 53.6 us (0.66)
  waiting for transfers between devices: 51.2 us -> 14.2 us
  starting transfers between devices: 10.4 us -> 24.5 us
  Pallas kernels: 15.8 us -> 12.9 us
  local copies, waits for them, and re-layouts: 3.24 us -> 0.99 us
    ppermute x9 -> x15, waiting for transfers between devices: 51.2 us -> 14.2 us  [permute(): return lax.ppermute(x, 'ctx', [(i, move(i)) for i in range(n)])]
    ppermute x9 -> x15, starting transfers between devices: 10.4 us -> 24.5 us  [permute(): return lax.ppermute(x, 'ctx', [(i, move(i)) for i in range(n)])]
    pallas_call x7 -> x11, Pallas kernels: 15.8 us -> 12.9 us  [call(): pl.pallas_call(kernel, out_shape=out_shape, in_specs=specs or [VMEM] * le...]
    unnamed x15 -> x10, local copies, waits for them, and re-layouts: 3.24 us -> 0.99 us
  transfers between devices with their start and end apart: 9 -> 15, of which waited for: 4 -> 8; matrix products, arithmetic and copies ran while one was open for 2% -> 0% of each run, Pallas kernels for 16% -> 22%
where the time goes in v2:
time: 53.6 us; the launch traced here: 53.4 us
  starting transfers between devices  24.5 us (46%)
  waiting for transfers between devices  14.2 us (26%)
  Pallas kernels  12.9 us (24%)
  local copies, waits for them, and re-layouts  0.99 us (2%)
  between operations  0.74 us (1%)
    ppermute x15, starting transfers between devices, permute(): return lax.ppermute(x, 'ctx', [(i, move(i)) for i in range(n)])  24.5 us
    ppermute x15, waiting for transfers between devices, permute(): return lax.ppermute(x, 'ctx', [(i, move(i)) for i in range(n)])  14.2 us
    pallas_call x11, Pallas kernels, call(): pl.pallas_call(kernel, out_shape=out_shape, in_specs=specs or [VMEM] * le...  12.9 us
  transfers between devices with their start and end apart: 15, of which 8 were waited for; matrix products, arithmetic and copies ran while one was open for 0% of the time, Pallas kernels for 22%

profile of v2, /device:TPU:0, one launch (start us, length us, event | category | flops | bytes accessed | tf_op | source)
XLA Modules:
  0.0 53.4 jit_solution(8602965361055920622)
XLA Ops:
  0.6 3.0 %collective-permute-start.6 = (bf16[576,512]{1,0:T(8,128)(2,1)}, bf16[576,512]{1,0:T(8,128)(2,1)S(1)}, u32[]{:S(2)}, u32[]{:S(2)}) collective-permute-start(bf16[576,512]{1,0:T(8,128)(2,1)} %bitcast.9), channel_id=1, source_target_pairs={{0,2},{1,5},{2,0},{3,7},{4,6},{5,1},{6,4},{7,3},{8,10},{9,13},{10,... | collective-permute-start | bytes 1769480 | tf_op jit(solution)/shard_map/ppermute | solution.py:310
  3.7 1.6 %collective-permute-start.1 = (bf16[576,512]{1,0:T(8,128)(2,1)}, bf16[576,512]{1,0:T(8,128)(2,1)S(1)}, u32[]{:S(2)}, u32[]{:S(2)}) collective-permute-start(bf16[576,512]{1,0:T(8,128)(2,1)} %bitcast.10), channel_id=1, source_target_pairs={{0,4},{1,3},{2,6},{3,1},{4,0},{5,7},{6,2},{7,5},{8,12},{9,11},{10,... | collective-permute-start | bytes 1769480 | tf_op jit(solution)/shard_map/ppermute | solution.py:310
  5.2 2.5 %pack.1 = (bf16[1296,128]{1,0:T(8,128)(2,1)}, bf16[64,128]{1,0:T(8,128)(2,1)}, bf16[528,128]{1,0:T(8,128)(2,1)}, bf16[576,512]{1,0:T(8,128)(2,1)}) custom-call(bf16[1152,128]{1,0:T(8,128)(2,1)} %bitcast.12, bf16[64,128]{1,0:T(8,128)(2,1)} %bitcast.13, bf16[2,32]{1,0:T(2,128)(2,1)} %w_in.1, bf16[512,128]{1,0:T(8,128)(2,1)} %keys_in.1, ...), custom_call_target="tpu_custom_call" | custom-call | flops 33554432 | bytes 1049984 | tf_op jit(solution)/shard_map/pack/pallas_call | solution.py:264
  7.8 2.7 %collective-permute-start = (bf16[1296,128]{1,0:T(8,128)(2,1)}, bf16[1296,128]{1,0:T(8,128)(2,1)S(1)}, u32[]{:S(2)}, u32[]{:S(2)}) collective-permute-start(bf16[1296,128]{1,0:T(8,128)(2,1)} %get-tuple-element.38.own_ref.wire_ref), channel_id=1, source_target_pairs={{0,8},{1,9},{2,10},{3,11},{4,12},{5,13},{6,14},{7,15},{8,0},{9,1},... | collective-permute-start | bytes 995336 | tf_op jit(solution)/shard_map/ppermute | solution.py:310
  10.4 0.5 collective-permute-start.3
  10.9 0.0 collective-permute-start.5
  10.9 6.6 %collective-permute-done.6.refs_4_ = bf16[576,512]{1,0:T(8,128)(2,1)S(1)} collective-permute-done((bf16[576,512]{1,0:T(8,128)(2,1)}, bf16[576,512]{1,0:T(8,128)(2,1)S(1)}, u32[]{:S(2)}, u32[]{:S(2)}) %collective-permute-start.6) | collective-permute-done | bytes 589856 | tf_op jit(solution)/shard_map/ppermute | solution.py:310
  17.5 2.6 %collective-permute-start.7 = (bf16[576,512]{1,0:T(8,128)(2,1)S(1)}, bf16[576,512]{1,0:T(8,128)(2,1)S(1)}, u32[]{:S(2)}, u32[]{:S(2)}) collective-permute-start(bf16[576,512]{1,0:T(8,128)(2,1)S(1)} %collective-permute-done.6.refs_4_), channel_id=1, source_target_pairs={{0,4},{1,3},{2,6},{3,1},{4,0},{5,7},{6,2},{7,5},{8,12},{9,11},{10,... | collective-permute-start | bytes 1769480 | tf_op jit(solution)/shard_map/ppermute | solution.py:310
  20.1 0.3 collective-permute-done.3.refs_4_
  20.4 4.2 %collective-permute-start.2 = (bf16[528,128]{1,0:T(8,128)(2,1)}, bf16[528,128]{1,0:T(8,128)(2,1)S(1)}, u32[]{:S(2)}, u32[]{:S(2)}) collective-permute-start(bf16[528,128]{1,0:T(8,128)(2,1)} %get-tuple-element.52.refs_2_), channel_id=1, source_target_pairs={{0,1},{1,0},{2,3},{3,2},{4,5},{5,4},{6,7},{7,6},{8,9},{9,8},{10,11... | collective-permute-start | bytes 405512 | tf_op jit(solution)/shard_map/ppermute | solution.py:310
  24.6 0.0 collective-permute-done.wire_ref.bias_ref
  24.6 0.1 collective-permute-start.4
  24.7 0.0 collective-permute-done.1.refs_5_.refs_6_
  24.7 1.1 %collective-permute-done.2.refs_3_ = bf16[528,128]{1,0:T(8,128)(2,1)S(1)} collective-permute-done((bf16[528,128]{1,0:T(8,128)(2,1)}, bf16[528,128]{1,0:T(8,128)(2,1)S(1)}, u32[]{:S(2)}, u32[]{:S(2)}) %collective-permute-start.2) | collective-permute-done | bytes 135200 | tf_op jit(solution)/shard_map/ppermute | solution.py:310
  25.8 0.2 collective-permute-done.4.refs_5_
  26.0 0.0 copy-start
  26.0 1.0 %copy-done = bf16[1296,128]{1,0:T(8,128)(2,1)S(1)} copy-done((bf16[1296,128]{1,0:T(8,128)(2,1)S(1)}, bf16[1296,128]{1,0:T(8,128)(2,1)}, u32[]{:S(2)}) %copy-start) | copy-done | bytes 331800
  27.0 0.0 copy-start.4
  27.0 0.3 unpack_far.1
  27.2 2.5 %collective-permute-start.8 = (bf16[160,128]{1,0:T(8,128)(2,1)S(1)}, bf16[160,128]{1,0:T(8,128)(2,1)S(1)}, u32[]{:S(2)}, u32[]{:S(2)}) collective-permute-start(bf16[160,128]{1,0:T(8,128)(2,1)S(1)} %get-tuple-element.50.refs_0_), channel_id=1, source_target_pairs={{0,4},{1,5},{2,6},{3,7},{4,0},{5,1},{6,2},{7,3},{8,12},{9,13},{10,... | collective-permute-start | bytes 122888 | tf_op jit(solution)/shard_map/ppermute | solution.py:310
  29.8 0.0 collective-permute-start.11
  29.8 0.5 collective-permute-start.10
  30.3 0.0 collective-permute-done.5.refs_3_
  30.3 0.0 copy-done.4
  30.3 1.8 %far_early.1 = (f32[256,512]{1,0:T(8,128)S(1)}, f32[256,128]{1,0:T(8,128)S(1)}, f32[256,128]{1,0:T(8,128)S(1)}) custom-call(bf16[256,576]{1,0:T(8,128)(2,1)S(1)} %get-tuple-element.42.refs_0_, f32[16,512]{1,0:T(8,128)S(1)} %get-tuple-element.43.refs_1_, bf16[576,512]{1,0:T(8,128)(2,1)S(1)} %copy-done.4, bf16[576,512]{1,0:T(8,128)(2,1)S(1)} %collective-permute-done.5.refs_3_, ...), custom_call_target="tpu_custom_call" | custom-call | flops 1140850688 | bytes 2686976 | tf_op jit(solution)/shard_map/far_early/pallas_call | solution.py:264
  32.1 0.0 collective-permute-done.8.refs_1_
  32.2 0.0 collective-permute-done.7.refs_8_.refs_4_
  32.2 0.1 collective-permute-start.12
  32.2 0.4 collective-permute-done.10.refs_5_.refs_2_
  32.6 0.0 collective-permute-done.11.refs_7_.refs_3_
  32.6 1.5 %far_late_0.1 = (f32[256,512]{1,0:T(8,128)S(1)}, f32[256,128]{1,0:T(8,128)S(1)}, f32[256,128]{1,0:T(8,128)S(1)}) custom-call(bf16[256,576]{1,0:T(8,128)(2,1)S(1)} %get-tuple-element.42.refs_0_, f32[16,512]{1,0:T(8,128)S(1)} %get-tuple-element.43.refs_1_, bf16[576,512]{1,0:T(8,128)(2,1)S(1)} %collective-permute-done.10.refs_5_.refs_2_, ...), custom_call_target="tpu_custom_call" | custom-call | flops 855638016 | bytes 2883584 | tf_op jit(solution)/shard_map/far_late_0/pallas_call | solution.py:264
  34.2 0.1 collective-permute-done.12.refs_9_.refs_2_
  34.2 0.0 copy-start.2
  34.2 0.8 %far_late_1.1 = bf16[272,512]{1,0:T(8,128)(2,1)S(1)} custom-call(bf16[256,576]{1,0:T(8,128)(2,1)S(1)} %get-tuple-element.42.refs_0_, f32[16,512]{1,0:T(8,128)S(1)} %get-tuple-element.43.refs_1_, bf16[576,512]{1,0:T(8,128)(2,1)S(1)} %collective-permute-done.12.refs_9_.refs_2_, f32[256,512]{1,0:T(8,128)S(1)} %get-tuple-element.68.refs_3_, ...), custom_call_target="tpu_custom_call" | custom-call | flops 285212672 | bytes 1703936 | tf_op jit(solution)/shard_map/far_late_1/pallas_call | solution.py:264
  35.0 0.0 copy-start.1
  35.0 0.0 copy-start.3
  35.0 2.2 %collective-permute-start.13 = (bf16[272,512]{1,0:T(8,128)(2,1)S(1)}, bf16[272,512]{1,0:T(8,128)(2,1)S(1)}, u32[]{:S(2)}, u32[]{:S(2)}) collective-permute-start(bf16[272,512]{1,0:T(8,128)(2,1)S(1)} %far_late_1.1), channel_id=1, source_target_pairs={{0,8},{1,9},{2,10},{3,11},{4,12},{5,13},{6,14},{7,15},{8,0},{9,1},... | collective-permute-start | bytes 835592 | tf_op jit(solution)/shard_map/ppermute | solution.py:310
  37.2 0.0 copy-done.2
  37.2 0.6 %index_scores.1 = (f32[4,2048]{1,0:T(4,128)S(1)}, f32[4,2048]{1,0:T(4,128)S(1)}) custom-call(bf16[160,128]{1,0:T(8,128)(2,1)S(1)} %get-tuple-element.50.refs_0_, bf16[160,128]{1,0:T(8,128)(2,1)S(1)} %collective-permute-done.8.refs_1_, bf16[528,128]{1,0:T(8,128)(2,1)S(1)} %copy-done.2, bf16[528,128]{1,0:T(8,128)(2,1)S(1)} %collective-permute-done.2.refs_3_, ...), custom_call_target="tpu_custom_call" | custom-call | flops 134217728 | bytes 622592 | tf_op jit(solution)/shard_map/index_scores/pallas_call | solution.py:264
  37.8 1.7 %collective-permute-start.9 = (f32[4,2048]{1,0:T(4,128)S(1)}, f32[4,2048]{1,0:T(4,128)S(1)}, u32[]{:S(2)}, u32[]{:S(2)}) collective-permute-start(f32[4,2048]{1,0:T(4,128)S(1)} %get-tuple-element.57), channel_id=1, source_target_pairs={{0,4},{1,5},{2,6},{3,7},{4,0},{5,1},{6,2},{7,3},{8,12},{9,13},{10,... | collective-permute-start | bytes 98312 | tf_op jit(solution)/shard_map/ppermute | solution.py:310
  39.4 0.0 copy-done.1
  39.4 0.0 copy-done.3
  39.4 0.3 unpack_own.1
  39.7 4.4 %collective-permute-done.9.refs_1_ = f32[4,2048]{1,0:T(4,128)S(1)} collective-permute-done((f32[4,2048]{1,0:T(4,128)S(1)}, f32[4,2048]{1,0:T(4,128)S(1)}, u32[]{:S(2)}, u32[]{:S(2)}) %collective-permute-start.9) | collective-permute-done | bytes 32800 | tf_op jit(solution)/shard_map/ppermute | solution.py:310
  44.2 2.9 %collective-permute-start.14 = (f32[2,4096]{1,0:T(2,128)S(1)}, f32[2,4096]{1,0:T(2,128)S(1)}, u32[]{:S(2)}, u32[]{:S(2)}) collective-permute-start(f32[2,4096]{1,0:T(2,128)S(1)} %get-tuple-element.71), channel_id=1, source_target_pairs={{0,8},{1,9},{2,10},{3,11},{4,12},{5,13},{6,14},{7,15},{8,0},{9,1},... | collective-permute-start | bytes 98312 | tf_op jit(solution)/shard_map/ppermute | solution.py:310
  47.1 3.5 %own_late_0.1 = (f32[256,512]{1,0:T(8,128)S(1)}, f32[256,128]{1,0:T(8,128)S(1)}) custom-call(bf16[256,576]{1,0:T(8,128)(2,1)S(1)} %get-tuple-element.60.refs_0_, f32[16,512]{1,0:T(8,128)S(1)} %get-tuple-element.61.refs_1_, bf16[576,512]{1,0:T(8,128)(2,1)S(1)} %copy-done.4, bf16[576,512]{1,0:T(8,128)(2,1)S(1)} %collective-permute-done.5.refs_3_, ...), custom_call_target="tpu_custom_call" | custom-call | flops 2281701376 | bytes 5046272 | tf_op jit(solution)/shard_map/own_late_0/pallas_call | solution.py:264
  50.6 1.1 %collective-permute-done.13.wire_ref = bf16[272,512]{1,0:T(8,128)(2,1)S(1)} collective-permute-done((bf16[272,512]{1,0:T(8,128)(2,1)S(1)}, bf16[272,512]{1,0:T(8,128)(2,1)S(1)}, u32[]{:S(2)}, u32[]{:S(2)}) %collective-permute-start.13) | collective-permute-done | bytes 278560 | tf_op jit(solution)/shard_map/ppermute | solution.py:310
  51.7 1.0 %combine.1 = bf16[2,128,512]{2,1,0:T(8,128)(2,1)} custom-call(f32[256,512]{1,0:T(8,128)S(1)} %get-tuple-element.63.o_ref, f32[256,128]{1,0:T(8,128)S(1)} %get-tuple-element.64.lse_ref, bf16[272,512]{1,0:T(8,128)(2,1)S(1)} %collective-permute-done.13.wire_ref), custom_call_target="tpu_custom_call" | custom-call | flops 11500000256 | bytes 933888 | tf_op jit(solution)/shard_map/combine/pallas_call | solution.py:264
  52.7 0.0 collective-permute-done.14.far_ref
  52.7 0.6 %join_scores.1 = f32[2,8192]{1,0:T(2,128)} custom-call(f32[2,4096]{1,0:T(2,128)S(1)} %get-tuple-element.58.own_ref, f32[2,4096]{1,0:T(2,128)S(1)} %collective-permute-done.14.far_ref), custom_call_target="tpu_custom_call" | custom-call | bytes 65536 | tf_op jit(solution)/shard_map/join_scores/pallas_call | solution.py:264
  (1 shorter events, 0.0 us)
Async XLA Ops:
  0.6 16.9 %collective-permute-start.6 = (bf16[576,512]{1,0:T(8,128)(2,1)}, bf16[576,512]{1,0:T(8,128)(2,1)S(1)}, u32[]{:S(2)}, u32[]{:S(2)}) collective-permute-start(bf16[576,512]{1,0:T(8,128)(2,1)} %bitcast.9), channel_id=1, source_target_pairs={{0,2},{1,5},{2,0},{3,7},{4,6},{5,1},{6,4},{7,3},{8,10},{9,13},{10,... | collective-permute-start | bytes 1769480 | tf_op jit(solution)/shard_map/ppermute | solution.py:310
  3.7 21.0 %collective-permute-start.1 = (bf16[576,512]{1,0:T(8,128)(2,1)}, bf16[576,512]{1,0:T(8,128)(2,1)S(1)}, u32[]{:S(2)}, u32[]{:S(2)}) collective-permute-start(bf16[576,512]{1,0:T(8,128)(2,1)} %bitcast.10), channel_id=1, source_target_pairs={{0,4},{1,3},{2,6},{3,1},{4,0},{5,7},{6,2},{7,5},{8,12},{9,11},{10,... | collective-permute-start | bytes 1769480 | tf_op jit(solution)/shard_map/ppermute | solution.py:310
  7.8 16.9 %collective-permute-start = (bf16[1296,128]{1,0:T(8,128)(2,1)}, bf16[1296,128]{1,0:T(8,128)(2,1)S(1)}, u32[]{:S(2)}, u32[]{:S(2)}) collective-permute-start(bf16[1296,128]{1,0:T(8,128)(2,1)} %get-tuple-element.38.own_ref.wire_ref), channel_id=1, source_target_pairs={{0,8},{1,9},{2,10},{3,11},{4,12},{5,13},{6,14},{7,15},{8,0},{9,1},... | collective-permute-start | bytes 995336 | tf_op jit(solution)/shard_map/ppermute | solution.py:310
  10.4 10.0 %collective-permute-start.3 = (bf16[528,128]{1,0:T(8,128)(2,1)}, bf16[528,128]{1,0:T(8,128)(2,1)S(1)}, u32[]{:S(2)}, u32[]{:S(2)}) collective-permute-start(bf16[528,128]{1,0:T(8,128)(2,1)} %get-tuple-element.52.refs_2_), channel_id=1, source_target_pairs={{0,2},{1,3},{2,0},{3,1},{4,6},{5,7},{6,4},{7,5},{8,10},{9,11},{10,... | collective-permute-start | bytes 405512 | tf_op jit(solution)/shard_map/ppermute | solution.py:310
  10.9 19.4 %collective-permute-start.5 = (bf16[576,512]{1,0:T(8,128)(2,1)}, bf16[576,512]{1,0:T(8,128)(2,1)S(1)}, u32[]{:S(2)}, u32[]{:S(2)}) collective-permute-start(bf16[576,512]{1,0:T(8,128)(2,1)} %get-tuple-element.44.refs_2_), channel_id=1, source_target_pairs={{0,1},{1,0},{2,3},{3,2},{4,5},{5,4},{6,7},{7,6},{8,9},{9,8},{10,11... | collective-permute-start | bytes 1769480 | tf_op jit(solution)/shard_map/ppermute | solution.py:310
  17.5 14.6 %collective-permute-start.7 = (bf16[576,512]{1,0:T(8,128)(2,1)S(1)}, bf16[576,512]{1,0:T(8,128)(2,1)S(1)}, u32[]{:S(2)}, u32[]{:S(2)}) collective-permute-start(bf16[576,512]{1,0:T(8,128)(2,1)S(1)} %collective-permute-done.6.refs_4_), channel_id=1, source_target_pairs={{0,4},{1,3},{2,6},{3,1},{4,0},{5,7},{6,2},{7,5},{8,12},{9,11},{10,... | collective-permute-start | bytes 1769480 | tf_op jit(solution)/shard_map/ppermute | solution.py:310
  20.4 5.4 %collective-permute-start.2 = (bf16[528,128]{1,0:T(8,128)(2,1)}, bf16[528,128]{1,0:T(8,128)(2,1)S(1)}, u32[]{:S(2)}, u32[]{:S(2)}) collective-permute-start(bf16[528,128]{1,0:T(8,128)(2,1)} %get-tuple-element.52.refs_2_), channel_id=1, source_target_pairs={{0,1},{1,0},{2,3},{3,2},{4,5},{5,4},{6,7},{7,6},{8,9},{9,8},{10,11... | collective-permute-start | bytes 405512 | tf_op jit(solution)/shard_map/ppermute | solution.py:310
  24.6 1.4 %collective-permute-start.4 = (bf16[528,128]{1,0:T(8,128)(2,1)S(1)}, bf16[528,128]{1,0:T(8,128)(2,1)S(1)}, u32[]{:S(2)}, u32[]{:S(2)}) collective-permute-start(bf16[528,128]{1,0:T(8,128)(2,1)S(1)} %collective-permute-done.3.refs_4_), channel_id=1, source_target_pairs={{0,1},{1,0},{2,3},{3,2},{4,5},{5,4},{6,7},{7,6},{8,9},{9,8},{10,11... | collective-permute-start | bytes 405512 | tf_op jit(solution)/shard_map/ppermute | solution.py:310
  26.0 1.0 %copy-start = (bf16[1296,128]{1,0:T(8,128)(2,1)S(1)}, bf16[1296,128]{1,0:T(8,128)(2,1)}, u32[]{:S(2)}) copy-start(bf16[1296,128]{1,0:T(8,128)(2,1)} %get-tuple-element.38.own_ref.wire_ref) | copy-start | bytes 995332
  27.0 3.3 %copy-start.4 = (bf16[576,512]{1,0:T(8,128)(2,1)S(1)}, bf16[576,512]{1,0:T(8,128)(2,1)}, u32[]{:S(2)}) copy-start(bf16[576,512]{1,0:T(8,128)(2,1)} %get-tuple-element.44.refs_2_) | copy-start | bytes 1769476
  27.2 4.9 %collective-permute-start.8 = (bf16[160,128]{1,0:T(8,128)(2,1)S(1)}, bf16[160,128]{1,0:T(8,128)(2,1)S(1)}, u32[]{:S(2)}, u32[]{:S(2)}) collective-permute-start(bf16[160,128]{1,0:T(8,128)(2,1)S(1)} %get-tuple-element.50.refs_0_), channel_id=1, source_target_pairs={{0,4},{1,5},{2,6},{3,7},{4,0},{5,1},{6,2},{7,3},{8,12},{9,13},{10,... | collective-permute-start | bytes 122888 | tf_op jit(solution)/shard_map/ppermute | solution.py:310
  29.8 2.9 %collective-permute-start.11 = (bf16[576,512]{1,0:T(8,128)(2,1)S(1)}, bf16[576,512]{1,0:T(8,128)(2,1)S(1)}, u32[]{:S(2)}, u32[]{:S(2)}) collective-permute-start(bf16[576,512]{1,0:T(8,128)(2,1)S(1)} %collective-permute-done.1.refs_5_.refs_6_), channel_id=1, source_target_pairs={{0,1},{1,0},{2,3},{3,2},{4,5},{5,4},{6,7},{7,6},{8,9},{9,8},{10,11... | collective-permute-start | bytes 1769480 | tf_op jit(solution)/shard_map/ppermute | solution.py:310
  29.8 2.8 %collective-permute-start.10 = (bf16[576,512]{1,0:T(8,128)(2,1)S(1)}, bf16[576,512]{1,0:T(8,128)(2,1)S(1)}, u32[]{:S(2)}, u32[]{:S(2)}) collective-permute-start(bf16[576,512]{1,0:T(8,128)(2,1)S(1)} %collective-permute-done.6.refs_4_), channel_id=1, source_target_pairs={{0,1},{1,0},{2,3},{3,2},{4,5},{5,4},{6,7},{7,6},{8,9},{9,8},{10,11... | collective-permute-start | bytes 1769480 | tf_op jit(solution)/shard_map/ppermute | solution.py:310
  32.2 2.1 %collective-permute-start.12 = (bf16[576,512]{1,0:T(8,128)(2,1)S(1)}, bf16[576,512]{1,0:T(8,128)(2,1)S(1)}, u32[]{:S(2)}, u32[]{:S(2)}) collective-permute-start(bf16[576,512]{1,0:T(8,128)(2,1)S(1)} %collective-permute-done.7.refs_8_.refs_4_), channel_id=1, source_target_pairs={{0,1},{1,0},{2,3},{3,2},{4,5},{5,4},{6,7},{7,6},{8,9},{9,8},{10,11... | collective-permute-start | bytes 1769480 | tf_op jit(solution)/shard_map/ppermute | solution.py:310
  34.2 3.0 %copy-start.2 = (bf16[528,128]{1,0:T(8,128)(2,1)S(1)}, bf16[528,128]{1,0:T(8,128)(2,1)}, u32[]{:S(2)}) copy-start(bf16[528,128]{1,0:T(8,128)(2,1)} %get-tuple-element.52.refs_2_) | copy-start | bytes 405508
  35.0 4.4 %copy-start.1 = (bf16[1296,128]{1,0:T(8,128)(2,1)S(1)}, bf16[1296,128]{1,0:T(8,128)(2,1)}, u32[]{:S(2)}) copy-start(bf16[1296,128]{1,0:T(8,128)(2,1)} %get-tuple-element.38.own_ref.wire_ref) | copy-start | bytes 995332
  35.0 4.4 %copy-start.3 = (bf16[64,128]{1,0:T(8,128)(2,1)S(1)}, bf16[64,128]{1,0:T(8,128)(2,1)}, u32[]{:S(2)}) copy-start(bf16[64,128]{1,0:T(8,128)(2,1)} %get-tuple-element.59.bias_ref) | copy-start | bytes 49156
  35.0 16.7 %collective-permute-start.13 = (bf16[272,512]{1,0:T(8,128)(2,1)S(1)}, bf16[272,512]{1,0:T(8,128)(2,1)S(1)}, u32[]{:S(2)}, u32[]{:S(2)}) collective-permute-start(bf16[272,512]{1,0:T(8,128)(2,1)S(1)} %far_late_1.1), channel_id=1, source_target_pairs={{0,8},{1,9},{2,10},{3,11},{4,12},{5,13},{6,14},{7,15},{8,0},{9,1},... | collective-permute-start | bytes 835592 | tf_op jit(solution)/shard_map/ppermute | solution.py:310
  37.8 6.4 %collective-permute-start.9 = (f32[4,2048]{1,0:T(4,128)S(1)}, f32[4,2048]{1,0:T(4,128)S(1)}, u32[]{:S(2)}, u32[]{:S(2)}) collective-permute-start(f32[4,2048]{1,0:T(4,128)S(1)} %get-tuple-element.57), channel_id=1, source_target_pairs={{0,4},{1,5},{2,6},{3,7},{4,0},{5,1},{6,2},{7,3},{8,12},{9,13},{10,... | collective-permute-start | bytes 98312 | tf_op jit(solution)/shard_map/ppermute | solution.py:310
  44.2 8.6 %collective-permute-start.14 = (f32[2,4096]{1,0:T(2,128)S(1)}, f32[2,4096]{1,0:T(2,128)S(1)}, u32[]{:S(2)}, u32[]{:S(2)}) collective-permute-start(f32[2,4096]{1,0:T(2,128)S(1)} %get-tuple-element.71), channel_id=1, source_target_pairs={{0,8},{1,9},{2,10},{3,11},{4,12},{5,13},{6,14},{7,15},{8,0},{9,1},... | collective-permute-start | bytes 98312 | tf_op jit(solution)/shard_map/ppermute | solution.py:310

commit v3 on v2

--- a/solution.py
+++ b/solution.py
@@ -57,8 +57,8 @@
 
 
 def pack_kernel(
-    half_size, q_in, iq_in, w_in, keys_in, scale_in, sel_in, want_in, lat_in,
-    wire_ref, own_ref, k_ref, lat_ref, w_ref, scale_ref, sel_ref, want_ref, bias, sems,
+    half_size, q_in, iq_in, w_in, keys_in, scale_in, sel_in, want_in,
+    wire_ref, own_ref, k_ref, i_ref, w_ref, scale_ref, sel_ref, want_ref, bias, sems,
 ):
     moves = [
         (sel_in, sel_ref),
@@ -68,7 +68,7 @@
         (q_in, wire_ref.at[0:Q_IDX]),
         (iq_in, wire_ref.at[Q_IDX : Q_IDX + I_W]),
         (keys_in, k_ref.at[0:TOK]),
-        (lat_in, lat_ref),
+        (iq_in, i_ref.at[0:I_W]),
     ]
     copies = [
         pltpu.make_async_copy(src, dst, sems.at[k]) for k, (src, dst) in enumerate(moves)
@@ -76,10 +76,12 @@
     for copy in copies:
         copy.start()
     wire_ref[Q_IDX + I_W : Q_BIAS, :] = jnp.zeros((16, IDX), BF)
+    i_ref[I_W:I_ROWS, :] = jnp.zeros((16, IDX), BF)
     k_ref[TOK:K_ROWS, :] = jnp.zeros((16, IDX), BF)
     for copy in copies[:4]:
         copy.wait()
     wire_ref[Q_IDX + I_W : Q_IDX + I_W + 2, 0:IH] = w_ref[...]
+    i_ref[I_W : I_W + 2, 0:IH] = w_ref[...]
     k_ref[TOK : TOK + CHUNKS, :] = scale_ref[...]
     me = lax.axis_index("ctx")
     half = me // half_size
@@ -117,7 +119,24 @@
         copy.wait()
 
 
-def unpack_kernel(half_size, own_ref, wire_ref, bias_ref, q_ref, out_ref, *more):
+def stage_kernel(kv_in, i_in, kv_ref, i_ref, sems):
+    copies = [
+        pltpu.make_async_copy(kv_in, kv_ref, sems.at[0]),
+        pltpu.make_async_copy(i_in, i_ref, sems.at[1]),
+    ]
+    for copy in copies:
+        copy.start()
+    for copy in copies:
+        copy.wait()
+
+
+def unpack_kernel(half_size, *refs):
+    if len(refs) == 6:
+        wire_ref, bias_ref, own_ref, q_ref, out_ref, pair_ref = refs
+        pair_ref[0:I_ROWS, :] = own_ref[...]
+        pair_ref[I_ROWS : 2 * I_ROWS, :] = wire_ref[Q_IDX:Q_BIAS, :]
+    else:
+        wire_ref, bias_ref, q_ref, out_ref = refs
     for t in range(2):
         rows = nt(eye(HEADS), wire_ref[t * WIDTH : (t + 1) * WIDTH, :])
         q_ref[t * HEADS : (t + 1) * HEADS, :] = rows.astype(BF)
@@ -127,20 +146,9 @@
         out_ref[:, c * 128 : (c + 1) * 128] = bias_ref[
             base + c * rows : base + (c + 1) * rows, :
         ].astype(F32)
-    if more:
-        (pair_ref,) = more
-        pair_ref[0:I_ROWS, :] = own_ref[Q_IDX:Q_BIAS, :]
-        pair_ref[I_ROWS : 2 * I_ROWS, :] = wire_ref[Q_IDX:Q_BIAS, :]
-
-
-def split3(x):
-    hi = x.astype(BF)
-    rest = x - hi.astype(F32)
-    mid = rest.astype(BF)
-    return hi, mid, (rest - mid.astype(F32)).astype(BF)
-
-
-def attend_kernel(half_size, masks, first, mode, *refs):
+
+
+def attend_kernel(half_size, masks, first, mode, queries, *refs):
     count = len(masks)
     refs = list(refs)
     q_ref, bias_ref = refs[:2]
@@ -154,17 +162,19 @@
 
     me = lax.axis_index("ctx")
     core = me % 2
-    q = q_ref[...]
-    m_prev = None if first else m_in[:, 0:1]
+    span = slice(queries[0] * HEADS, (queries[-1] + 1) * HEADS)
+    size = len(queries) * HEADS
+    q = q_ref[span, :]
+    m_prev = None if first else m_in[span, 0:1]
     m_new = m_prev
     for p in range(count):
         kv = pieces[p]
         src = lax.bitwise_xor(me, jnp.where(core == 0, masks[p][0], masks[p][1]))
         src = src % half_size
         s = nn(q, kv[0:WIDTH, :]) * TO_LOG2
-        for t in range(2):
-            part = s[t * HEADS : (t + 1) * HEADS, :] + bias_ref[pl.ds(t * half_size + src, 1), :]
-            logits[t * HEADS : (t + 1) * HEADS, p * TOK : (p + 1) * TOK] = part
+        for k, t in enumerate(queries):
+            part = s[k * HEADS : (k + 1) * HEADS, :] + bias_ref[pl.ds(t * half_size + src, 1), :]
+            logits[k * HEADS : (k + 1) * HEADS, p * TOK : (p + 1) * TOK] = part
     top = jnp.max(logits[...], axis=1, keepdims=True)
     m_new = top if first else jnp.maximum(m_prev, top)
 
@@ -178,8 +188,8 @@
         acc = out if acc is None else acc + out
     if not first:
         alpha = jnp.exp2(m_prev - m_new)
-        total = total + l_in[:, 0:1] * alpha
-        acc = acc + acc_in[...] * alpha
+        total = total + l_in[span, 0:1] * alpha
+        acc = acc + acc_in[span, :] * alpha
     if mode == "state":
         acc_out, m_out, l_out = outs
         acc_out[...] = acc
@@ -193,26 +203,31 @@
         o_out[...] = norm
         lse_out[...] = jnp.broadcast_to(lse, lse_out.shape)
         return
-    (wire_out,) = outs
-    wire_out[0:ROWS, :] = norm.astype(BF)
-    diag = iota((ROWS, ROWS), 0) == iota((ROWS, ROWS), 1)
-    row = jnp.sum(jnp.where(diag, lse, 0.0), axis=0, keepdims=True)
-    hi, mid, lo = [x.astype(F32) for x in split3(row)]
-    which = iota((16, ROWS), 0)
-    left = jnp.where(which == 0, hi, jnp.where(which == 1, lo, 0.0))
-    right = jnp.where(which == 0, mid, 0.0)
-    wire_out[ROWS : ROWS + 16, 0:ROWS] = left.astype(BF)
-    wire_out[ROWS : ROWS + 16, ROWS : 2 * ROWS] = right.astype(BF)
+    wire_out, lse_out = outs
+    wire_out[...] = norm.astype(BF)
+    diag = iota((HEADS, HEADS), 0) == iota((HEADS, HEADS), 1)
+    for t in range(2):
+        column = lse[t * HEADS : (t + 1) * HEADS, :]
+        lse_out[t : t + 1, :] = jnp.sum(jnp.where(diag, column, 0.0), axis=0, keepdims=True)
+
+
+def pairs_kernel(*refs):
+    pairs, outs = refs[: len(refs) // 3], refs[len(refs) // 3 :]
+    for j, pair in enumerate(pairs):
+        q_ref, w_ref = outs[2 * j : 2 * j + 2]
+        for k in range(2):
+            at = k * I_ROWS
+            q_ref[k * I_W : (k + 1) * I_W, :] = pair[at : at + I_W, :]
+            w_ref[k] = nt(eye(IH), pair[at + I_W : at + I_ROWS, 0:IH])
 
 
 def score_kernel(count, *refs):
-    pairs, keys, outs = refs[:count], refs[count : count + 4], refs[count + 4 :]
+    pairs, refs = refs[: 2 * count], refs[2 * count :]
+    keys, outs = refs[:4], refs[4:]
     me = lax.axis_index("ctx")
-    unit = eye(IH)
-    for pair, out in zip(pairs, outs):
-        starts = (0, I_ROWS)
-        both = jnp.concatenate([pair[k : k + I_W, :] for k in starts], axis=0)
-        w_cols = [nt(unit, pair[k + I_W : k + I_ROWS, 0:IH]) for k in starts]
+    for j, out in enumerate(outs):
+        both = pairs[2 * j][...]
+        w_cols = [pairs[2 * j + 1][k] for k in range(2)]
         for p in range(4):
             raw = jnp.maximum(nt(both, keys[p][0:TOK, :]), 0.0)
             scales = keys[p][TOK:K_ROWS, :].astype(F32)
@@ -228,8 +243,9 @@
 
 def order_kernel(half_size, masks, *refs):
     me = lax.axis_index("ctx")
-    own_ref, far_ref = refs[-2:]
+    lse_ref, own_ref, far_ref = refs[-3:]
     span = 4 * TOK
+    far_ref[:, half_size * TOK :] = lse_ref[...]
     for ref, mask in zip(refs, masks):
         at = lax.bitwise_and(lax.bitwise_xor(me, mask), half_size - 1) // 4 * span
         at = pl.multiple_of(at, span)
@@ -237,24 +253,25 @@
         far_ref[:, pl.ds(at, span)] = ref[2:4, :]
 
 
-def halves_kernel(half_size, own_ref, far_ref, out_ref):
+def finish_kernel(half_size, o_ref, lse_ref, wire_ref, own_ref, far_ref, scores_ref, out_ref):
     half = lax.axis_index("ctx") // half_size
     width = half_size * TOK
-    out_ref[:, pl.ds(pl.multiple_of(half * width, width), width)] = own_ref[...]
-    out_ref[:, pl.ds(pl.multiple_of((1 - half) * width, width), width)] = far_ref[...]
-
-
-def final_kernel(o_ref, lse_ref, wire_ref, out_ref):
-    stats = wire_ref[ROWS : ROWS + 16, :].astype(F32)
-    row = stats[0:1, 0:ROWS] + stats[0:1, ROWS : 2 * ROWS] + stats[1:2, 0:ROWS]
-    diag = iota((ROWS, ROWS), 0) == iota((ROWS, ROWS), 1)
-    lse_r = jnp.sum(jnp.where(diag, row, 0.0), axis=1, keepdims=True)
+    scores_ref[:, pl.ds(pl.multiple_of(half * width, width), width)] = own_ref[...]
+    scores_ref[:, pl.ds(pl.multiple_of((1 - half) * width, width), width)] = far_ref[:, 0:width]
+    diag = iota((HEADS, HEADS), 0) == iota((HEADS, HEADS), 1)
+    lse_r = jnp.concatenate(
+        [
+            jnp.sum(jnp.where(diag, far_ref[t : t + 1, width:], 0.0), axis=1, keepdims=True)
+            for t in range(2)
+        ],
+        axis=0,
+    )
     lse_o = lse_ref[:, 0:1]
     top = jnp.maximum(lse_r, lse_o)
     e_r = jnp.exp2(lse_r - top)
     e_o = jnp.exp2(lse_o - top)
     inv = 1.0 / (e_r + e_o)
-    out = o_ref[...] * (e_o * inv) + wire_ref[0:ROWS, :].astype(F32) * (e_r * inv)
+    out = o_ref[...] * (e_o * inv) + wire_ref[...].astype(F32) * (e_r * inv)
     for t in range(2):
         out_ref[t] = out[t * HEADS : (t + 1) * HEADS, :].astype(BF)
 
@@ -277,22 +294,23 @@
     return jax.ShapeDtypeStruct(dims, dtype)
 
 
-def attend(half_size, q, bias, group, state, mode, name):
+def attend(half_size, q, bias, group, state, mode, name, queries=(0, 1)):
     masks = tuple(mask for _, mask in group)
     args = [q, bias] + [piece for piece, _ in group]
+    size = len(queries) * HEADS
     state_shape = (shape((ROWS, KVR), F32), shape((ROWS, 128), F32), shape((ROWS, 128), F32))
     if state is not None:
         args += list(state)
     if mode == "state":
         outs = state_shape
     elif mode == "wire":
-        outs = shape((ROWS + 16, LANES), BF)
+        outs = (shape((ROWS, KVR), BF), shape((2, HEADS), F32))
     else:
         outs = state_shape[:2]
-    scratch = [pltpu.VMEM((ROWS, TOK * len(group)), F32)]
-    flops = 2 * ROWS * TOK * len(group) * (2 * KVR + ROPE)
+    scratch = [pltpu.VMEM((size, TOK * len(group)), F32)]
+    flops = 2 * size * TOK * len(group) * (2 * KVR + ROPE)
     return call(
-        functools.partial(attend_kernel, half_size, masks, state is None, mode),
+        functools.partial(attend_kernel, half_size, masks, state is None, mode, queries),
         outs,
         name,
         flops,
@@ -322,13 +340,13 @@
     r1 = permute(kv, first)
 
     rows = 2 * half_size
-    q_wire, bias_own, k_wire, kv_here = call(
+    q_wire, bias_own, k_wire, i_own = call(
         functools.partial(pack_kernel, half_size),
         (
             shape((Q_BIAS + CHUNKS * rows, 128), BF),
             shape((CHUNKS * rows, 128), BF),
             shape((K_ROWS, IDX), BF),
-            shape((WIDTH, TOK), BF),
+            shape((I_ROWS, IDX), BF),
         ),
         "pack",
         2 * 2 * n * 4 * 2048 * 64,
@@ -339,8 +357,7 @@
         key_scales.reshape(CHUNKS, 128),
         selected,
         wanted[0].T,
-        kv,
-        specs=[HBM] * 8,
+        specs=[HBM] * 7,
         limit=None,
         scratch=[
             pltpu.VMEM((2, IH), BF),
@@ -351,11 +368,12 @@
             pltpu.SemaphoreType.DMA((8,)),
         ],
     )
+    kv, q_wire = lax.optimization_barrier((kv, q_wire))
     q_far = permute(q_wire, lambda i: i ^ top)
     r2 = permute(kv, second)
     q_far, r2 = lax.optimization_barrier((q_far, r2))
     r3 = permute(r1, second)
-    held = [(kv_here, (0, 0)), (r1, (2, 4)), (r2, (4, 2)), (r3, (6, 6))]
+    held = [(kv, (0, 0)), (r1, (2, 4)), (r2, (4, 2)), (r3, (6, 6))]
     for bit in range(3, bits - 1):
         step = 1 << bit
         held = held + [
@@ -363,28 +381,29 @@
         ]
 
     k_next = permute(k_wire, lambda i: i ^ 2)
+    kv_here, i_own = call(
+        stage_kernel,
+        (shape((WIDTH, TOK), BF), shape((I_ROWS, IDX), BF)),
+        "stage",
+        0,
+        kv,
+        i_own,
+        specs=[HBM] * 2,
+        scratch=[pltpu.SemaphoreType.DMA((2,))],
+    )
+    kv_core = swap(kv_here)
+    k_next, kv_core = lax.optimization_barrier((k_next, kv_core))
     keys = [k_wire, swap(k_wire), k_next, swap(k_next)]
 
-    def unpack(wire, bias, name, flops, more=()):
-        return call(
-            functools.partial(unpack_kernel, half_size),
-            (shape((ROWS, WIDTH), BF), shape((rows, TOK), F32), *more),
-            name,
-            flops,
-            q_wire,
-            wire,
-            bias,
-        )
+    def unpack(name, flops, *args):
+        outs = [shape((ROWS, WIDTH), BF), shape((rows, TOK), F32)]
+        if len(args) == 3:
+            outs.append(shape((2 * I_ROWS, IDX), BF))
+        return call(functools.partial(unpack_kernel, half_size), tuple(outs), name, flops, *args)
 
     q_far, *keys = lax.optimization_barrier((q_far, *keys))
-    q_there, bias_there, i_pair = unpack(
-        q_far, q_far, "unpack_far", 3 * 1.15e9, [shape((2 * I_ROWS, IDX), BF)]
-    )
-    i_pairs = [i_pair]
-    for bit in range(2, bits - 1):
-        step = 1 << bit
-        i_pairs = i_pairs + [permute(x, lambda i: i ^ step) for x in i_pairs]
-    q_here, bias_here = unpack(q_wire, bias_own, "unpack_own", 0)
+    q_there, bias_there, i_pair = unpack("unpack_far", 3 * 1.15e9, q_far, q_far, i_own)
+    q_here, bias_here = unpack("unpack_own", 0, q_wire, bias_own)
 
     def pair(item):
         piece, (a, b) = item
@@ -396,16 +415,30 @@
             state = attend(half_size, q, bias, group, state, mode, f"{name}_{k}")
         return state
 
-    near = [pair(item) for item in held[:3]]
+    near = [[(kv_here, (0, 0)), (kv_core, (1, 1))]] + [pair(item) for item in held[1:3]]
     (own0, own1), (r1a, r1b), (r2a, r2b) = near
     far = attend(half_size, q_there, bias_there, [own0, own1, r1a, r2a], None, "state", "far_early")
-    far, r3, *i_pairs = lax.optimization_barrier((far, r3, *i_pairs))
+    i_pairs = [i_pair]
+    for bit in range(2, bits - 1):
+        step = 1 << bit
+        i_pairs = i_pairs + [permute(x, lambda i: i ^ step) for x in i_pairs]
+    far, r3 = lax.optimization_barrier((far, r3))
     held[3] = (r3, held[3][1])
     late = [pair(item) for item in held[3:]]
     rest = sum(late[1:], [])
     groups = [[r1b, r2b, late[0][0]], [late[0][1]]]
     groups += [rest[at : at + 6] for at in range(0, len(rest), 6)]
-    wire = run(q_there, bias_there, groups, "wire", "far_late", far)
+    far = run(q_there, bias_there, groups[:-1], "state", "far_late", far)
+    prepared = call(
+        pairs_kernel,
+        (shape((2 * I_W, IDX), BF), shape((2, IH, 16), F32)) * len(i_pairs),
+        "index_pairs",
+        6 * 1.15e9,
+        *i_pairs,
+    )
+    *far, prepared = lax.optimization_barrier((*far, prepared))
+    wire = attend(half_size, q_there, bias_there, groups[-1], far, "wire", "far_last")
+    wire, lse_far = wire
     o_far = permute(wire, lambda i: i ^ top)
 
     parts = call(
@@ -413,7 +446,7 @@
         tuple(shape((4, 4 * TOK), F32) for _ in i_pairs),
         "index_scores",
         2 * len(i_pairs) * 4 * IH * 4 * TOK * IDX,
-        *i_pairs,
+        *prepared,
         *keys,
     )
     parts = [[(part, 0)] for part in parts]
@@ -424,36 +457,30 @@
             parts[j] + [(permute(x, lambda i: i ^ step), mask ^ step) for x, mask in parts[j + count]]
             for j in range(count)
         ]
-    ranges = parts[0]
+    late = [sum(near + late[:1], [])] + groups[2:]
+    o_own, lse_own = run(q_here, bias_here, late, "own", "own_late")
+    ranges, o_own = lax.optimization_barrier((parts[0], o_own))
     scores_own, scores_far = call(
-        functools.partial(order_kernel, half_size, tuple(mask for _, mask in ranges)),
-        (shape((2, half_size * TOK), F32), shape((2, half_size * TOK), F32)),
+        functools.partial(order_kernel, half_size, tuple(mask for _, mask in parts[0])),
+        (shape((2, half_size * TOK), F32), shape((2, half_size * TOK + HEADS), F32)),
         "order_scores",
         0,
         *[x for x, _ in ranges],
+        lse_far,
     )
     scores_far = permute(scores_far, lambda i: i ^ top)
-    late = [sum(near + late[:1], [])] + groups[2:]
-    o_own, lse_own = run(q_here, bias_here, late, "own", "own_late")
-    attended = call(
-        final_kernel,
-        shape((2, HEADS, KVR), BF),
-        "combine",
-        10 * 1.15e9,
+
+    return call(
+        functools.partial(finish_kernel, half_size),
+        (shape((2, n * TOK), F32), shape((2, HEADS, KVR), BF)),
+        "finish",
+        ROWS * KVR * 4,
         o_own,
         lse_own,
         o_far,
-    )
-    attended, scores_far = lax.optimization_barrier((attended, scores_far))
-    scores = call(
-        functools.partial(halves_kernel, half_size),
-        shape((2, n * TOK), F32),
-        "join_scores",
-        0,
         scores_own,
         scores_far,
     )
-    return scores, attended
 
 
 def solution(mesh):

time: 53.6 us -> 52.3 us (0.976)
  starting transfers between devices: 24.5 us -> 21.9 us
  waiting for transfers between devices: 14.2 us -> 15.4 us
  local copies, waits for them, and re-layouts: 0.99 us -> 1.8 us
  Pallas kernels: 12.9 us -> 12.2 us
    ppermute x15, starting transfers between devices: 24.5 us -> 21.9 us  [permute(): return lax.ppermute(x, 'ctx', [(i, move(i)) for i in range(n)])]
    ppermute x15, waiting for transfers between devices: 14.2 us -> 15.4 us  [permute(): return lax.ppermute(x, 'ctx', [(i, move(i)) for i in range(n)])]
    unnamed x10, local copies, waits for them, and re-layouts: 0.99 us -> 1.8 us
    pallas_call x11 -> x12, Pallas kernels: 12.9 us -> 12.2 us  [call(): pl.pallas_call(kernel, out_shape=out_shape, in_specs=specs or [VMEM] * le...]
  transfers between devices with their start and end apart: 15 -> 15, of which waited for: 8 -> 8; matrix products, arithmetic and copies ran while one was open for 0% -> 0% of each run, Pallas kernels for 22% -> 20%
where the time goes in v3:
time: 52.3 us; the launch traced here: 52.1 us
  starting transfers between devices  21.9 us (42%)
  waiting for transfers between devices  15.4 us (29%)
  Pallas kernels  12.2 us (23%)
  local copies, waits for them, and re-layouts  1.8 us (3%)
  between operations  0.76 us (1%)
    ppermute x15, starting transfers between devices, permute(): return lax.ppermute(x, 'ctx', [(i, move(i)) for i in range(n)])  21.9 us
    ppermute x15, waiting for transfers between devices, permute(): return lax.ppermute(x, 'ctx', [(i, move(i)) for i in range(n)])  15.4 us
    pallas_call x12, Pallas kernels, call(): pl.pallas_call(kernel, out_shape=out_shape, in_specs=specs or [VMEM] * le...  12.2 us
    unnamed x10, local copies, waits for them, and re-layouts  1.8 us
  transfers between devices with their start and end apart: 15, of which 8 were waited for; matrix products, arithmetic and copies ran while one was open for 0% of the time, Pallas kernels for 20%

profile of v3, /device:TPU:0, one launch (start us, length us, event | category | flops | bytes accessed | tf_op | source)
XLA Modules:
  0.0 52.1 jit_solution(2519000154553250974)
XLA Ops:
  0.6 3.0 %collective-permute-start.6 = (bf16[576,512]{1,0:T(8,128)(2,1)}, bf16[576,512]{1,0:T(8,128)(2,1)S(1)}, u32[]{:S(2)}, u32[]{:S(2)}) collective-permute-start(bf16[576,512]{1,0:T(8,128)(2,1)} %bitcast.9), channel_id=1, source_target_pairs={{0,2},{1,5},{2,0},{3,7},{4,6},{5,1},{6,4},{7,3},{8,10},{9,13},{10,... | collective-permute-start | bytes 1769480 | tf_op jit(solution)/shard_map/ppermute | solution.py:328
  3.7 2.3 %pack.1 = (bf16[1296,128]{1,0:T(8,128)(2,1)}, bf16[64,128]{1,0:T(8,128)(2,1)}, bf16[528,128]{1,0:T(8,128)(2,1)}, bf16[80,128]{1,0:T(8,128)(2,1)}) custom-call(bf16[1152,128]{1,0:T(8,128)(2,1)} %bitcast.12, bf16[64,128]{1,0:T(8,128)(2,1)} %bitcast.13, bf16[2,32]{1,0:T(2,128)(2,1)} %w_in.1, bf16[512,128]{1,0:T(8,128)(2,1)} %keys_in.1, ...), custom_call_target="tpu_custom_call" | custom-call | flops 33554432 | bytes 460160 | tf_op jit(solution)/shard_map/pack/pallas_call | solution.py:281
  5.9 0.0 copy-start
  6.0 1.1 %copy-done = bf16[512,576]{0,1:T(8,128)(2,1)S(1)} copy-done((bf16[512,576]{0,1:T(8,128)(2,1)S(1)}, bf16[512,576]{0,1:T(8,128)(2,1)}, u32[]{:S(2)}) %copy-start) | copy-done | bytes 589848
  7.0 0.0 copy-start.3
  7.0 0.7 %copy-done.3 = bf16[80,128]{1,0:T(8,128)(2,1)S(1)} copy-done((bf16[80,128]{1,0:T(8,128)(2,1)S(1)}, bf16[80,128]{1,0:T(8,128)(2,1)}, u32[]{:S(2)}) %copy-start.3) | copy-done | bytes 20504
  7.7 0.0 copy-start.1
  7.7 0.0 copy-start.2
  7.7 0.2 stage.1
  7.9 0.1 collective-permute-start.4
  8.0 1.6 %collective-permute-start.1 = (bf16[576,512]{1,0:T(8,128)(2,1)S(1)}, bf16[576,512]{1,0:T(8,128)(2,1)S(1)}, u32[]{:S(2)}, u32[]{:S(2)}) collective-permute-start(bf16[576,512]{1,0:T(8,128)(2,1)S(1)} %bitcast.11), channel_id=1, source_target_pairs={{0,4},{1,3},{2,6},{3,1},{4,0},{5,7},{6,2},{7,5},{8,12},{9,11},{10,... | collective-permute-start | bytes 1769480 | tf_op jit(solution)/shard_map/ppermute | solution.py:328
  9.6 0.0 copy-done.1
  9.6 2.6 %collective-permute-start = (bf16[1296,128]{1,0:T(8,128)(2,1)S(1)}, bf16[1296,128]{1,0:T(8,128)(2,1)S(1)}, u32[]{:S(2)}, u32[]{:S(2)}) collective-permute-start(bf16[1296,128]{1,0:T(8,128)(2,1)S(1)} %copy-done.1), channel_id=1, source_target_pairs={{0,8},{1,9},{2,10},{3,11},{4,12},{5,13},{6,14},{7,15},{8,0},{9,1},... | collective-permute-start | bytes 995336 | tf_op jit(solution)/shard_map/ppermute | solution.py:328
  12.2 0.0 copy-done.2
  12.2 0.5 collective-permute-start.3
  12.7 0.6 %collective-permute-done.6.refs_4_ = bf16[576,512]{1,0:T(8,128)(2,1)S(1)} collective-permute-done((bf16[576,512]{1,0:T(8,128)(2,1)}, bf16[576,512]{1,0:T(8,128)(2,1)S(1)}, u32[]{:S(2)}, u32[]{:S(2)}) %collective-permute-start.6) | collective-permute-done | bytes 589856 | tf_op jit(solution)/shard_map/ppermute | solution.py:328
  13.3 1.8 %collective-permute-start.9 = (bf16[576,512]{1,0:T(8,128)(2,1)S(1)}, bf16[576,512]{1,0:T(8,128)(2,1)S(1)}, u32[]{:S(2)}, u32[]{:S(2)}) collective-permute-start(bf16[576,512]{1,0:T(8,128)(2,1)S(1)} %collective-permute-done.6.refs_4_), channel_id=1, source_target_pairs={{0,4},{1,3},{2,6},{3,1},{4,0},{5,7},{6,2},{7,5},{8,12},{9,11},{10,... | collective-permute-start | bytes 1769480 | tf_op jit(solution)/shard_map/ppermute | solution.py:328
  15.1 3.7 %collective-permute-done.3.refs_6_ = bf16[528,128]{1,0:T(8,128)(2,1)S(1)} collective-permute-done((bf16[528,128]{1,0:T(8,128)(2,1)S(1)}, bf16[528,128]{1,0:T(8,128)(2,1)S(1)}, u32[]{:S(2)}, u32[]{:S(2)}) %collective-permute-start.3) | collective-permute-done | bytes 135200 | tf_op jit(solution)/shard_map/ppermute | solution.py:328
  18.8 2.3 %collective-permute-start.2 = (bf16[528,128]{1,0:T(8,128)(2,1)S(1)}, bf16[528,128]{1,0:T(8,128)(2,1)S(1)}, u32[]{:S(2)}, u32[]{:S(2)}) collective-permute-start(bf16[528,128]{1,0:T(8,128)(2,1)S(1)} %copy-done.2), channel_id=1, source_target_pairs={{0,1},{1,0},{2,3},{3,2},{4,5},{5,4},{6,7},{7,6},{8,9},{9,8},{10,11... | collective-permute-start | bytes 405512 | tf_op jit(solution)/shard_map/ppermute | solution.py:328
  21.1 0.0 collective-permute-done.4.refs_3_
  21.1 0.0 collective-permute-start.5
  21.1 3.1 %collective-permute-done.refs_0_.refs_1_ = bf16[1296,128]{1,0:T(8,128)(2,1)S(1)} collective-permute-done((bf16[1296,128]{1,0:T(8,128)(2,1)S(1)}, bf16[1296,128]{1,0:T(8,128)(2,1)S(1)}, u32[]{:S(2)}, u32[]{:S(2)}) %collective-permute-start) | collective-permute-done | bytes 331808 | tf_op jit(solution)/shard_map/ppermute | solution.py:328
  24.2 0.9 %collective-permute-done.1.refs_5_.refs_6_ = bf16[576,512]{1,0:T(8,128)(2,1)S(1)} collective-permute-done((bf16[576,512]{1,0:T(8,128)(2,1)S(1)}, bf16[576,512]{1,0:T(8,128)(2,1)S(1)}, u32[]{:S(2)}, u32[]{:S(2)}) %collective-permute-start.1) | collective-permute-done | bytes 589856 | tf_op jit(solution)/shard_map/ppermute | solution.py:328
  25.0 0.0 collective-permute-start.8
  25.1 0.5 collective-permute-start.7
  25.6 0.0 collective-permute-done.2.refs_5_
  25.6 0.0 collective-permute-done.5.refs_7_
  25.6 0.3 unpack_far.1
  25.8 2.3 %collective-permute-start.10 = (bf16[160,128]{1,0:T(8,128)(2,1)S(1)}, bf16[160,128]{1,0:T(8,128)(2,1)S(1)}, u32[]{:S(2)}, u32[]{:S(2)}) collective-permute-start(bf16[160,128]{1,0:T(8,128)(2,1)S(1)} %get-tuple-element.80.refs_0_), channel_id=1, source_target_pairs={{0,4},{1,5},{2,6},{3,7},{4,0},{5,1},{6,2},{7,3},{8,12},{9,13},{10,... | collective-permute-start | bytes 122888 | tf_op jit(solution)/shard_map/ppermute | solution.py:328
  28.1 1.8 %far_early.1 = (f32[256,512]{1,0:T(8,128)S(1)}, f32[256,128]{1,0:T(8,128)S(1)}, f32[256,128]{1,0:T(8,128)S(1)}) custom-call(bf16[256,576]{1,0:T(8,128)(2,1)S(1)} %get-tuple-element.66.refs_0_, f32[16,512]{1,0:T(8,128)S(1)} %get-tuple-element.67.refs_1_, bf16[576,512]{1,0:T(8,128)(2,1)S(1)} %get-tuple-element.62.refs_2_, ...), custom_call_target="tpu_custom_call" | custom-call | flops 1140850688 | bytes 2686976 | tf_op jit(solution)/shard_map/far_early/pallas_call | solution.py:281
  30.0 1.8 %collective-permute-done.9.refs_4_.refs_8_ = bf16[576,512]{1,0:T(8,128)(2,1)S(1)} collective-permute-done((bf16[576,512]{1,0:T(8,128)(2,1)S(1)}, bf16[576,512]{1,0:T(8,128)(2,1)S(1)}, u32[]{:S(2)}, u32[]{:S(2)}) %collective-permute-start.9) | collective-permute-done | bytes 589856 | tf_op jit(solution)/shard_map/ppermute | solution.py:328
  31.8 0.0 collective-permute-start.12
  31.8 0.4 collective-permute-done.10.refs_1_
  32.2 0.1 index_pairs.1
  32.4 0.0 collective-permute-done.7.refs_2_.refs_5_
  32.4 0.0 collective-permute-done.8.refs_3_.refs_7_
  32.4 1.6 %far_late_0.1 = (f32[256,512]{1,0:T(8,128)S(1)}, f32[256,128]{1,0:T(8,128)S(1)}, f32[256,128]{1,0:T(8,128)S(1)}) custom-call(bf16[256,576]{1,0:T(8,128)(2,1)S(1)} %get-tuple-element.66.refs_0_, f32[16,512]{1,0:T(8,128)S(1)} %get-tuple-element.67.refs_1_, bf16[576,512]{1,0:T(8,128)(2,1)S(1)} %collective-permute-done.7.refs_2_.refs_5_, ...), custom_call_target="tpu_custom_call" | custom-call | flops 855638016 | bytes 2883584 | tf_op jit(solution)/shard_map/far_late_0/pallas_call | solution.py:281
  34.0 0.0 copy-start.4
  34.0 0.0 collective-permute-done.12.refs_9_.refs_2_
  34.0 0.8 %far_last.1 = (bf16[256,512]{1,0:T(8,128)(2,1)S(1)}, f32[2,128]{1,0:T(2,128)S(1)}) custom-call(bf16[256,576]{1,0:T(8,128)(2,1)S(1)} %get-tuple-element.66.refs_0_, f32[16,512]{1,0:T(8,128)S(1)} %get-tuple-element.67.refs_1_, bf16[576,512]{1,0:T(8,128)(2,1)S(1)} %collective-permute-done.12.refs_9_.refs_2_, f32[256,512]{1,0:T(8,128)S(1)} %get-tuple-element.101.refs_3_, ...), custom_call_target="tpu_custom_call" | custom-call | flops 285212672 | bytes 1703936 | tf_op jit(solution)/shard_map/far_last/pallas_call | solution.py:281
  34.7 2.2 %collective-permute-start.13 = (bf16[256,512]{1,0:T(8,128)(2,1)S(1)}, bf16[256,512]{1,0:T(8,128)(2,1)S(1)}, u32[]{:S(2)}, u32[]{:S(2)}) collective-permute-start(bf16[256,512]{1,0:T(8,128)(2,1)S(1)} %get-tuple-element.104), channel_id=1, source_target_pairs={{0,8},{1,9},{2,10},{3,11},{4,12},{5,13},{6,14},{7,15},{8,0},{9,1},... | collective-permute-start | bytes 786440 | tf_op jit(solution)/shard_map/ppermute | solution.py:328
  37.0 0.0 copy-done.4
  37.0 0.3 unpack_own.1
  37.2 0.5 %index_scores.1 = (f32[4,2048]{1,0:T(4,128)S(1)}, f32[4,2048]{1,0:T(4,128)S(1)}) custom-call(bf16[128,128]{1,0:T(8,128)(2,1)S(1)} %get-tuple-element.85.refs_0_, f32[2,32,16]{2,1,0:T(8,128)S(1)} %get-tuple-element.86.refs_1_, bf16[128,128]{1,0:T(8,128)(2,1)S(1)} %get-tuple-element.87.refs_2_, f32[2,32,16]{2,1,0:T(8,128)S(1)} %get-tuple-element.88.refs_3_, ...), custom_call_target="tpu_custom_call" | custom-call | flops 134217728 | bytes 614400 | tf_op jit(solution)/shard_map/index_scores/pallas_call | solution.py:281
  37.8 2.1 %collective-permute-start.11 = (f32[4,2048]{1,0:T(4,128)S(1)}, f32[4,2048]{1,0:T(4,128)S(1)}, u32[]{:S(2)}, u32[]{:S(2)}) collective-permute-start(f32[4,2048]{1,0:T(4,128)S(1)} %get-tuple-element.94), channel_id=1, source_target_pairs={{0,4},{1,5},{2,6},{3,7},{4,0},{5,1},{6,2},{7,3},{8,12},{9,13},{10,... | collective-permute-start | bytes 98312 | tf_op jit(solution)/shard_map/ppermute | solution.py:328
  39.8 3.4 %own_late_0.1 = (f32[256,512]{1,0:T(8,128)S(1)}, f32[256,128]{1,0:T(8,128)S(1)}) custom-call(bf16[256,576]{1,0:T(8,128)(2,1)S(1)} %get-tuple-element.96.refs_0_, f32[16,512]{1,0:T(8,128)S(1)} %get-tuple-element.97.refs_1_, bf16[576,512]{1,0:T(8,128)(2,1)S(1)} %get-tuple-element.62.refs_2_, bf16[576,512]{1,0:T(8,128)(2,1)S(1)} %collective-permute-done.4.refs_3_, ...), custom_call_target="tpu_custom_call" | custom-call | flops 2281701376 | bytes 5046272 | tf_op jit(solution)/shard_map/own_late_0/pallas_call | solution.py:281
  43.3 0.2 collective-permute-done.11.refs_1_
  43.5 2.9 %collective-permute-start.14 = (f32[2,4224]{1,0:T(2,128)S(1)}, f32[2,4224]{1,0:T(2,128)S(1)}, u32[]{:S(2)}, u32[]{:S(2)}) collective-permute-start(f32[2,4224]{1,0:T(2,128)S(1)} %get-tuple-element.109), channel_id=1, source_target_pairs={{0,8},{1,9},{2,10},{3,11},{4,12},{5,13},{6,14},{7,15},{8,0},{9,1},... | collective-permute-start | bytes 101384 | tf_op jit(solution)/shard_map/ppermute | solution.py:328
  46.5 4.6 %collective-permute-done.14.far_ref = f32[2,4224]{1,0:T(2,128)S(1)} collective-permute-done((f32[2,4224]{1,0:T(2,128)S(1)}, f32[2,4224]{1,0:T(2,128)S(1)}, u32[]{:S(2)}, u32[]{:S(2)}) %collective-permute-start.14) | collective-permute-done | bytes 33824 | tf_op jit(solution)/shard_map/ppermute | solution.py:328
  51.1 0.0 collective-permute-done.13.wire_ref
  51.1 1.0 %finish.1 = (f32[2,8192]{1,0:T(2,128)}, bf16[2,128,512]{2,1,0:T(8,128)(2,1)}) custom-call(f32[256,512]{1,0:T(8,128)S(1)} %get-tuple-element.99.o_ref, f32[256,128]{1,0:T(8,128)S(1)} %get-tuple-element.100.lse_ref, bf16[256,512]{1,0:T(8,128)(2,1)S(1)} %collective-permute-done.13.wire_ref, f32[2,4096]{1,0:T(2,128)S(1)} %get-tuple-element.108.own_ref, ...), custom_call_target="tpu_custom_call" | custom-call | flops 524288 | bytes 984064 | tf_op jit(solution)/shard_map/finish/pallas_call | solution.py:281
  (1 shorter events, 0.0 us)
Async XLA Ops:
  0.6 12.7 %collective-permute-start.6 = (bf16[576,512]{1,0:T(8,128)(2,1)}, bf16[576,512]{1,0:T(8,128)(2,1)S(1)}, u32[]{:S(2)}, u32[]{:S(2)}) collective-permute-start(bf16[576,512]{1,0:T(8,128)(2,1)} %bitcast.9), channel_id=1, source_target_pairs={{0,2},{1,5},{2,0},{3,7},{4,6},{5,1},{6,4},{7,3},{8,10},{9,13},{10,... | collective-permute-start | bytes 1769480 | tf_op jit(solution)/shard_map/ppermute | solution.py:328
  5.9 1.1 %copy-start = (bf16[512,576]{0,1:T(8,128)(2,1)S(1)}, bf16[512,576]{0,1:T(8,128)(2,1)}, u32[]{:S(2)}) copy-start(bf16[512,576]{0,1:T(8,128)(2,1)} %param.13) | copy-start | bytes 1769476
  7.0 0.7 %copy-start.3 = (bf16[80,128]{1,0:T(8,128)(2,1)S(1)}, bf16[80,128]{1,0:T(8,128)(2,1)}, u32[]{:S(2)}) copy-start(bf16[80,128]{1,0:T(8,128)(2,1)} %get-tuple-element.61.i_in) | copy-start | bytes 61444
  7.7 1.9 %copy-start.1 = (bf16[1296,128]{1,0:T(8,128)(2,1)S(1)}, bf16[1296,128]{1,0:T(8,128)(2,1)}, u32[]{:S(2)}) copy-start(bf16[1296,128]{1,0:T(8,128)(2,1)} %get-tuple-element.57.refs_0_) | copy-start | bytes 995332
  7.7 4.5 %copy-start.2 = (bf16[528,128]{1,0:T(8,128)(2,1)S(1)}, bf16[528,128]{1,0:T(8,128)(2,1)}, u32[]{:S(2)}) copy-start(bf16[528,128]{1,0:T(8,128)(2,1)} %get-tuple-element.89.refs_4_) | copy-start | bytes 405508
  7.9 13.2 %collective-permute-start.4 = (bf16[576,512]{1,0:T(8,128)(2,1)S(1)}, bf16[576,512]{1,0:T(8,128)(2,1)S(1)}, u32[]{:S(2)}, u32[]{:S(2)}) collective-permute-start(bf16[576,512]{1,0:T(8,128)(2,1)S(1)} %get-tuple-element.62.refs_2_), channel_id=1, source_target_pairs={{0,1},{1,0},{2,3},{3,2},{4,5},{5,4},{6,7},{7,6},{8,9},{9,8},{10,11... | collective-permute-start | bytes 1769480 | tf_op jit(solution)/shard_map/ppermute | solution.py:328
  8.0 17.1 %collective-permute-start.1 = (bf16[576,512]{1,0:T(8,128)(2,1)S(1)}, bf16[576,512]{1,0:T(8,128)(2,1)S(1)}, u32[]{:S(2)}, u32[]{:S(2)}) collective-permute-start(bf16[576,512]{1,0:T(8,128)(2,1)S(1)} %bitcast.11), channel_id=1, source_target_pairs={{0,4},{1,3},{2,6},{3,1},{4,0},{5,7},{6,2},{7,5},{8,12},{9,11},{10,... | collective-permute-start | bytes 1769480 | tf_op jit(solution)/shard_map/ppermute | solution.py:328
  9.6 14.6 %collective-permute-start = (bf16[1296,128]{1,0:T(8,128)(2,1)S(1)}, bf16[1296,128]{1,0:T(8,128)(2,1)S(1)}, u32[]{:S(2)}, u32[]{:S(2)}) collective-permute-start(bf16[1296,128]{1,0:T(8,128)(2,1)S(1)} %copy-done.1), channel_id=1, source_target_pairs={{0,8},{1,9},{2,10},{3,11},{4,12},{5,13},{6,14},{7,15},{8,0},{9,1},... | collective-permute-start | bytes 995336 | tf_op jit(solution)/shard_map/ppermute | solution.py:328
  12.2 6.5 %collective-permute-start.3 = (bf16[528,128]{1,0:T(8,128)(2,1)S(1)}, bf16[528,128]{1,0:T(8,128)(2,1)S(1)}, u32[]{:S(2)}, u32[]{:S(2)}) collective-permute-start(bf16[528,128]{1,0:T(8,128)(2,1)S(1)} %copy-done.2), channel_id=1, source_target_pairs={{0,2},{1,3},{2,0},{3,1},{4,6},{5,7},{6,4},{7,5},{8,10},{9,11},{10,... | collective-permute-start | bytes 405512 | tf_op jit(solution)/shard_map/ppermute | solution.py:328
  13.3 18.5 %collective-permute-start.9 = (bf16[576,512]{1,0:T(8,128)(2,1)S(1)}, bf16[576,512]{1,0:T(8,128)(2,1)S(1)}, u32[]{:S(2)}, u32[]{:S(2)}) collective-permute-start(bf16[576,512]{1,0:T(8,128)(2,1)S(1)} %collective-permute-done.6.refs_4_), channel_id=1, source_target_pairs={{0,4},{1,3},{2,6},{3,1},{4,0},{5,7},{6,2},{7,5},{8,12},{9,11},{10,... | collective-permute-start | bytes 1769480 | tf_op jit(solution)/shard_map/ppermute | solution.py:328
  18.8 6.8 %collective-permute-start.2 = (bf16[528,128]{1,0:T(8,128)(2,1)S(1)}, bf16[528,128]{1,0:T(8,128)(2,1)S(1)}, u32[]{:S(2)}, u32[]{:S(2)}) collective-permute-start(bf16[528,128]{1,0:T(8,128)(2,1)S(1)} %copy-done.2), channel_id=1, source_target_pairs={{0,1},{1,0},{2,3},{3,2},{4,5},{5,4},{6,7},{7,6},{8,9},{9,8},{10,11... | collective-permute-start | bytes 405512 | tf_op jit(solution)/shard_map/ppermute | solution.py:328
  21.1 4.5 %collective-permute-start.5 = (bf16[528,128]{1,0:T(8,128)(2,1)S(1)}, bf16[528,128]{1,0:T(8,128)(2,1)S(1)}, u32[]{:S(2)}, u32[]{:S(2)}) collective-permute-start(bf16[528,128]{1,0:T(8,128)(2,1)S(1)} %collective-permute-done.3.refs_6_), channel_id=1, source_target_pairs={{0,1},{1,0},{2,3},{3,2},{4,5},{5,4},{6,7},{7,6},{8,9},{9,8},{10,11... | collective-permute-start | bytes 405512 | tf_op jit(solution)/shard_map/ppermute | solution.py:328
  25.0 7.3 %collective-permute-start.8 = (bf16[576,512]{1,0:T(8,128)(2,1)S(1)}, bf16[576,512]{1,0:T(8,128)(2,1)S(1)}, u32[]{:S(2)}, u32[]{:S(2)}) collective-permute-start(bf16[576,512]{1,0:T(8,128)(2,1)S(1)} %collective-permute-done.1.refs_5_.refs_6_), channel_id=1, source_target_pairs={{0,1},{1,0},{2,3},{3,2},{4,5},{5,4},{6,7},{7,6},{8,9},{9,8},{10,11... | collective-permute-start | bytes 1769480 | tf_op jit(solution)/shard_map/ppermute | solution.py:328
  25.1 7.3 %collective-permute-start.7 = (bf16[576,512]{1,0:T(8,128)(2,1)S(1)}, bf16[576,512]{1,0:T(8,128)(2,1)S(1)}, u32[]{:S(2)}, u32[]{:S(2)}) collective-permute-start(bf16[576,512]{1,0:T(8,128)(2,1)S(1)} %collective-permute-done.6.refs_4_), channel_id=1, source_target_pairs={{0,1},{1,0},{2,3},{3,2},{4,5},{5,4},{6,7},{7,6},{8,9},{9,8},{10,11... | collective-permute-start | bytes 1769480 | tf_op jit(solution)/shard_map/ppermute | solution.py:328
  25.8 6.4 %collective-permute-start.10 = (bf16[160,128]{1,0:T(8,128)(2,1)S(1)}, bf16[160,128]{1,0:T(8,128)(2,1)S(1)}, u32[]{:S(2)}, u32[]{:S(2)}) collective-permute-start(bf16[160,128]{1,0:T(8,128)(2,1)S(1)} %get-tuple-element.80.refs_0_), channel_id=1, source_target_pairs={{0,4},{1,5},{2,6},{3,7},{4,0},{5,1},{6,2},{7,3},{8,12},{9,13},{10,... | collective-permute-start | bytes 122888 | tf_op jit(solution)/shard_map/ppermute | solution.py:328
  31.8 2.2 %collective-permute-start.12 = (bf16[576,512]{1,0:T(8,128)(2,1)S(1)}, bf16[576,512]{1,0:T(8,128)(2,1)S(1)}, u32[]{:S(2)}, u32[]{:S(2)}) collective-permute-start(bf16[576,512]{1,0:T(8,128)(2,1)S(1)} %collective-permute-done.9.refs_4_.refs_8_), channel_id=1, source_target_pairs={{0,1},{1,0},{2,3},{3,2},{4,5},{5,4},{6,7},{7,6},{8,9},{9,8},{10,11... | collective-permute-start | bytes 1769480 | tf_op jit(solution)/shard_map/ppermute | solution.py:328
  34.0 3.0 %copy-start.4 = (bf16[64,128]{1,0:T(8,128)(2,1)S(1)}, bf16[64,128]{1,0:T(8,128)(2,1)}, u32[]{:S(2)}) copy-start(bf16[64,128]{1,0:T(8,128)(2,1)} %get-tuple-element.95.refs_1_) | copy-start | bytes 49156
  34.7 16.3 %collective-permute-start.13 = (bf16[256,512]{1,0:T(8,128)(2,1)S(1)}, bf16[256,512]{1,0:T(8,128)(2,1)S(1)}, u32[]{:S(2)}, u32[]{:S(2)}) collective-permute-start(bf16[256,512]{1,0:T(8,128)(2,1)S(1)} %get-tuple-element.104), channel_id=1, source_target_pairs={{0,8},{1,9},{2,10},{3,11},{4,12},{5,13},{6,14},{7,15},{8,0},{9,1},... | collective-permute-start | bytes 786440 | tf_op jit(solution)/shard_map/ppermute | solution.py:328
  37.8 5.8 %collective-permute-start.11 = (f32[4,2048]{1,0:T(4,128)S(1)}, f32[4,2048]{1,0:T(4,128)S(1)}, u32[]{:S(2)}, u32[]{:S(2)}) collective-permute-start(f32[4,2048]{1,0:T(4,128)S(1)} %get-tuple-element.94), channel_id=1, source_target_pairs={{0,4},{1,5},{2,6},{3,7},{4,0},{5,1},{6,2},{7,3},{8,12},{9,13},{10,... | collective-permute-start | bytes 98312 | tf_op jit(solution)/shard_map/ppermute | solution.py:328
  43.5 7.5 %collective-permute-start.14 = (f32[2,4224]{1,0:T(2,128)S(1)}, f32[2,4224]{1,0:T(2,128)S(1)}, u32[]{:S(2)}, u32[]{:S(2)}) collective-permute-start(f32[2,4224]{1,0:T(2,128)S(1)} %get-tuple-element.109), channel_id=1, source_target_pairs={{0,8},{1,9},{2,10},{3,11},{4,12},{5,13},{6,14},{7,15},{8,0},{9,1},... | collective-permute-start | bytes 101384 | tf_op jit(solution)/shard_map/ppermute | solution.py:328

commit v4 on v3

--- a/solution.py
+++ b/solution.py
@@ -196,7 +196,7 @@
         m_out[...] = jnp.broadcast_to(m_new, m_out.shape)
         l_out[...] = jnp.broadcast_to(total, l_out.shape)
         return
-    norm = acc / total
+    norm = acc * (1.0 / total)
     lse = m_new + jnp.log(total) * LOG2E
     if mode == "own":
         o_out, lse_out = outs
@@ -245,23 +245,31 @@
     me = lax.axis_index("ctx")
     lse_ref, own_ref, far_ref = refs[-3:]
     span = 4 * TOK
-    far_ref[:, half_size * TOK :] = lse_ref[...]
+    width = half_size * TOK
+    hi = lse_ref[...].astype(BF)
+    rest = lse_ref[...] - hi.astype(F32)
+    mid = rest.astype(BF)
+    parts = (hi, mid, (rest - mid.astype(F32)).astype(BF))
+    for k, part in enumerate(parts):
+        far_ref[:, width + k * HEADS : width + (k + 1) * HEADS] = part
     for ref, mask in zip(refs, masks):
         at = lax.bitwise_and(lax.bitwise_xor(me, mask), half_size - 1) // 4 * span
         at = pl.multiple_of(at, span)
         own_ref[:, pl.ds(at, span)] = ref[0:2, :]
-        far_ref[:, pl.ds(at, span)] = ref[2:4, :]
+        far_ref[:, pl.ds(at, span)] = ref[2:4, :].astype(BF)
 
 
 def finish_kernel(half_size, o_ref, lse_ref, wire_ref, own_ref, far_ref, scores_ref, out_ref):
     half = lax.axis_index("ctx") // half_size
     width = half_size * TOK
     scores_ref[:, pl.ds(pl.multiple_of(half * width, width), width)] = own_ref[...]
-    scores_ref[:, pl.ds(pl.multiple_of((1 - half) * width, width), width)] = far_ref[:, 0:width]
+    scores_ref[:, pl.ds(pl.multiple_of((1 - half) * width, width), width)] = far_ref[:, 0:width].astype(F32)
+    stats = far_ref[:, width:].astype(F32)
+    stats = stats[:, 0:HEADS] + stats[:, HEADS : 2 * HEADS] + stats[:, 2 * HEADS : 3 * HEADS]
     diag = iota((HEADS, HEADS), 0) == iota((HEADS, HEADS), 1)
     lse_r = jnp.concatenate(
         [
-            jnp.sum(jnp.where(diag, far_ref[t : t + 1, width:], 0.0), axis=1, keepdims=True)
+            jnp.sum(jnp.where(diag, stats[t : t + 1, :], 0.0), axis=1, keepdims=True)
             for t in range(2)
         ],
         axis=0,
@@ -392,7 +400,6 @@
         scratch=[pltpu.SemaphoreType.DMA((2,))],
     )
     kv_core = swap(kv_here)
-    k_next, kv_core = lax.optimization_barrier((k_next, kv_core))
     keys = [k_wire, swap(k_wire), k_next, swap(k_next)]
 
     def unpack(name, flops, *args):
@@ -417,7 +424,7 @@
 
     near = [[(kv_here, (0, 0)), (kv_core, (1, 1))]] + [pair(item) for item in held[1:3]]
     (own0, own1), (r1a, r1b), (r2a, r2b) = near
-    far = attend(half_size, q_there, bias_there, [own0, own1, r1a, r2a], None, "state", "far_early")
+    far = attend(half_size, q_there, bias_there, [own0, r1a, r2a], None, "state", "far_early")
     i_pairs = [i_pair]
     for bit in range(2, bits - 1):
         step = 1 << bit
@@ -426,7 +433,7 @@
     held[3] = (r3, held[3][1])
     late = [pair(item) for item in held[3:]]
     rest = sum(late[1:], [])
-    groups = [[r1b, r2b, late[0][0]], [late[0][1]]]
+    groups = [[own1, r1b, r2b, late[0][0]], [late[0][1]]]
     groups += [rest[at : at + 6] for at in range(0, len(rest), 6)]
     far = run(q_there, bias_there, groups[:-1], "state", "far_late", far)
     prepared = call(
@@ -462,7 +469,7 @@
     ranges, o_own = lax.optimization_barrier((parts[0], o_own))
     scores_own, scores_far = call(
         functools.partial(order_kernel, half_size, tuple(mask for _, mask in parts[0])),
-        (shape((2, half_size * TOK), F32), shape((2, half_size * TOK + HEADS), F32)),
+        (shape((2, half_size * TOK), F32), shape((2, half_size * TOK + 3 * HEADS), BF)),
         "order_scores",
         0,
         *[x for x, _ in ranges],

time: 52.3 us -> 51.2 us (0.979)
  waiting for transfers between devices: 15.4 us -> 10.3 us
  starting transfers between devices: 21.9 us -> 25.3 us
  local copies, waits for them, and re-layouts: 1.8 us -> 2.44 us
    ppermute x15, waiting for transfers between devices: 15.4 us -> 10.3 us  [permute(): return lax.ppermute(x, 'ctx', [(i, move(i)) for i in range(n)])]
    ppermute x15, starting transfers between devices: 21.9 us -> 25.3 us  [permute(): return lax.ppermute(x, 'ctx', [(i, move(i)) for i in range(n)])]
    unnamed x10, local copies, waits for them, and re-layouts: 1.8 us -> 2.44 us
  transfers between devices with their start and end apart: 15 -> 15, of which waited for: 8 -> 4; matrix products, arithmetic and copies ran while one was open for 0% -> 0% of each run, Pallas kernels for 20% -> 20%
where the time goes in v4:
time: 51.2 us; the launch traced here: 51 us
  starting transfers between devices  25.3 us (49%)
  Pallas kernels  12.1 us (24%)
  waiting for transfers between devices  10.3 us (20%)
  local copies, waits for them, and re-layouts  2.44 us (5%)
  between operations  0.77 us (2%)
    ppermute x15, starting transfers between devices, permute(): return lax.ppermute(x, 'ctx', [(i, move(i)) for i in range(n)])  25.3 us
    pallas_call x12, Pallas kernels, call(): pl.pallas_call(kernel, out_shape=out_shape, in_specs=specs or [VMEM] * le...  12.1 us
    ppermute x15, waiting for transfers between devices, permute(): return lax.ppermute(x, 'ctx', [(i, move(i)) for i in range(n)])  10.3 us
    unnamed x10, local copies, waits for them, and re-layouts  2.44 us
  transfers between devices with their start and end apart: 15, of which 4 were waited for; matrix products, arithmetic and copies ran while one was open for 0% of the time, Pallas kernels for 20%

profile of v4, /device:TPU:0, one launch (start us, length us, event | category | flops | bytes accessed | tf_op | source)
XLA Modules:
  0.0 51.0 jit_solution(10369767934593311166)
XLA Ops:
  0.6 3.0 %collective-permute-start.6 = (bf16[576,512]{1,0:T(8,128)(2,1)}, bf16[576,512]{1,0:T(8,128)(2,1)S(1)}, u32[]{:S(2)}, u32[]{:S(2)}) collective-permute-start(bf16[576,512]{1,0:T(8,128)(2,1)} %bitcast.9), channel_id=1, source_target_pairs={{0,2},{1,5},{2,0},{3,7},{4,6},{5,1},{6,4},{7,3},{8,10},{9,13},{10,... | collective-permute-start | bytes 1769480 | tf_op jit(solution)/shard_map/ppermute | solution.py:336
  3.7 2.3 %pack.1 = (bf16[1296,128]{1,0:T(8,128)(2,1)}, bf16[64,128]{1,0:T(8,128)(2,1)}, bf16[528,128]{1,0:T(8,128)(2,1)}, bf16[80,128]{1,0:T(8,128)(2,1)}) custom-call(bf16[1152,128]{1,0:T(8,128)(2,1)} %bitcast.12, bf16[64,128]{1,0:T(8,128)(2,1)} %bitcast.13, bf16[2,32]{1,0:T(2,128)(2,1)} %w_in.1, bf16[512,128]{1,0:T(8,128)(2,1)} %keys_in.1, ...), custom_call_target="tpu_custom_call" | custom-call | flops 33554432 | bytes 460160 | tf_op jit(solution)/shard_map/pack/pallas_call | solution.py:289
  5.9 1.6 %collective-permute-start.1 = (bf16[576,512]{1,0:T(8,128)(2,1)}, bf16[576,512]{1,0:T(8,128)(2,1)S(1)}, u32[]{:S(2)}, u32[]{:S(2)}) collective-permute-start(bf16[576,512]{1,0:T(8,128)(2,1)} %bitcast.10), channel_id=1, source_target_pairs={{0,4},{1,3},{2,6},{3,1},{4,0},{5,7},{6,2},{7,5},{8,12},{9,11},{10,... | collective-permute-start | bytes 1769480 | tf_op jit(solution)/shard_map/ppermute | solution.py:336
  7.6 2.6 %collective-permute-start = (bf16[1296,128]{1,0:T(8,128)(2,1)}, bf16[1296,128]{1,0:T(8,128)(2,1)S(1)}, u32[]{:S(2)}, u32[]{:S(2)}) collective-permute-start(bf16[1296,128]{1,0:T(8,128)(2,1)} %get-tuple-element.55.refs_0_), channel_id=1, source_target_pairs={{0,8},{1,9},{2,10},{3,11},{4,12},{5,13},{6,14},{7,15},{8,0},{9,1},... | collective-permute-start | bytes 995336 | tf_op jit(solution)/shard_map/ppermute | solution.py:336
  10.2 0.5 collective-permute-start.3
  10.7 4.4 %collective-permute-done.6.refs_3_.refs_4_ = bf16[576,512]{1,0:T(8,128)(2,1)S(1)} collective-permute-done((bf16[576,512]{1,0:T(8,128)(2,1)}, bf16[576,512]{1,0:T(8,128)(2,1)S(1)}, u32[]{:S(2)}, u32[]{:S(2)}) %collective-permute-start.6) | collective-permute-done | bytes 589856 | tf_op jit(solution)/shard_map/ppermute | solution.py:336
  15.1 3.7 %collective-permute-start.9 = (bf16[576,512]{1,0:T(8,128)(2,1)S(1)}, bf16[576,512]{1,0:T(8,128)(2,1)S(1)}, u32[]{:S(2)}, u32[]{:S(2)}) collective-permute-start(bf16[576,512]{1,0:T(8,128)(2,1)S(1)} %collective-permute-done.6.refs_3_.refs_4_), channel_id=1, source_target_pairs={{0,4},{1,3},{2,6},{3,1},{4,0},{5,7},{6,2},{7,5},{8,12},{9,11},{10,... | collective-permute-start | bytes 1769480 | tf_op jit(solution)/shard_map/ppermute | solution.py:336
  18.9 3.4 %collective-permute-start.2 = (bf16[528,128]{1,0:T(8,128)(2,1)}, bf16[528,128]{1,0:T(8,128)(2,1)S(1)}, u32[]{:S(2)}, u32[]{:S(2)}) collective-permute-start(bf16[528,128]{1,0:T(8,128)(2,1)} %get-tuple-element.85.refs_4_), channel_id=1, source_target_pairs={{0,1},{1,0},{2,3},{3,2},{4,5},{5,4},{6,7},{7,6},{8,9},{9,8},{10,11... | collective-permute-start | bytes 405512 | tf_op jit(solution)/shard_map/ppermute | solution.py:336
  22.3 0.0 collective-permute-done.3.refs_6_
  22.3 0.0 collective-permute-start.4
  22.3 0.0 copy-start
  22.3 1.1 %copy-done = bf16[512,576]{0,1:T(8,128)(2,1)S(1)} copy-done((bf16[512,576]{0,1:T(8,128)(2,1)S(1)}, bf16[512,576]{0,1:T(8,128)(2,1)}, u32[]{:S(2)}) %copy-start) | copy-done | bytes 589848
  23.4 0.0 copy-start.3
  23.4 0.7 %copy-done.3 = bf16[80,128]{1,0:T(8,128)(2,1)S(1)} copy-done((bf16[80,128]{1,0:T(8,128)(2,1)S(1)}, bf16[80,128]{1,0:T(8,128)(2,1)}, u32[]{:S(2)}) %copy-start.3) | copy-done | bytes 20504
  24.1 0.2 stage.1
  24.2 0.0 collective-permute-done.refs_0_.refs_1_
  24.3 0.6 %collective-permute-start.5 = (bf16[576,512]{1,0:T(8,128)(2,1)S(1)}, bf16[576,512]{1,0:T(8,128)(2,1)S(1)}, u32[]{:S(2)}, u32[]{:S(2)}) collective-permute-start(bf16[576,512]{1,0:T(8,128)(2,1)S(1)} %get-tuple-element.64.refs_2_), channel_id=1, source_target_pairs={{0,1},{1,0},{2,3},{3,2},{4,5},{5,4},{6,7},{7,6},{8,9},{9,8},{10,11... | collective-permute-start | bytes 1769480 | tf_op jit(solution)/shard_map/ppermute | solution.py:336
  24.8 0.0 collective-permute-done.1.refs_4_.refs_6_
  24.8 0.0 collective-permute-done.2.refs_5_
  24.8 0.0 collective-permute-done.4.refs_7_
  24.8 0.1 collective-permute-start.8
  24.9 0.3 unpack_far.1
  25.2 2.8 %collective-permute-start.10 = (bf16[160,128]{1,0:T(8,128)(2,1)S(1)}, bf16[160,128]{1,0:T(8,128)(2,1)S(1)}, u32[]{:S(2)}, u32[]{:S(2)}) collective-permute-start(bf16[160,128]{1,0:T(8,128)(2,1)S(1)} %get-tuple-element.76.refs_0_), channel_id=1, source_target_pairs={{0,4},{1,5},{2,6},{3,7},{4,0},{5,1},{6,2},{7,3},{8,12},{9,13},{10,... | collective-permute-start | bytes 122888 | tf_op jit(solution)/shard_map/ppermute | solution.py:336
  28.0 0.0 collective-permute-start.7
  28.0 1.4 %far_early.1 = (f32[256,512]{1,0:T(8,128)S(1)}, f32[256,128]{1,0:T(8,128)S(1)}, f32[256,128]{1,0:T(8,128)S(1)}) custom-call(bf16[256,576]{1,0:T(8,128)(2,1)S(1)} %get-tuple-element.62.refs_0_, f32[16,512]{1,0:T(8,128)S(1)} %get-tuple-element.63.refs_1_, bf16[576,512]{1,0:T(8,128)(2,1)S(1)} %get-tuple-element.64.refs_2_, ...), custom_call_target="tpu_custom_call" | custom-call | flops 855638016 | bytes 2097152 | tf_op jit(solution)/shard_map/far_early/pallas_call | solution.py:289
  29.5 1.7 %collective-permute-done.9.refs_5_.refs_8_ = bf16[576,512]{1,0:T(8,128)(2,1)S(1)} collective-permute-done((bf16[576,512]{1,0:T(8,128)(2,1)S(1)}, bf16[576,512]{1,0:T(8,128)(2,1)S(1)}, u32[]{:S(2)}, u32[]{:S(2)}) %collective-permute-start.9) | collective-permute-done | bytes 589856 | tf_op jit(solution)/shard_map/ppermute | solution.py:336
  31.1 0.0 collective-permute-start.12
  31.1 0.4 collective-permute-done.10.refs_1_
  31.6 0.1 index_pairs.1
  31.7 0.0 collective-permute-done.5.refs_2_.refs_3_
  31.7 0.0 collective-permute-done.7.refs_3_.refs_5_
  31.7 0.0 collective-permute-done.8.refs_4_.refs_7_
  31.7 1.9 %far_late_0.1 = (f32[256,512]{1,0:T(8,128)S(1)}, f32[256,128]{1,0:T(8,128)S(1)}, f32[256,128]{1,0:T(8,128)S(1)}) custom-call(bf16[256,576]{1,0:T(8,128)(2,1)S(1)} %get-tuple-element.62.refs_0_, f32[16,512]{1,0:T(8,128)S(1)} %get-tuple-element.63.refs_1_, bf16[576,512]{1,0:T(8,128)(2,1)S(1)} %collective-permute-done.5.refs_2_.refs_3_, ...), custom_call_target="tpu_custom_call" | custom-call | flops 1140850688 | bytes 3473408 | tf_op jit(solution)/shard_map/far_late_0/pallas_call | solution.py:289
  33.6 0.0 copy-start.1
  33.6 0.0 copy-start.4
  33.6 0.0 collective-permute-done.12.refs_9_.refs_2_
  33.7 0.8 %far_last.1 = (bf16[256,512]{1,0:T(8,128)(2,1)S(1)}, f32[2,128]{1,0:T(2,128)S(1)}) custom-call(bf16[256,576]{1,0:T(8,128)(2,1)S(1)} %get-tuple-element.62.refs_0_, f32[16,512]{1,0:T(8,128)S(1)} %get-tuple-element.63.refs_1_, bf16[576,512]{1,0:T(8,128)(2,1)S(1)} %collective-permute-done.12.refs_9_.refs_2_, f32[256,512]{1,0:T(8,128)S(1)} %get-tuple-element.97.refs_3_, ...), custom_call_target="tpu_custom_call" | custom-call | flops 285212672 | bytes 1703936 | tf_op jit(solution)/shard_map/far_last/pallas_call | solution.py:289
  34.4 2.8 %collective-permute-start.13 = (bf16[256,512]{1,0:T(8,128)(2,1)S(1)}, bf16[256,512]{1,0:T(8,128)(2,1)S(1)}, u32[]{:S(2)}, u32[]{:S(2)}) collective-permute-start(bf16[256,512]{1,0:T(8,128)(2,1)S(1)} %get-tuple-element.100), channel_id=1, source_target_pairs={{0,8},{1,9},{2,10},{3,11},{4,12},{5,13},{6,14},{7,15},{8,0},{9,1},... | collective-permute-start | bytes 786440 | tf_op jit(solution)/shard_map/ppermute | solution.py:336
  37.2 0.0 copy-done.1
  37.2 0.0 copy-done.4
  37.2 0.0 copy-start.2
  37.2 0.3 unpack_own.1
  37.5 0.6 %copy-done.2 = bf16[528,128]{1,0:T(8,128)(2,1)S(1)} copy-done((bf16[528,128]{1,0:T(8,128)(2,1)S(1)}, bf16[528,128]{1,0:T(8,128)(2,1)}, u32[]{:S(2)}) %copy-start.2) | copy-done | bytes 135192
  38.1 0.5 %index_scores.1 = (f32[4,2048]{1,0:T(4,128)S(1)}, f32[4,2048]{1,0:T(4,128)S(1)}) custom-call(bf16[128,128]{1,0:T(8,128)(2,1)S(1)} %get-tuple-element.81.refs_0_, f32[2,32,16]{2,1,0:T(8,128)S(1)} %get-tuple-element.82.refs_1_, bf16[128,128]{1,0:T(8,128)(2,1)S(1)} %get-tuple-element.83.refs_2_, f32[2,32,16]{2,1,0:T(8,128)S(1)} %get-tuple-element.84.refs_3_, ...), custom_call_target="tpu_custom_call" | custom-call | flops 134217728 | bytes 614400 | tf_op jit(solution)/shard_map/index_scores/pallas_call | solution.py:289
  38.7 1.6 %collective-permute-start.11 = (f32[4,2048]{1,0:T(4,128)S(1)}, f32[4,2048]{1,0:T(4,128)S(1)}, u32[]{:S(2)}, u32[]{:S(2)}) collective-permute-start(f32[4,2048]{1,0:T(4,128)S(1)} %get-tuple-element.90), channel_id=1, source_target_pairs={{0,4},{1,5},{2,6},{3,7},{4,0},{5,1},{6,2},{7,3},{8,12},{9,13},{10,... | collective-permute-start | bytes 98312 | tf_op jit(solution)/shard_map/ppermute | solution.py:336
  40.3 3.4 %own_late_0.1 = (f32[256,512]{1,0:T(8,128)S(1)}, f32[256,128]{1,0:T(8,128)S(1)}) custom-call(bf16[256,576]{1,0:T(8,128)(2,1)S(1)} %get-tuple-element.92.refs_0_, f32[16,512]{1,0:T(8,128)S(1)} %get-tuple-element.93.refs_1_, bf16[576,512]{1,0:T(8,128)(2,1)S(1)} %get-tuple-element.64.refs_2_, bf16[576,512]{1,0:T(8,128)(2,1)S(1)} %collective-permute-done.5.refs_2_.refs_3_, ...), custom_call_target="tpu_custom_call" | custom-call | flops 2281701376 | bytes 5046272 | tf_op jit(solution)/shard_map/own_late_0/pallas_call | solution.py:289
  43.8 0.0 collective-permute-done.11.refs_1_
  43.8 2.4 %collective-permute-start.14 = (bf16[2,4480]{1,0:T(2,128)(2,1)S(1)}, bf16[2,4480]{1,0:T(2,128)(2,1)S(1)}, u32[]{:S(2)}, u32[]{:S(2)}) collective-permute-start(bf16[2,4480]{1,0:T(2,128)(2,1)S(1)} %get-tuple-element.105), channel_id=1, source_target_pairs={{0,8},{1,9},{2,10},{3,11},{4,12},{5,13},{6,14},{7,15},{8,0},{9,1},... | collective-permute-start | bytes 53768 | tf_op jit(solution)/shard_map/ppermute | solution.py:336
  46.2 3.7 %collective-permute-done.14.far_ref = bf16[2,4480]{1,0:T(2,128)(2,1)S(1)} collective-permute-done((bf16[2,4480]{1,0:T(2,128)(2,1)S(1)}, bf16[2,4480]{1,0:T(2,128)(2,1)S(1)}, u32[]{:S(2)}, u32[]{:S(2)}) %collective-permute-start.14) | collective-permute-done | bytes 17952 | tf_op jit(solution)/shard_map/ppermute | solution.py:336
  50.0 0.0 collective-permute-done.13.wire_ref
  50.0 1.0 %finish.1 = (f32[2,8192]{1,0:T(2,128)}, bf16[2,128,512]{2,1,0:T(8,128)(2,1)}) custom-call(f32[256,512]{1,0:T(8,128)S(1)} %get-tuple-element.95.o_ref, f32[256,128]{1,0:T(8,128)S(1)} %get-tuple-element.96.lse_ref, bf16[256,512]{1,0:T(8,128)(2,1)S(1)} %collective-permute-done.13.wire_ref, f32[2,4096]{1,0:T(2,128)S(1)} %get-tuple-element.104.own_ref, ...), custom_call_target="tpu_custom_call" | custom-call | flops 524288 | bytes 968192 | tf_op jit(solution)/shard_map/finish/pallas_call | solution.py:289
  (1 shorter events, 0.0 us)
Async XLA Ops:
  0.6 14.5 %collective-permute-start.6 = (bf16[576,512]{1,0:T(8,128)(2,1)}, bf16[576,512]{1,0:T(8,128)(2,1)S(1)}, u32[]{:S(2)}, u32[]{:S(2)}) collective-permute-start(bf16[576,512]{1,0:T(8,128)(2,1)} %bitcast.9), channel_id=1, source_target_pairs={{0,2},{1,5},{2,0},{3,7},{4,6},{5,1},{6,4},{7,3},{8,10},{9,13},{10,... | collective-permute-start | bytes 1769480 | tf_op jit(solution)/shard_map/ppermute | solution.py:336
  5.9 18.9 %collective-permute-start.1 = (bf16[576,512]{1,0:T(8,128)(2,1)}, bf16[576,512]{1,0:T(8,128)(2,1)S(1)}, u32[]{:S(2)}, u32[]{:S(2)}) collective-permute-start(bf16[576,512]{1,0:T(8,128)(2,1)} %bitcast.10), channel_id=1, source_target_pairs={{0,4},{1,3},{2,6},{3,1},{4,0},{5,7},{6,2},{7,5},{8,12},{9,11},{10,... | collective-permute-start | bytes 1769480 | tf_op jit(solution)/shard_map/ppermute | solution.py:336
  7.6 16.7 %collective-permute-start = (bf16[1296,128]{1,0:T(8,128)(2,1)}, bf16[1296,128]{1,0:T(8,128)(2,1)S(1)}, u32[]{:S(2)}, u32[]{:S(2)}) collective-permute-start(bf16[1296,128]{1,0:T(8,128)(2,1)} %get-tuple-element.55.refs_0_), channel_id=1, source_target_pairs={{0,8},{1,9},{2,10},{3,11},{4,12},{5,13},{6,14},{7,15},{8,0},{9,1},... | collective-permute-start | bytes 995336 | tf_op jit(solution)/shard_map/ppermute | solution.py:336
  10.2 12.1 %collective-permute-start.3 = (bf16[528,128]{1,0:T(8,128)(2,1)}, bf16[528,128]{1,0:T(8,128)(2,1)S(1)}, u32[]{:S(2)}, u32[]{:S(2)}) collective-permute-start(bf16[528,128]{1,0:T(8,128)(2,1)} %get-tuple-element.85.refs_4_), channel_id=1, source_target_pairs={{0,2},{1,3},{2,0},{3,1},{4,6},{5,7},{6,4},{7,5},{8,10},{9,11},{10,... | collective-permute-start | bytes 405512 | tf_op jit(solution)/shard_map/ppermute | solution.py:336
  15.1 16.0 %collective-permute-start.9 = (bf16[576,512]{1,0:T(8,128)(2,1)S(1)}, bf16[576,512]{1,0:T(8,128)(2,1)S(1)}, u32[]{:S(2)}, u32[]{:S(2)}) collective-permute-start(bf16[576,512]{1,0:T(8,128)(2,1)S(1)} %collective-permute-done.6.refs_3_.refs_4_), channel_id=1, source_target_pairs={{0,4},{1,3},{2,6},{3,1},{4,0},{5,7},{6,2},{7,5},{8,12},{9,11},{10,... | collective-permute-start | bytes 1769480 | tf_op jit(solution)/shard_map/ppermute | solution.py:336
  18.9 6.0 %collective-permute-start.2 = (bf16[528,128]{1,0:T(8,128)(2,1)}, bf16[528,128]{1,0:T(8,128)(2,1)S(1)}, u32[]{:S(2)}, u32[]{:S(2)}) collective-permute-start(bf16[528,128]{1,0:T(8,128)(2,1)} %get-tuple-element.85.refs_4_), channel_id=1, source_target_pairs={{0,1},{1,0},{2,3},{3,2},{4,5},{5,4},{6,7},{7,6},{8,9},{9,8},{10,11... | collective-permute-start | bytes 405512 | tf_op jit(solution)/shard_map/ppermute | solution.py:336
  22.3 2.6 %collective-permute-start.4 = (bf16[528,128]{1,0:T(8,128)(2,1)S(1)}, bf16[528,128]{1,0:T(8,128)(2,1)S(1)}, u32[]{:S(2)}, u32[]{:S(2)}) collective-permute-start(bf16[528,128]{1,0:T(8,128)(2,1)S(1)} %collective-permute-done.3.refs_6_), channel_id=1, source_target_pairs={{0,1},{1,0},{2,3},{3,2},{4,5},{5,4},{6,7},{7,6},{8,9},{9,8},{10,11... | collective-permute-start | bytes 405512 | tf_op jit(solution)/shard_map/ppermute | solution.py:336
  22.3 1.1 %copy-start = (bf16[512,576]{0,1:T(8,128)(2,1)S(1)}, bf16[512,576]{0,1:T(8,128)(2,1)}, u32[]{:S(2)}) copy-start(bf16[512,576]{0,1:T(8,128)(2,1)} %param.13) | copy-start | bytes 1769476
  23.4 0.7 %copy-start.3 = (bf16[80,128]{1,0:T(8,128)(2,1)S(1)}, bf16[80,128]{1,0:T(8,128)(2,1)}, u32[]{:S(2)}) copy-start(bf16[80,128]{1,0:T(8,128)(2,1)} %get-tuple-element.60.i_in) | copy-start | bytes 61444
  24.3 7.4 %collective-permute-start.5 = (bf16[576,512]{1,0:T(8,128)(2,1)S(1)}, bf16[576,512]{1,0:T(8,128)(2,1)S(1)}, u32[]{:S(2)}, u32[]{:S(2)}) collective-permute-start(bf16[576,512]{1,0:T(8,128)(2,1)S(1)} %get-tuple-element.64.refs_2_), channel_id=1, source_target_pairs={{0,1},{1,0},{2,3},{3,2},{4,5},{5,4},{6,7},{7,6},{8,9},{9,8},{10,11... | collective-permute-start | bytes 1769480 | tf_op jit(solution)/shard_map/ppermute | solution.py:336
  24.8 6.9 %collective-permute-start.8 = (bf16[576,512]{1,0:T(8,128)(2,1)S(1)}, bf16[576,512]{1,0:T(8,128)(2,1)S(1)}, u32[]{:S(2)}, u32[]{:S(2)}) collective-permute-start(bf16[576,512]{1,0:T(8,128)(2,1)S(1)} %collective-permute-done.1.refs_4_.refs_6_), channel_id=1, source_target_pairs={{0,1},{1,0},{2,3},{3,2},{4,5},{5,4},{6,7},{7,6},{8,9},{9,8},{10,11... | collective-permute-start | bytes 1769480 | tf_op jit(solution)/shard_map/ppermute | solution.py:336
  25.2 6.4 %collective-permute-start.10 = (bf16[160,128]{1,0:T(8,128)(2,1)S(1)}, bf16[160,128]{1,0:T(8,128)(2,1)S(1)}, u32[]{:S(2)}, u32[]{:S(2)}) collective-permute-start(bf16[160,128]{1,0:T(8,128)(2,1)S(1)} %get-tuple-element.76.refs_0_), channel_id=1, source_target_pairs={{0,4},{1,5},{2,6},{3,7},{4,0},{5,1},{6,2},{7,3},{8,12},{9,13},{10,... | collective-permute-start | bytes 122888 | tf_op jit(solution)/shard_map/ppermute | solution.py:336
  28.0 3.7 %collective-permute-start.7 = (bf16[576,512]{1,0:T(8,128)(2,1)S(1)}, bf16[576,512]{1,0:T(8,128)(2,1)S(1)}, u32[]{:S(2)}, u32[]{:S(2)}) collective-permute-start(bf16[576,512]{1,0:T(8,128)(2,1)S(1)} %collective-permute-done.6.refs_3_.refs_4_), channel_id=1, source_target_pairs={{0,1},{1,0},{2,3},{3,2},{4,5},{5,4},{6,7},{7,6},{8,9},{9,8},{10,11... | collective-permute-start | bytes 1769480 | tf_op jit(solution)/shard_map/ppermute | solution.py:336
  31.1 2.5 %collective-permute-start.12 = (bf16[576,512]{1,0:T(8,128)(2,1)S(1)}, bf16[576,512]{1,0:T(8,128)(2,1)S(1)}, u32[]{:S(2)}, u32[]{:S(2)}) collective-permute-start(bf16[576,512]{1,0:T(8,128)(2,1)S(1)} %collective-permute-done.9.refs_5_.refs_8_), channel_id=1, source_target_pairs={{0,1},{1,0},{2,3},{3,2},{4,5},{5,4},{6,7},{7,6},{8,9},{9,8},{10,11... | collective-permute-start | bytes 1769480 | tf_op jit(solution)/shard_map/ppermute | solution.py:336
  33.6 3.6 %copy-start.1 = (bf16[1296,128]{1,0:T(8,128)(2,1)S(1)}, bf16[1296,128]{1,0:T(8,128)(2,1)}, u32[]{:S(2)}) copy-start(bf16[1296,128]{1,0:T(8,128)(2,1)} %get-tuple-element.55.refs_0_) | copy-start | bytes 995332
  33.6 3.6 %copy-start.4 = (bf16[64,128]{1,0:T(8,128)(2,1)S(1)}, bf16[64,128]{1,0:T(8,128)(2,1)}, u32[]{:S(2)}) copy-start(bf16[64,128]{1,0:T(8,128)(2,1)} %get-tuple-element.91.refs_1_) | copy-start | bytes 49156
  34.4 15.6 %collective-permute-start.13 = (bf16[256,512]{1,0:T(8,128)(2,1)S(1)}, bf16[256,512]{1,0:T(8,128)(2,1)S(1)}, u32[]{:S(2)}, u32[]{:S(2)}) collective-permute-start(bf16[256,512]{1,0:T(8,128)(2,1)S(1)} %get-tuple-element.100), channel_id=1, source_target_pairs={{0,8},{1,9},{2,10},{3,11},{4,12},{5,13},{6,14},{7,15},{8,0},{9,1},... | collective-permute-start | bytes 786440 | tf_op jit(solution)/shard_map/ppermute | solution.py:336
  37.2 0.9 %copy-start.2 = (bf16[528,128]{1,0:T(8,128)(2,1)S(1)}, bf16[528,128]{1,0:T(8,128)(2,1)}, u32[]{:S(2)}) copy-start(bf16[528,128]{1,0:T(8,128)(2,1)} %get-tuple-element.85.refs_4_) | copy-start | bytes 405508
  38.7 5.1 %collective-permute-start.11 = (f32[4,2048]{1,0:T(4,128)S(1)}, f32[4,2048]{1,0:T(4,128)S(1)}, u32[]{:S(2)}, u32[]{:S(2)}) collective-permute-start(f32[4,2048]{1,0:T(4,128)S(1)} %get-tuple-element.90), channel_id=1, source_target_pairs={{0,4},{1,5},{2,6},{3,7},{4,0},{5,1},{6,2},{7,3},{8,12},{9,13},{10,... | collective-permute-start | bytes 98312 | tf_op jit(solution)/shard_map/ppermute | solution.py:336
  43.8 6.2 %collective-permute-start.14 = (bf16[2,4480]{1,0:T(2,128)(2,1)S(1)}, bf16[2,4480]{1,0:T(2,128)(2,1)S(1)}, u32[]{:S(2)}, u32[]{:S(2)}) collective-permute-start(bf16[2,4480]{1,0:T(2,128)(2,1)S(1)} %get-tuple-element.105), channel_id=1, source_target_pairs={{0,8},{1,9},{2,10},{3,11},{4,12},{5,13},{6,14},{7,15},{8,0},{9,1},... | collective-permute-start | bytes 53768 | tf_op jit(solution)/shard_map/ppermute | solution.py:336

commit v5 on v4

--- a/solution.py
+++ b/solution.py
@@ -119,10 +119,11 @@
         copy.wait()
 
 
-def stage_kernel(kv_in, i_in, kv_ref, i_ref, sems):
+def stage_kernel(kv_in, i_in, k_in, kv_ref, i_ref, k_ref, sems):
     copies = [
         pltpu.make_async_copy(kv_in, kv_ref, sems.at[0]),
         pltpu.make_async_copy(i_in, i_ref, sems.at[1]),
+        pltpu.make_async_copy(k_in, k_ref, sems.at[2]),
     ]
     for copy in copies:
         copy.start()
@@ -389,18 +390,19 @@
         ]
 
     k_next = permute(k_wire, lambda i: i ^ 2)
-    kv_here, i_own = call(
+    kv_here, i_own, k_here = call(
         stage_kernel,
-        (shape((WIDTH, TOK), BF), shape((I_ROWS, IDX), BF)),
+        (shape((WIDTH, TOK), BF), shape((I_ROWS, IDX), BF), shape((K_ROWS, IDX), BF)),
         "stage",
         0,
         kv,
         i_own,
-        specs=[HBM] * 2,
-        scratch=[pltpu.SemaphoreType.DMA((2,))],
+        k_wire,
+        specs=[HBM] * 3,
+        scratch=[pltpu.SemaphoreType.DMA((3,))],
     )
     kv_core = swap(kv_here)
-    keys = [k_wire, swap(k_wire), k_next, swap(k_next)]
+    keys = [k_here, swap(k_wire), k_next, swap(k_next)]
 
     def unpack(name, flops, *args):
         outs = [shape((ROWS, WIDTH), BF), shape((rows, TOK), F32)]
@@ -424,7 +426,7 @@
 
     near = [[(kv_here, (0, 0)), (kv_core, (1, 1))]] + [pair(item) for item in held[1:3]]
     (own0, own1), (r1a, r1b), (r2a, r2b) = near
-    far = attend(half_size, q_there, bias_there, [own0, r1a, r2a], None, "state", "far_early")
+    far = attend(half_size, q_there, bias_there, [own0, own1, r1a, r2a], None, "state", "far_early")
     i_pairs = [i_pair]
     for bit in range(2, bits - 1):
         step = 1 << bit
@@ -433,7 +435,7 @@
     held[3] = (r3, held[3][1])
     late = [pair(item) for item in held[3:]]
     rest = sum(late[1:], [])
-    groups = [[own1, r1b, r2b, late[0][0]], [late[0][1]]]
+    groups = [[r1b, r2b, late[0][0]], [late[0][1]]]
     groups += [rest[at : at + 6] for at in range(0, len(rest), 6)]
     far = run(q_there, bias_there, groups[:-1], "state", "far_late", far)
     prepared = call(
@@ -464,9 +466,12 @@
             parts[j] + [(permute(x, lambda i: i ^ step), mask ^ step) for x, mask in parts[j + count]]
             for j in range(count)
         ]
-    late = [sum(near + late[:1], [])] + groups[2:]
-    o_own, lse_own = run(q_here, bias_here, late, "own", "own_late")
-    ranges, o_own = lax.optimization_barrier((parts[0], o_own))
+    pieces = sum(near + late[:1], [])
+    own = attend(half_size, q_here, bias_here, pieces[:4], None, "state", "own_first")
+    ranges, own = lax.optimization_barrier((parts[0], own))
+    o_own, lse_own = run(
+        q_here, bias_here, [pieces[4:]] + groups[2:], "own", "own_late", own
+    )
     scores_own, scores_far = call(
         functools.partial(order_kernel, half_size, tuple(mask for _, mask in parts[0])),
         (shape((2, half_size * TOK), F32), shape((2, half_size * TOK + 3 * HEADS), BF)),

time: 51.2 us -> 50.9 us (level)
  waiting for transfers between devices: 10.3 us -> 8.89 us
  Pallas kernels: 12.1 us -> 12.8 us
    ppermute x15, waiting for transfers between devices: 10.3 us -> 8.89 us  [permute(): return lax.ppermute(x, 'ctx', [(i, move(i)) for i in range(n)])]
    pallas_call x12 -> x13, Pallas kernels: 12.1 us -> 12.8 us  [call(): pl.pallas_call(kernel, out_shape=out_shape, in_specs=specs or [VMEM] * le...]
  transfers between devices with their start and end apart: 15 -> 15, of which waited for: 4 -> 8; matrix products, arithmetic and copies ran while one was open for 0% -> 0% of each run, Pallas kernels for 20% -> 22%
where the time goes in v5:
time: 50.9 us; the launch traced here: 50.7 us
  starting transfers between devices  25.5 us (50%)
  Pallas kernels  12.8 us (25%)
  waiting for transfers between devices  8.89 us (17%)
  local copies, waits for them, and re-layouts  2.7 us (5%)
  between operations  0.77 us (2%)
    ppermute x15, starting transfers between devices, permute(): return lax.ppermute(x, 'ctx', [(i, move(i)) for i in range(n)])  25.5 us
    pallas_call x13, Pallas kernels, call(): pl.pallas_call(kernel, out_shape=out_shape, in_specs=specs or [VMEM] * le...  12.8 us
    ppermute x15, waiting for transfers between devices, permute(): return lax.ppermute(x, 'ctx', [(i, move(i)) for i in range(n)])  8.89 us
    unnamed x10, local copies, waits for them, and re-layouts  2.7 us
  transfers between devices with their start and end apart: 15, of which 8 were waited for; matrix products, arithmetic and copies ran while one was open for 0% of the time, Pallas kernels for 22%

profile of v5, /device:TPU:0, one launch (start us, length us, event | category | flops | bytes accessed | tf_op | source)
XLA Modules:
  0.0 50.7 jit_solution(10894451436513059549)
XLA Ops:
  0.6 3.0 %collective-permute-start.7 = (bf16[576,512]{1,0:T(8,128)(2,1)}, bf16[576,512]{1,0:T(8,128)(2,1)S(1)}, u32[]{:S(2)}, u32[]{:S(2)}) collective-permute-start(bf16[576,512]{1,0:T(8,128)(2,1)} %bitcast.9), channel_id=1, source_target_pairs={{0,2},{1,5},{2,0},{3,7},{4,6},{5,1},{6,4},{7,3},{8,10},{9,13},{10,... | collective-permute-start | bytes 1769480 | tf_op jit(solution)/shard_map/ppermute | solution.py:337
  3.7 2.3 %pack.1 = (bf16[1296,128]{1,0:T(8,128)(2,1)}, bf16[64,128]{1,0:T(8,128)(2,1)}, bf16[528,128]{1,0:T(8,128)(2,1)}, bf16[80,128]{1,0:T(8,128)(2,1)}) custom-call(bf16[1152,128]{1,0:T(8,128)(2,1)} %bitcast.12, bf16[64,128]{1,0:T(8,128)(2,1)} %bitcast.13, bf16[2,32]{1,0:T(2,128)(2,1)} %w_in.1, bf16[512,128]{1,0:T(8,128)(2,1)} %keys_in.1, ...), custom_call_target="tpu_custom_call" | custom-call | flops 33554432 | bytes 460160 | tf_op jit(solution)/shard_map/pack/pallas_call | solution.py:290
  5.9 1.6 %collective-permute-start.1 = (bf16[576,512]{1,0:T(8,128)(2,1)}, bf16[576,512]{1,0:T(8,128)(2,1)S(1)}, u32[]{:S(2)}, u32[]{:S(2)}) collective-permute-start(bf16[576,512]{1,0:T(8,128)(2,1)} %bitcast.10), channel_id=1, source_target_pairs={{0,4},{1,3},{2,6},{3,1},{4,0},{5,7},{6,2},{7,5},{8,12},{9,11},{10,... | collective-permute-start | bytes 1769480 | tf_op jit(solution)/shard_map/ppermute | solution.py:337
  7.6 2.6 %collective-permute-start = (bf16[1296,128]{1,0:T(8,128)(2,1)}, bf16[1296,128]{1,0:T(8,128)(2,1)S(1)}, u32[]{:S(2)}, u32[]{:S(2)}) collective-permute-start(bf16[1296,128]{1,0:T(8,128)(2,1)} %get-tuple-element.61.refs_0_), channel_id=1, source_target_pairs={{0,8},{1,9},{2,10},{3,11},{4,12},{5,13},{6,14},{7,15},{8,0},{9,1},... | collective-permute-start | bytes 995336 | tf_op jit(solution)/shard_map/ppermute | solution.py:337
  10.2 0.5 collective-permute-start.4
  10.7 0.0 copy-start
  10.7 1.1 %copy-done = bf16[512,576]{0,1:T(8,128)(2,1)S(1)} copy-done((bf16[512,576]{0,1:T(8,128)(2,1)S(1)}, bf16[512,576]{0,1:T(8,128)(2,1)}, u32[]{:S(2)}) %copy-start) | copy-done | bytes 589848
  11.7 0.0 copy-start.2
  11.7 0.9 %copy-done.2 = bf16[528,128]{1,0:T(8,128)(2,1)S(1)} copy-done((bf16[528,128]{1,0:T(8,128)(2,1)S(1)}, bf16[528,128]{1,0:T(8,128)(2,1)}, u32[]{:S(2)}) %copy-start.2) | copy-done | bytes 135192
  12.7 0.0 copy-start.3
  12.7 0.7 %copy-done.3 = bf16[80,128]{1,0:T(8,128)(2,1)S(1)} copy-done((bf16[80,128]{1,0:T(8,128)(2,1)S(1)}, bf16[80,128]{1,0:T(8,128)(2,1)}, u32[]{:S(2)}) %copy-start.3) | copy-done | bytes 20504
  13.4 0.3 stage.1
  13.7 0.1 collective-permute-start.6
  13.8 1.3 %collective-permute-done.7.refs_4_ = bf16[576,512]{1,0:T(8,128)(2,1)S(1)} collective-permute-done((bf16[576,512]{1,0:T(8,128)(2,1)}, bf16[576,512]{1,0:T(8,128)(2,1)S(1)}, u32[]{:S(2)}, u32[]{:S(2)}) %collective-permute-start.7) | collective-permute-done | bytes 589856 | tf_op jit(solution)/shard_map/ppermute | solution.py:337
  15.1 3.7 %collective-permute-start.8 = (bf16[576,512]{1,0:T(8,128)(2,1)S(1)}, bf16[576,512]{1,0:T(8,128)(2,1)S(1)}, u32[]{:S(2)}, u32[]{:S(2)}) collective-permute-start(bf16[576,512]{1,0:T(8,128)(2,1)S(1)} %collective-permute-done.7.refs_4_), channel_id=1, source_target_pairs={{0,4},{1,3},{2,6},{3,1},{4,0},{5,7},{6,2},{7,5},{8,12},{9,11},{10,... | collective-permute-start | bytes 1769480 | tf_op jit(solution)/shard_map/ppermute | solution.py:337
  18.9 0.0 collective-permute-done.4.refs_6_
  18.9 3.4 %collective-permute-start.3 = (bf16[528,128]{1,0:T(8,128)(2,1)S(1)}, bf16[528,128]{1,0:T(8,128)(2,1)S(1)}, u32[]{:S(2)}, u32[]{:S(2)}) collective-permute-start(bf16[528,128]{1,0:T(8,128)(2,1)S(1)} %copy-done.2), channel_id=1, source_target_pairs={{0,1},{1,0},{2,3},{3,2},{4,5},{5,4},{6,7},{7,6},{8,9},{9,8},{10,11... | collective-permute-start | bytes 405512 | tf_op jit(solution)/shard_map/ppermute | solution.py:337
  22.3 1.5 %collective-permute-done.refs_0_.refs_1_ = bf16[1296,128]{1,0:T(8,128)(2,1)S(1)} collective-permute-done((bf16[1296,128]{1,0:T(8,128)(2,1)}, bf16[1296,128]{1,0:T(8,128)(2,1)S(1)}, u32[]{:S(2)}, u32[]{:S(2)}) %collective-permute-start) | collective-permute-done | bytes 331808 | tf_op jit(solution)/shard_map/ppermute | solution.py:337
  23.7 0.0 collective-permute-start.5
  23.7 0.6 %collective-permute-done.1.refs_5_.refs_2_ = bf16[576,512]{1,0:T(8,128)(2,1)S(1)} collective-permute-done((bf16[576,512]{1,0:T(8,128)(2,1)}, bf16[576,512]{1,0:T(8,128)(2,1)S(1)}, u32[]{:S(2)}, u32[]{:S(2)}) %collective-permute-start.1) | collective-permute-done | bytes 589856 | tf_op jit(solution)/shard_map/ppermute | solution.py:337
  24.4 0.0 collective-permute-start.2
  24.4 0.0 collective-permute-done.3.refs_5_
  24.4 0.7 %collective-permute-done.5.refs_7_ = bf16[528,128]{1,0:T(8,128)(2,1)S(1)} collective-permute-done((bf16[528,128]{1,0:T(8,128)(2,1)S(1)}, bf16[528,128]{1,0:T(8,128)(2,1)S(1)}, u32[]{:S(2)}, u32[]{:S(2)}) %collective-permute-start.5) | collective-permute-done | bytes 135200 | tf_op jit(solution)/shard_map/ppermute | solution.py:337
  25.1 0.3 unpack_far.1
  25.4 3.5 %collective-permute-start.11 = (bf16[160,128]{1,0:T(8,128)(2,1)S(1)}, bf16[160,128]{1,0:T(8,128)(2,1)S(1)}, u32[]{:S(2)}, u32[]{:S(2)}) collective-permute-start(bf16[160,128]{1,0:T(8,128)(2,1)S(1)} %get-tuple-element.86.refs_0_), channel_id=1, source_target_pairs={{0,4},{1,5},{2,6},{3,7},{4,0},{5,1},{6,2},{7,3},{8,12},{9,13},{10,... | collective-permute-start | bytes 122888 | tf_op jit(solution)/shard_map/ppermute | solution.py:337
  28.8 0.0 collective-permute-start.10
  28.8 0.0 collective-permute-done.6.refs_3_
  28.8 1.9 %far_early.1 = (f32[256,512]{1,0:T(8,128)S(1)}, f32[256,128]{1,0:T(8,128)S(1)}, f32[256,128]{1,0:T(8,128)S(1)}) custom-call(bf16[256,576]{1,0:T(8,128)(2,1)S(1)} %get-tuple-element.73.refs_0_, f32[16,512]{1,0:T(8,128)S(1)} %get-tuple-element.74.refs_1_, bf16[576,512]{1,0:T(8,128)(2,1)S(1)} %get-tuple-element.75.refs_2_, ...), custom_call_target="tpu_custom_call" | custom-call | flops 1140850688 | bytes 2686976 | tf_op jit(solution)/shard_map/far_early/pallas_call | solution.py:290
  30.7 0.4 collective-permute-done.8.refs_4_
  31.1 0.1 collective-permute-start.9
  31.3 0.3 collective-permute-done.11.refs_1_
  31.6 0.1 index_pairs.1
  31.7 0.0 collective-permute-done.2.refs_3_
  31.7 0.0 collective-permute-done.10.refs_2_.refs_5_
  31.7 1.6 %far_late_0.1 = (f32[256,512]{1,0:T(8,128)S(1)}, f32[256,128]{1,0:T(8,128)S(1)}, f32[256,128]{1,0:T(8,128)S(1)}) custom-call(bf16[256,576]{1,0:T(8,128)(2,1)S(1)} %get-tuple-element.73.refs_0_, f32[16,512]{1,0:T(8,128)S(1)} %get-tuple-element.74.refs_1_, bf16[576,512]{1,0:T(8,128)(2,1)S(1)} %collective-permute-done.10.refs_2_.refs_5_, ...), custom_call_target="tpu_custom_call" | custom-call | flops 855638016 | bytes 2883584 | tf_op jit(solution)/shard_map/far_late_0/pallas_call | solution.py:290
  33.3 0.0 copy-start.1
  33.3 0.0 copy-start.4
  33.3 0.0 collective-permute-done.9.refs_5_.refs_2_
  33.3 0.8 %far_last.1 = (bf16[256,512]{1,0:T(8,128)(2,1)S(1)}, f32[2,128]{1,0:T(2,128)S(1)}) custom-call(bf16[256,576]{1,0:T(8,128)(2,1)S(1)} %get-tuple-element.73.refs_0_, f32[16,512]{1,0:T(8,128)S(1)} %get-tuple-element.74.refs_1_, bf16[576,512]{1,0:T(8,128)(2,1)S(1)} %collective-permute-done.9.refs_5_.refs_2_, f32[256,512]{1,0:T(8,128)S(1)} %get-tuple-element.109.refs_3_, ...), custom_call_target="tpu_custom_call" | custom-call | flops 285212672 | bytes 1703936 | tf_op jit(solution)/shard_map/far_last/pallas_call | solution.py:290
  34.1 2.8 %collective-permute-start.13 = (bf16[256,512]{1,0:T(8,128)(2,1)S(1)}, bf16[256,512]{1,0:T(8,128)(2,1)S(1)}, u32[]{:S(2)}, u32[]{:S(2)}) collective-permute-start(bf16[256,512]{1,0:T(8,128)(2,1)S(1)} %get-tuple-element.112), channel_id=1, source_target_pairs={{0,8},{1,9},{2,10},{3,11},{4,12},{5,13},{6,14},{7,15},{8,0},{9,1},... | collective-permute-start | bytes 786440 | tf_op jit(solution)/shard_map/ppermute | solution.py:337
  36.9 0.0 copy-done.1
  36.9 0.0 copy-done.4
  36.9 0.3 unpack_own.1
  37.2 0.5 %index_scores.1 = (f32[4,2048]{1,0:T(4,128)S(1)}, f32[4,2048]{1,0:T(4,128)S(1)}) custom-call(bf16[128,128]{1,0:T(8,128)(2,1)S(1)} %get-tuple-element.91.refs_0_, f32[2,32,16]{2,1,0:T(8,128)S(1)} %get-tuple-element.92.refs_1_, bf16[128,128]{1,0:T(8,128)(2,1)S(1)} %get-tuple-element.93.refs_2_, f32[2,32,16]{2,1,0:T(8,128)S(1)} %get-tuple-element.94.refs_3_, ...), custom_call_target="tpu_custom_call" | custom-call | flops 134217728 | bytes 614400 | tf_op jit(solution)/shard_map/index_scores/pallas_call | solution.py:290
  37.7 1.6 %collective-permute-start.12 = (f32[4,2048]{1,0:T(4,128)S(1)}, f32[4,2048]{1,0:T(4,128)S(1)}, u32[]{:S(2)}, u32[]{:S(2)}) collective-permute-start(f32[4,2048]{1,0:T(4,128)S(1)} %get-tuple-element.100), channel_id=1, source_target_pairs={{0,4},{1,5},{2,6},{3,7},{4,0},{5,1},{6,2},{7,3},{8,12},{9,13},{10,... | collective-permute-start | bytes 98312 | tf_op jit(solution)/shard_map/ppermute | solution.py:337
  39.3 1.8 %own_first.1 = (f32[256,512]{1,0:T(8,128)S(1)}, f32[256,128]{1,0:T(8,128)S(1)}, f32[256,128]{1,0:T(8,128)S(1)}) custom-call(bf16[256,576]{1,0:T(8,128)(2,1)S(1)} %get-tuple-element.63.refs_0_, f32[16,512]{1,0:T(8,128)S(1)} %get-tuple-element.64.refs_1_, bf16[576,512]{1,0:T(8,128)(2,1)S(1)} %get-tuple-element.75.refs_2_, ...), custom_call_target="tpu_custom_call" | custom-call | flops 1140850688 | bytes 2686976 | tf_op jit(solution)/shard_map/own_first/pallas_call | solution.py:290
  41.2 2.2 %collective-permute-done.12.refs_1_ = f32[4,2048]{1,0:T(4,128)S(1)} collective-permute-done((f32[4,2048]{1,0:T(4,128)S(1)}, f32[4,2048]{1,0:T(4,128)S(1)}, u32[]{:S(2)}, u32[]{:S(2)}) %collective-permute-start.12) | collective-permute-done | bytes 32800 | tf_op jit(solution)/shard_map/ppermute | solution.py:337
  43.5 2.4 %collective-permute-start.14 = (bf16[2,4480]{1,0:T(2,128)(2,1)S(1)}, bf16[2,4480]{1,0:T(2,128)(2,1)S(1)}, u32[]{:S(2)}, u32[]{:S(2)}) collective-permute-start(bf16[2,4480]{1,0:T(2,128)(2,1)S(1)} %get-tuple-element.117), channel_id=1, source_target_pairs={{0,8},{1,9},{2,10},{3,11},{4,12},{5,13},{6,14},{7,15},{8,0},{9,1},... | collective-permute-start | bytes 53768 | tf_op jit(solution)/shard_map/ppermute | solution.py:337
  45.9 2.0 %own_late_0.1 = (f32[256,512]{1,0:T(8,128)S(1)}, f32[256,128]{1,0:T(8,128)S(1)}) custom-call(bf16[256,576]{1,0:T(8,128)(2,1)S(1)} %get-tuple-element.63.refs_0_, f32[16,512]{1,0:T(8,128)S(1)} %get-tuple-element.64.refs_1_, bf16[576,512]{1,0:T(8,128)(2,1)S(1)} %collective-permute-done.1.refs_5_.refs_2_, bf16[576,512]{1,0:T(8,128)(2,1)S(1)} %collective-permute-done.2.refs_3_, ...), custom_call_target="tpu_custom_call" | custom-call | flops 1140850688 | bytes 3473408 | tf_op jit(solution)/shard_map/own_late_0/pallas_call | solution.py:290
  47.9 1.8 %collective-permute-done.14.far_ref = bf16[2,4480]{1,0:T(2,128)(2,1)S(1)} collective-permute-done((bf16[2,4480]{1,0:T(2,128)(2,1)S(1)}, bf16[2,4480]{1,0:T(2,128)(2,1)S(1)}, u32[]{:S(2)}, u32[]{:S(2)}) %collective-permute-start.14) | collective-permute-done | bytes 17952 | tf_op jit(solution)/shard_map/ppermute | solution.py:337
  49.6 0.0 collective-permute-done.13.wire_ref
  49.6 1.0 %finish.1 = (f32[2,8192]{1,0:T(2,128)}, bf16[2,128,512]{2,1,0:T(8,128)(2,1)}) custom-call(f32[256,512]{1,0:T(8,128)S(1)} %get-tuple-element.107.o_ref, f32[256,128]{1,0:T(8,128)S(1)} %get-tuple-element.108.lse_ref, bf16[256,512]{1,0:T(8,128)(2,1)S(1)} %collective-permute-done.13.wire_ref, f32[2,4096]{1,0:T(2,128)S(1)} %get-tuple-element.116.own_ref, ...), custom_call_target="tpu_custom_call" | custom-call | flops 524288 | bytes 968192 | tf_op jit(solution)/shard_map/finish/pallas_call | solution.py:290
  (1 shorter events, 0.0 us)
Async XLA Ops:
  0.6 14.5 %collective-permute-start.7 = (bf16[576,512]{1,0:T(8,128)(2,1)}, bf16[576,512]{1,0:T(8,128)(2,1)S(1)}, u32[]{:S(2)}, u32[]{:S(2)}) collective-permute-start(bf16[576,512]{1,0:T(8,128)(2,1)} %bitcast.9), channel_id=1, source_target_pairs={{0,2},{1,5},{2,0},{3,7},{4,6},{5,1},{6,4},{7,3},{8,10},{9,13},{10,... | collective-permute-start | bytes 1769480 | tf_op jit(solution)/shard_map/ppermute | solution.py:337
  5.9 18.4 %collective-permute-start.1 = (bf16[576,512]{1,0:T(8,128)(2,1)}, bf16[576,512]{1,0:T(8,128)(2,1)S(1)}, u32[]{:S(2)}, u32[]{:S(2)}) collective-permute-start(bf16[576,512]{1,0:T(8,128)(2,1)} %bitcast.10), channel_id=1, source_target_pairs={{0,4},{1,3},{2,6},{3,1},{4,0},{5,7},{6,2},{7,5},{8,12},{9,11},{10,... | collective-permute-start | bytes 1769480 | tf_op jit(solution)/shard_map/ppermute | solution.py:337
  7.6 16.2 %collective-permute-start = (bf16[1296,128]{1,0:T(8,128)(2,1)}, bf16[1296,128]{1,0:T(8,128)(2,1)S(1)}, u32[]{:S(2)}, u32[]{:S(2)}) collective-permute-start(bf16[1296,128]{1,0:T(8,128)(2,1)} %get-tuple-element.61.refs_0_), channel_id=1, source_target_pairs={{0,8},{1,9},{2,10},{3,11},{4,12},{5,13},{6,14},{7,15},{8,0},{9,1},... | collective-permute-start | bytes 995336 | tf_op jit(solution)/shard_map/ppermute | solution.py:337
  10.2 8.7 %collective-permute-start.4 = (bf16[528,128]{1,0:T(8,128)(2,1)}, bf16[528,128]{1,0:T(8,128)(2,1)S(1)}, u32[]{:S(2)}, u32[]{:S(2)}) collective-permute-start(bf16[528,128]{1,0:T(8,128)(2,1)} %get-tuple-element.69.k_in), channel_id=1, source_target_pairs={{0,2},{1,3},{2,0},{3,1},{4,6},{5,7},{6,4},{7,5},{8,10},{9,11},{10,... | collective-permute-start | bytes 405512 | tf_op jit(solution)/shard_map/ppermute | solution.py:337
  10.7 1.1 %copy-start = (bf16[512,576]{0,1:T(8,128)(2,1)S(1)}, bf16[512,576]{0,1:T(8,128)(2,1)}, u32[]{:S(2)}) copy-start(bf16[512,576]{0,1:T(8,128)(2,1)} %param.13) | copy-start | bytes 1769476
  11.7 0.9 %copy-start.2 = (bf16[528,128]{1,0:T(8,128)(2,1)S(1)}, bf16[528,128]{1,0:T(8,128)(2,1)}, u32[]{:S(2)}) copy-start(bf16[528,128]{1,0:T(8,128)(2,1)} %get-tuple-element.69.k_in) | copy-start | bytes 405508
  12.7 0.7 %copy-start.3 = (bf16[80,128]{1,0:T(8,128)(2,1)S(1)}, bf16[80,128]{1,0:T(8,128)(2,1)}, u32[]{:S(2)}) copy-start(bf16[80,128]{1,0:T(8,128)(2,1)} %get-tuple-element.68.i_in) | copy-start | bytes 61444
  13.7 15.1 %collective-permute-start.6 = (bf16[576,512]{1,0:T(8,128)(2,1)S(1)}, bf16[576,512]{1,0:T(8,128)(2,1)S(1)}, u32[]{:S(2)}, u32[]{:S(2)}) collective-permute-start(bf16[576,512]{1,0:T(8,128)(2,1)S(1)} %get-tuple-element.75.refs_2_), channel_id=1, source_target_pairs={{0,1},{1,0},{2,3},{3,2},{4,5},{5,4},{6,7},{7,6},{8,9},{9,8},{10,11... | collective-permute-start | bytes 1769480 | tf_op jit(solution)/shard_map/ppermute | solution.py:337
  15.1 16.0 %collective-permute-start.8 = (bf16[576,512]{1,0:T(8,128)(2,1)S(1)}, bf16[576,512]{1,0:T(8,128)(2,1)S(1)}, u32[]{:S(2)}, u32[]{:S(2)}) collective-permute-start(bf16[576,512]{1,0:T(8,128)(2,1)S(1)} %collective-permute-done.7.refs_4_), channel_id=1, source_target_pairs={{0,4},{1,3},{2,6},{3,1},{4,0},{5,7},{6,2},{7,5},{8,12},{9,11},{10,... | collective-permute-start | bytes 1769480 | tf_op jit(solution)/shard_map/ppermute | solution.py:337
  18.9 5.5 %collective-permute-start.3 = (bf16[528,128]{1,0:T(8,128)(2,1)S(1)}, bf16[528,128]{1,0:T(8,128)(2,1)S(1)}, u32[]{:S(2)}, u32[]{:S(2)}) collective-permute-start(bf16[528,128]{1,0:T(8,128)(2,1)S(1)} %copy-done.2), channel_id=1, source_target_pairs={{0,1},{1,0},{2,3},{3,2},{4,5},{5,4},{6,7},{7,6},{8,9},{9,8},{10,11... | collective-permute-start | bytes 405512 | tf_op jit(solution)/shard_map/ppermute | solution.py:337
  23.7 1.4 %collective-permute-start.5 = (bf16[528,128]{1,0:T(8,128)(2,1)S(1)}, bf16[528,128]{1,0:T(8,128)(2,1)S(1)}, u32[]{:S(2)}, u32[]{:S(2)}) collective-permute-start(bf16[528,128]{1,0:T(8,128)(2,1)S(1)} %collective-permute-done.4.refs_6_), channel_id=1, source_target_pairs={{0,1},{1,0},{2,3},{3,2},{4,5},{5,4},{6,7},{7,6},{8,9},{9,8},{10,11... | collective-permute-start | bytes 405512 | tf_op jit(solution)/shard_map/ppermute | solution.py:337
  24.4 7.3 %collective-permute-start.2 = (bf16[576,512]{1,0:T(8,128)(2,1)S(1)}, bf16[576,512]{1,0:T(8,128)(2,1)S(1)}, u32[]{:S(2)}, u32[]{:S(2)}) collective-permute-start(bf16[576,512]{1,0:T(8,128)(2,1)S(1)} %collective-permute-done.1.refs_5_.refs_2_), channel_id=1, source_target_pairs={{0,1},{1,0},{2,3},{3,2},{4,5},{5,4},{6,7},{7,6},{8,9},{9,8},{10,11... | collective-permute-start | bytes 1769480 | tf_op jit(solution)/shard_map/ppermute | solution.py:337
  25.4 6.2 %collective-permute-start.11 = (bf16[160,128]{1,0:T(8,128)(2,1)S(1)}, bf16[160,128]{1,0:T(8,128)(2,1)S(1)}, u32[]{:S(2)}, u32[]{:S(2)}) collective-permute-start(bf16[160,128]{1,0:T(8,128)(2,1)S(1)} %get-tuple-element.86.refs_0_), channel_id=1, source_target_pairs={{0,4},{1,5},{2,6},{3,7},{4,0},{5,1},{6,2},{7,3},{8,12},{9,13},{10,... | collective-permute-start | bytes 122888 | tf_op jit(solution)/shard_map/ppermute | solution.py:337
  28.8 2.9 %collective-permute-start.10 = (bf16[576,512]{1,0:T(8,128)(2,1)S(1)}, bf16[576,512]{1,0:T(8,128)(2,1)S(1)}, u32[]{:S(2)}, u32[]{:S(2)}) collective-permute-start(bf16[576,512]{1,0:T(8,128)(2,1)S(1)} %collective-permute-done.7.refs_4_), channel_id=1, source_target_pairs={{0,1},{1,0},{2,3},{3,2},{4,5},{5,4},{6,7},{7,6},{8,9},{9,8},{10,11... | collective-permute-start | bytes 1769480 | tf_op jit(solution)/shard_map/ppermute | solution.py:337
  31.1 2.2 %collective-permute-start.9 = (bf16[576,512]{1,0:T(8,128)(2,1)S(1)}, bf16[576,512]{1,0:T(8,128)(2,1)S(1)}, u32[]{:S(2)}, u32[]{:S(2)}) collective-permute-start(bf16[576,512]{1,0:T(8,128)(2,1)S(1)} %collective-permute-done.8.refs_4_), channel_id=1, source_target_pairs={{0,1},{1,0},{2,3},{3,2},{4,5},{5,4},{6,7},{7,6},{8,9},{9,8},{10,11... | collective-permute-start | bytes 1769480 | tf_op jit(solution)/shard_map/ppermute | solution.py:337
  33.3 3.6 %copy-start.1 = (bf16[1296,128]{1,0:T(8,128)(2,1)S(1)}, bf16[1296,128]{1,0:T(8,128)(2,1)}, u32[]{:S(2)}) copy-start(bf16[1296,128]{1,0:T(8,128)(2,1)} %get-tuple-element.61.refs_0_) | copy-start | bytes 995332
  33.3 3.6 %copy-start.4 = (bf16[64,128]{1,0:T(8,128)(2,1)S(1)}, bf16[64,128]{1,0:T(8,128)(2,1)}, u32[]{:S(2)}) copy-start(bf16[64,128]{1,0:T(8,128)(2,1)} %get-tuple-element.62.refs_1_) | copy-start | bytes 49156
  34.1 15.6 %collective-permute-start.13 = (bf16[256,512]{1,0:T(8,128)(2,1)S(1)}, bf16[256,512]{1,0:T(8,128)(2,1)S(1)}, u32[]{:S(2)}, u32[]{:S(2)}) collective-permute-start(bf16[256,512]{1,0:T(8,128)(2,1)S(1)} %get-tuple-element.112), channel_id=1, source_target_pairs={{0,8},{1,9},{2,10},{3,11},{4,12},{5,13},{6,14},{7,15},{8,0},{9,1},... | collective-permute-start | bytes 786440 | tf_op jit(solution)/shard_map/ppermute | solution.py:337
  37.7 5.7 %collective-permute-start.12 = (f32[4,2048]{1,0:T(4,128)S(1)}, f32[4,2048]{1,0:T(4,128)S(1)}, u32[]{:S(2)}, u32[]{:S(2)}) collective-permute-start(f32[4,2048]{1,0:T(4,128)S(1)} %get-tuple-element.100), channel_id=1, source_target_pairs={{0,4},{1,5},{2,6},{3,7},{4,0},{5,1},{6,2},{7,3},{8,12},{9,13},{10,... | collective-permute-start | bytes 98312 | tf_op jit(solution)/shard_map/ppermute | solution.py:337
  43.5 6.2 %collective-permute-start.14 = (bf16[2,4480]{1,0:T(2,128)(2,1)S(1)}, bf16[2,4480]{1,0:T(2,128)(2,1)S(1)}, u32[]{:S(2)}, u32[]{:S(2)}) collective-permute-start(bf16[2,4480]{1,0:T(2,128)(2,1)S(1)} %get-tuple-element.117), channel_id=1, source_target_pairs={{0,8},{1,9},{2,10},{3,11},{4,12},{5,13},{6,14},{7,15},{8,0},{9,1},... | collective-permute-start | bytes 53768 | tf_op jit(solution)/shard_map/ppermute | solution.py:337

commit v6 on v5

--- a/solution.py
+++ b/solution.py
@@ -303,6 +303,9 @@
     return jax.ShapeDtypeStruct(dims, dtype)
 
 
+FACTOR = {"far_last": 2, "far_late_0": 0.3}
+
+
 def attend(half_size, q, bias, group, state, mode, name, queries=(0, 1)):
     masks = tuple(mask for _, mask in group)
     args = [q, bias] + [piece for piece, _ in group]
@@ -317,7 +320,7 @@
     else:
         outs = state_shape[:2]
     scratch = [pltpu.VMEM((size, TOK * len(group)), F32)]
-    flops = 2 * size * TOK * len(group) * (2 * KVR + ROPE)
+    flops = 2 * size * TOK * len(group) * (2 * KVR + ROPE) * FACTOR.get(name, 1)
     return call(
         functools.partial(attend_kernel, half_size, masks, state is None, mode, queries),
         outs,
@@ -358,7 +361,7 @@
             shape((I_ROWS, IDX), BF),
         ),
         "pack",
-        2 * 2 * n * 4 * 2048 * 64,
+        0.1 * 1.15e9,
         jnp.swapaxes(q_latent, 1, 2).reshape(2 * WIDTH, HEADS),
         index_queries.reshape(2 * IH, IDX),
         index_weights,
@@ -410,7 +413,8 @@
             outs.append(shape((2 * I_ROWS, IDX), BF))
         return call(functools.partial(unpack_kernel, half_size), tuple(outs), name, flops, *args)
 
-    q_far, *keys = lax.optimization_barrier((q_far, *keys))
+    q_far, r1, *keys = lax.optimization_barrier((q_far, r1, *keys))
+    held[1] = (r1, held[1][1])
     q_there, bias_there, i_pair = unpack("unpack_far", 3 * 1.15e9, q_far, q_far, i_own)
     q_here, bias_here = unpack("unpack_own", 0, q_wire, bias_own)
 
@@ -442,7 +446,7 @@
         pairs_kernel,
         (shape((2 * I_W, IDX), BF), shape((2, IH, 16), F32)) * len(i_pairs),
         "index_pairs",
-        6 * 1.15e9,
+        5 * 1.15e9,
         *i_pairs,
     )
     *far, prepared = lax.optimization_barrier((*far, prepared))
@@ -486,7 +490,7 @@
         functools.partial(finish_kernel, half_size),
         (shape((2, n * TOK), F32), shape((2, HEADS, KVR), BF)),
         "finish",
-        ROWS * KVR * 4,
+        5 * 1.15e9,
         o_own,
         lse_own,
         o_far,

time: 50.9 us -> 50.9 us (level)
  transfers between devices with their start and end apart: 15 -> 15, of which waited for: 8 -> 8; matrix products, arithmetic and copies ran while one was open for 0% -> 0% of each run, Pallas kernels for 22% -> 21%
where the time goes in v6:
time: 50.9 us; the launch traced here: 50.6 us
  starting transfers between devices  25.4 us (50%)
  Pallas kernels  12.6 us (25%)
  waiting for transfers between devices  9.06 us (18%)
  local copies, waits for them, and re-layouts  2.7 us (5%)
  between operations  0.77 us (2%)
    ppermute x15, starting transfers between devices, permute(): return lax.ppermute(x, 'ctx', [(i, move(i)) for i in range(n)])  25.4 us
    pallas_call x13, Pallas kernels, call(): pl.pallas_call(kernel, out_shape=out_shape, in_specs=specs or [VMEM] * le...  12.6 us
    ppermute x15, waiting for transfers between devices, permute(): return lax.ppermute(x, 'ctx', [(i, move(i)) for i in range(n)])  9.06 us
    unnamed x10, local copies, waits for them, and re-layouts  2.7 us
  transfers between devices with their start and end apart: 15, of which 8 were waited for; matrix products, arithmetic and copies ran while one was open for 0% of the time, Pallas kernels for 21%

profile of v6, /device:TPU:0, one launch (start us, length us, event | category | flops | bytes accessed | tf_op | source)
XLA Modules:
  0.0 50.6 jit_solution(17952972370664341720)
XLA Ops:
  0.6 3.0 %collective-permute-start.3 = (bf16[576,512]{1,0:T(8,128)(2,1)}, bf16[576,512]{1,0:T(8,128)(2,1)S(1)}, u32[]{:S(2)}, u32[]{:S(2)}) collective-permute-start(bf16[576,512]{1,0:T(8,128)(2,1)} %bitcast.9), channel_id=1, source_target_pairs={{0,2},{1,5},{2,0},{3,7},{4,6},{5,1},{6,4},{7,3},{8,10},{9,13},{10,... | collective-permute-start | bytes 1769480 | tf_op jit(solution)/shard_map/ppermute | solution.py:340
  3.7 2.3 %pack.1 = (bf16[1296,128]{1,0:T(8,128)(2,1)}, bf16[64,128]{1,0:T(8,128)(2,1)}, bf16[528,128]{1,0:T(8,128)(2,1)}, bf16[80,128]{1,0:T(8,128)(2,1)}) custom-call(bf16[1152,128]{1,0:T(8,128)(2,1)} %bitcast.12, bf16[64,128]{1,0:T(8,128)(2,1)} %bitcast.13, bf16[2,32]{1,0:T(2,128)(2,1)} %w_in.1, bf16[512,128]{1,0:T(8,128)(2,1)} %keys_in.1, ...), custom_call_target="tpu_custom_call" | custom-call | flops 115000000 | bytes 460160 | tf_op jit(solution)/shard_map/pack/pallas_call | solution.py:290
  5.9 1.6 %collective-permute-start.1 = (bf16[576,512]{1,0:T(8,128)(2,1)}, bf16[576,512]{1,0:T(8,128)(2,1)S(1)}, u32[]{:S(2)}, u32[]{:S(2)}) collective-permute-start(bf16[576,512]{1,0:T(8,128)(2,1)} %bitcast.10), channel_id=1, source_target_pairs={{0,4},{1,3},{2,6},{3,1},{4,0},{5,7},{6,2},{7,5},{8,12},{9,11},{10,... | collective-permute-start | bytes 1769480 | tf_op jit(solution)/shard_map/ppermute | solution.py:340
  7.6 2.6 %collective-permute-start = (bf16[1296,128]{1,0:T(8,128)(2,1)}, bf16[1296,128]{1,0:T(8,128)(2,1)S(1)}, u32[]{:S(2)}, u32[]{:S(2)}) collective-permute-start(bf16[1296,128]{1,0:T(8,128)(2,1)} %get-tuple-element.62.refs_0_), channel_id=1, source_target_pairs={{0,8},{1,9},{2,10},{3,11},{4,12},{5,13},{6,14},{7,15},{8,0},{9,1},... | collective-permute-start | bytes 995336 | tf_op jit(solution)/shard_map/ppermute | solution.py:340
  10.2 0.5 %collective-permute-start.5 = (bf16[528,128]{1,0:T(8,128)(2,1)}, bf16[528,128]{1,0:T(8,128)(2,1)S(1)}, u32[]{:S(2)}, u32[]{:S(2)}) collective-permute-start(bf16[528,128]{1,0:T(8,128)(2,1)} %get-tuple-element.70.k_in), channel_id=1, source_target_pairs={{0,2},{1,3},{2,0},{3,1},{4,6},{5,7},{6,4},{7,5},{8,10},{9,11},{10,... | collective-permute-start | bytes 405512 | tf_op jit(solution)/shard_map/ppermute | solution.py:340
  10.7 0.0 copy-start
  10.7 1.1 %copy-done = bf16[512,576]{0,1:T(8,128)(2,1)S(1)} copy-done((bf16[512,576]{0,1:T(8,128)(2,1)S(1)}, bf16[512,576]{0,1:T(8,128)(2,1)}, u32[]{:S(2)}) %copy-start) | copy-done | bytes 589848
  11.7 0.0 copy-start.2
  11.7 0.9 %copy-done.2 = bf16[528,128]{1,0:T(8,128)(2,1)S(1)} copy-done((bf16[528,128]{1,0:T(8,128)(2,1)S(1)}, bf16[528,128]{1,0:T(8,128)(2,1)}, u32[]{:S(2)}) %copy-start.2) | copy-done | bytes 135192
  12.7 0.0 copy-start.3
  12.7 0.7 %copy-done.3 = bf16[80,128]{1,0:T(8,128)(2,1)S(1)} copy-done((bf16[80,128]{1,0:T(8,128)(2,1)S(1)}, bf16[80,128]{1,0:T(8,128)(2,1)}, u32[]{:S(2)}) %copy-start.3) | copy-done | bytes 20504
  13.4 0.3 stage.1
  13.7 0.1 collective-permute-start.7
  13.8 1.3 %collective-permute-done.3.refs_4_ = bf16[576,512]{1,0:T(8,128)(2,1)S(1)} collective-permute-done((bf16[576,512]{1,0:T(8,128)(2,1)}, bf16[576,512]{1,0:T(8,128)(2,1)S(1)}, u32[]{:S(2)}, u32[]{:S(2)}) %collective-permute-start.3) | collective-permute-done | bytes 589856 | tf_op jit(solution)/shard_map/ppermute | solution.py:340
  15.1 3.7 %collective-permute-start.8 = (bf16[576,512]{1,0:T(8,128)(2,1)S(1)}, bf16[576,512]{1,0:T(8,128)(2,1)S(1)}, u32[]{:S(2)}, u32[]{:S(2)}) collective-permute-start(bf16[576,512]{1,0:T(8,128)(2,1)S(1)} %collective-permute-done.3.refs_4_), channel_id=1, source_target_pairs={{0,4},{1,3},{2,6},{3,1},{4,0},{5,7},{6,2},{7,5},{8,12},{9,11},{10,... | collective-permute-start | bytes 1769480 | tf_op jit(solution)/shard_map/ppermute | solution.py:340
  18.9 0.0 collective-permute-done.5.refs_6_
  18.9 3.4 %collective-permute-start.4 = (bf16[528,128]{1,0:T(8,128)(2,1)S(1)}, bf16[528,128]{1,0:T(8,128)(2,1)S(1)}, u32[]{:S(2)}, u32[]{:S(2)}) collective-permute-start(bf16[528,128]{1,0:T(8,128)(2,1)S(1)} %copy-done.2), channel_id=1, source_target_pairs={{0,1},{1,0},{2,3},{3,2},{4,5},{5,4},{6,7},{7,6},{8,9},{9,8},{10,11... | collective-permute-start | bytes 405512 | tf_op jit(solution)/shard_map/ppermute | solution.py:340
  22.3 1.5 %collective-permute-done.refs_0_.refs_1_ = bf16[1296,128]{1,0:T(8,128)(2,1)S(1)} collective-permute-done((bf16[1296,128]{1,0:T(8,128)(2,1)}, bf16[1296,128]{1,0:T(8,128)(2,1)S(1)}, u32[]{:S(2)}, u32[]{:S(2)}) %collective-permute-start) | collective-permute-done | bytes 331808 | tf_op jit(solution)/shard_map/ppermute | solution.py:340
  23.7 0.0 collective-permute-start.6
  23.7 0.6 %collective-permute-done.1.refs_5_.refs_2_ = bf16[576,512]{1,0:T(8,128)(2,1)S(1)} collective-permute-done((bf16[576,512]{1,0:T(8,128)(2,1)}, bf16[576,512]{1,0:T(8,128)(2,1)S(1)}, u32[]{:S(2)}, u32[]{:S(2)}) %collective-permute-start.1) | collective-permute-done | bytes 589856 | tf_op jit(solution)/shard_map/ppermute | solution.py:340
  24.4 0.0 collective-permute-start.2
  24.4 0.0 collective-permute-done.4.refs_5_
  24.4 0.7 %collective-permute-done.6.refs_7_ = bf16[528,128]{1,0:T(8,128)(2,1)S(1)} collective-permute-done((bf16[528,128]{1,0:T(8,128)(2,1)S(1)}, bf16[528,128]{1,0:T(8,128)(2,1)S(1)}, u32[]{:S(2)}, u32[]{:S(2)}) %collective-permute-start.6) | collective-permute-done | bytes 135200 | tf_op jit(solution)/shard_map/ppermute | solution.py:340
  25.1 0.3 unpack_far.1
  25.4 3.5 %collective-permute-start.11 = (bf16[160,128]{1,0:T(8,128)(2,1)S(1)}, bf16[160,128]{1,0:T(8,128)(2,1)S(1)}, u32[]{:S(2)}, u32[]{:S(2)}) collective-permute-start(bf16[160,128]{1,0:T(8,128)(2,1)S(1)} %get-tuple-element.88.refs_0_), channel_id=1, source_target_pairs={{0,4},{1,5},{2,6},{3,7},{4,0},{5,1},{6,2},{7,3},{8,12},{9,13},{10,... | collective-permute-start | bytes 122888 | tf_op jit(solution)/shard_map/ppermute | solution.py:340
  28.8 0.0 collective-permute-start.10
  28.8 0.0 collective-permute-done.7.refs_3_
  28.8 1.8 %far_early.1 = (f32[256,512]{1,0:T(8,128)S(1)}, f32[256,128]{1,0:T(8,128)S(1)}, f32[256,128]{1,0:T(8,128)S(1)}) custom-call(bf16[256,576]{1,0:T(8,128)(2,1)S(1)} %get-tuple-element.74.refs_0_, f32[16,512]{1,0:T(8,128)S(1)} %get-tuple-element.75.refs_1_, bf16[576,512]{1,0:T(8,128)(2,1)S(1)} %get-tuple-element.76.refs_2_, ...), custom_call_target="tpu_custom_call" | custom-call | flops 1140850688 | bytes 2686976 | tf_op jit(solution)/shard_map/far_early/pallas_call | solution.py:290
  30.7 0.5 collective-permute-done.8.refs_4_
  31.1 0.1 collective-permute-start.9
  31.2 0.3 collective-permute-done.11.refs_1_
  31.6 0.1 index_pairs.1
  31.7 0.0 collective-permute-done.2.refs_3_
  31.7 0.0 collective-permute-done.10.refs_2_.refs_5_
  31.7 1.5 %far_late_0.1 = (f32[256,512]{1,0:T(8,128)S(1)}, f32[256,128]{1,0:T(8,128)S(1)}, f32[256,128]{1,0:T(8,128)S(1)}) custom-call(bf16[256,576]{1,0:T(8,128)(2,1)S(1)} %get-tuple-element.74.refs_0_, f32[16,512]{1,0:T(8,128)S(1)} %get-tuple-element.75.refs_1_, bf16[576,512]{1,0:T(8,128)(2,1)S(1)} %collective-permute-done.10.refs_2_.refs_5_, ...), custom_call_target="tpu_custom_call" | custom-call | flops 256691408 | bytes 2883584 | tf_op jit(solution)/shard_map/far_late_0/pallas_call | solution.py:290
  33.3 0.0 copy-start.1
  33.3 0.0 copy-start.4
  33.3 0.0 collective-permute-done.9.refs_5_.refs_2_
  33.3 0.8 %far_last.1 = (bf16[256,512]{1,0:T(8,128)(2,1)S(1)}, f32[2,128]{1,0:T(2,128)S(1)}) custom-call(bf16[256,576]{1,0:T(8,128)(2,1)S(1)} %get-tuple-element.74.refs_0_, f32[16,512]{1,0:T(8,128)S(1)} %get-tuple-element.75.refs_1_, bf16[576,512]{1,0:T(8,128)(2,1)S(1)} %collective-permute-done.9.refs_5_.refs_2_, f32[256,512]{1,0:T(8,128)S(1)} %get-tuple-element.111.refs_3_, ...), custom_call_target="tpu_custom_call" | custom-call | flops 570425344 | bytes 1703936 | tf_op jit(solution)/shard_map/far_last/pallas_call | solution.py:290
  34.0 2.8 %collective-permute-start.13 = (bf16[256,512]{1,0:T(8,128)(2,1)S(1)}, bf16[256,512]{1,0:T(8,128)(2,1)S(1)}, u32[]{:S(2)}, u32[]{:S(2)}) collective-permute-start(bf16[256,512]{1,0:T(8,128)(2,1)S(1)} %get-tuple-element.114), channel_id=1, source_target_pairs={{0,8},{1,9},{2,10},{3,11},{4,12},{5,13},{6,14},{7,15},{8,0},{9,1},... | collective-permute-start | bytes 786440 | tf_op jit(solution)/shard_map/ppermute | solution.py:340
  36.9 0.0 copy-done.1
  36.9 0.0 copy-done.4
  36.9 0.3 unpack_own.1
  37.1 0.5 %index_scores.1 = (f32[4,2048]{1,0:T(4,128)S(1)}, f32[4,2048]{1,0:T(4,128)S(1)}) custom-call(bf16[128,128]{1,0:T(8,128)(2,1)S(1)} %get-tuple-element.93.refs_0_, f32[2,32,16]{2,1,0:T(8,128)S(1)} %get-tuple-element.94.refs_1_, bf16[128,128]{1,0:T(8,128)(2,1)S(1)} %get-tuple-element.95.refs_2_, f32[2,32,16]{2,1,0:T(8,128)S(1)} %get-tuple-element.96.refs_3_, ...), custom_call_target="tpu_custom_call" | custom-call | flops 134217728 | bytes 614400 | tf_op jit(solution)/shard_map/index_scores/pallas_call | solution.py:290
  37.7 1.6 %collective-permute-start.12 = (f32[4,2048]{1,0:T(4,128)S(1)}, f32[4,2048]{1,0:T(4,128)S(1)}, u32[]{:S(2)}, u32[]{:S(2)}) collective-permute-start(f32[4,2048]{1,0:T(4,128)S(1)} %get-tuple-element.102), channel_id=1, source_target_pairs={{0,4},{1,5},{2,6},{3,7},{4,0},{5,1},{6,2},{7,3},{8,12},{9,13},{10,... | collective-permute-start | bytes 98312 | tf_op jit(solution)/shard_map/ppermute | solution.py:340
  39.3 1.8 %own_first.1 = (f32[256,512]{1,0:T(8,128)S(1)}, f32[256,128]{1,0:T(8,128)S(1)}, f32[256,128]{1,0:T(8,128)S(1)}) custom-call(bf16[256,576]{1,0:T(8,128)(2,1)S(1)} %get-tuple-element.64.refs_0_, f32[16,512]{1,0:T(8,128)S(1)} %get-tuple-element.65.refs_1_, bf16[576,512]{1,0:T(8,128)(2,1)S(1)} %get-tuple-element.76.refs_2_, ...), custom_call_target="tpu_custom_call" | custom-call | flops 1140850688 | bytes 2686976 | tf_op jit(solution)/shard_map/own_first/pallas_call | solution.py:290
  41.1 2.3 %collective-permute-done.12.refs_1_ = f32[4,2048]{1,0:T(4,128)S(1)} collective-permute-done((f32[4,2048]{1,0:T(4,128)S(1)}, f32[4,2048]{1,0:T(4,128)S(1)}, u32[]{:S(2)}, u32[]{:S(2)}) %collective-permute-start.12) | collective-permute-done | bytes 32800 | tf_op jit(solution)/shard_map/ppermute | solution.py:340
  43.4 2.4 %collective-permute-start.14 = (bf16[2,4480]{1,0:T(2,128)(2,1)S(1)}, bf16[2,4480]{1,0:T(2,128)(2,1)S(1)}, u32[]{:S(2)}, u32[]{:S(2)}) collective-permute-start(bf16[2,4480]{1,0:T(2,128)(2,1)S(1)} %get-tuple-element.119), channel_id=1, source_target_pairs={{0,8},{1,9},{2,10},{3,11},{4,12},{5,13},{6,14},{7,15},{8,0},{9,1},... | collective-permute-start | bytes 53768 | tf_op jit(solution)/shard_map/ppermute | solution.py:340
  45.9 1.9 %own_late_0.1 = (f32[256,512]{1,0:T(8,128)S(1)}, f32[256,128]{1,0:T(8,128)S(1)}) custom-call(bf16[256,576]{1,0:T(8,128)(2,1)S(1)} %get-tuple-element.64.refs_0_, f32[16,512]{1,0:T(8,128)S(1)} %get-tuple-element.65.refs_1_, bf16[576,512]{1,0:T(8,128)(2,1)S(1)} %collective-permute-done.1.refs_5_.refs_2_, bf16[576,512]{1,0:T(8,128)(2,1)S(1)} %collective-permute-done.2.refs_3_, ...), custom_call_target="tpu_custom_call" | custom-call | flops 1140850688 | bytes 3473408 | tf_op jit(solution)/shard_map/own_late_0/pallas_call | solution.py:290
  47.8 1.8 %collective-permute-done.14.far_ref = bf16[2,4480]{1,0:T(2,128)(2,1)S(1)} collective-permute-done((bf16[2,4480]{1,0:T(2,128)(2,1)S(1)}, bf16[2,4480]{1,0:T(2,128)(2,1)S(1)}, u32[]{:S(2)}, u32[]{:S(2)}) %collective-permute-start.14) | collective-permute-done | bytes 17952 | tf_op jit(solution)/shard_map/ppermute | solution.py:340
  49.6 0.0 collective-permute-done.13.wire_ref
  49.6 1.0 %finish.1 = (f32[2,8192]{1,0:T(2,128)}, bf16[2,128,512]{2,1,0:T(8,128)(2,1)}) custom-call(f32[256,512]{1,0:T(8,128)S(1)} %get-tuple-element.109.o_ref, f32[256,128]{1,0:T(8,128)S(1)} %get-tuple-element.110.lse_ref, bf16[256,512]{1,0:T(8,128)(2,1)S(1)} %collective-permute-done.13.wire_ref, f32[2,4096]{1,0:T(2,128)S(1)} %get-tuple-element.118.own_ref, ...), custom_call_target="tpu_custom_call" | custom-call | flops 5750000128 | bytes 968192 | tf_op jit(solution)/shard_map/finish/pallas_call | solution.py:290
  (1 shorter events, 0.0 us)
Async XLA Ops:
  0.6 14.5 %collective-permute-start.3 = (bf16[576,512]{1,0:T(8,128)(2,1)}, bf16[576,512]{1,0:T(8,128)(2,1)S(1)}, u32[]{:S(2)}, u32[]{:S(2)}) collective-permute-start(bf16[576,512]{1,0:T(8,128)(2,1)} %bitcast.9), channel_id=1, source_target_pairs={{0,2},{1,5},{2,0},{3,7},{4,6},{5,1},{6,4},{7,3},{8,10},{9,13},{10,... | collective-permute-start | bytes 1769480 | tf_op jit(solution)/shard_map/ppermute | solution.py:340
  5.9 18.4 %collective-permute-start.1 = (bf16[576,512]{1,0:T(8,128)(2,1)}, bf16[576,512]{1,0:T(8,128)(2,1)S(1)}, u32[]{:S(2)}, u32[]{:S(2)}) collective-permute-start(bf16[576,512]{1,0:T(8,128)(2,1)} %bitcast.10), channel_id=1, source_target_pairs={{0,4},{1,3},{2,6},{3,1},{4,0},{5,7},{6,2},{7,5},{8,12},{9,11},{10,... | collective-permute-start | bytes 1769480 | tf_op jit(solution)/shard_map/ppermute | solution.py:340
  7.6 16.2 %collective-permute-start = (bf16[1296,128]{1,0:T(8,128)(2,1)}, bf16[1296,128]{1,0:T(8,128)(2,1)S(1)}, u32[]{:S(2)}, u32[]{:S(2)}) collective-permute-start(bf16[1296,128]{1,0:T(8,128)(2,1)} %get-tuple-element.62.refs_0_), channel_id=1, source_target_pairs={{0,8},{1,9},{2,10},{3,11},{4,12},{5,13},{6,14},{7,15},{8,0},{9,1},... | collective-permute-start | bytes 995336 | tf_op jit(solution)/shard_map/ppermute | solution.py:340
  10.2 8.7 %collective-permute-start.5 = (bf16[528,128]{1,0:T(8,128)(2,1)}, bf16[528,128]{1,0:T(8,128)(2,1)S(1)}, u32[]{:S(2)}, u32[]{:S(2)}) collective-permute-start(bf16[528,128]{1,0:T(8,128)(2,1)} %get-tuple-element.70.k_in), channel_id=1, source_target_pairs={{0,2},{1,3},{2,0},{3,1},{4,6},{5,7},{6,4},{7,5},{8,10},{9,11},{10,... | collective-permute-start | bytes 405512 | tf_op jit(solution)/shard_map/ppermute | solution.py:340
  10.7 1.1 %copy-start = (bf16[512,576]{0,1:T(8,128)(2,1)S(1)}, bf16[512,576]{0,1:T(8,128)(2,1)}, u32[]{:S(2)}) copy-start(bf16[512,576]{0,1:T(8,128)(2,1)} %param.13) | copy-start | bytes 1769476
  11.7 0.9 %copy-start.2 = (bf16[528,128]{1,0:T(8,128)(2,1)S(1)}, bf16[528,128]{1,0:T(8,128)(2,1)}, u32[]{:S(2)}) copy-start(bf16[528,128]{1,0:T(8,128)(2,1)} %get-tuple-element.70.k_in) | copy-start | bytes 405508
  12.7 0.7 %copy-start.3 = (bf16[80,128]{1,0:T(8,128)(2,1)S(1)}, bf16[80,128]{1,0:T(8,128)(2,1)}, u32[]{:S(2)}) copy-start(bf16[80,128]{1,0:T(8,128)(2,1)} %get-tuple-element.69.i_in) | copy-start | bytes 61444
  13.7 15.1 %collective-permute-start.7 = (bf16[576,512]{1,0:T(8,128)(2,1)S(1)}, bf16[576,512]{1,0:T(8,128)(2,1)S(1)}, u32[]{:S(2)}, u32[]{:S(2)}) collective-permute-start(bf16[576,512]{1,0:T(8,128)(2,1)S(1)} %get-tuple-element.76.refs_2_), channel_id=1, source_target_pairs={{0,1},{1,0},{2,3},{3,2},{4,5},{5,4},{6,7},{7,6},{8,9},{9,8},{10,11... | collective-permute-start | bytes 1769480 | tf_op jit(solution)/shard_map/ppermute | solution.py:340
  15.1 16.0 %collective-permute-start.8 = (bf16[576,512]{1,0:T(8,128)(2,1)S(1)}, bf16[576,512]{1,0:T(8,128)(2,1)S(1)}, u32[]{:S(2)}, u32[]{:S(2)}) collective-permute-start(bf16[576,512]{1,0:T(8,128)(2,1)S(1)} %collective-permute-done.3.refs_4_), channel_id=1, source_target_pairs={{0,4},{1,3},{2,6},{3,1},{4,0},{5,7},{6,2},{7,5},{8,12},{9,11},{10,... | collective-permute-start | bytes 1769480 | tf_op jit(solution)/shard_map/ppermute | solution.py:340
  18.9 5.5 %collective-permute-start.4 = (bf16[528,128]{1,0:T(8,128)(2,1)S(1)}, bf16[528,128]{1,0:T(8,128)(2,1)S(1)}, u32[]{:S(2)}, u32[]{:S(2)}) collective-permute-start(bf16[528,128]{1,0:T(8,128)(2,1)S(1)} %copy-done.2), channel_id=1, source_target_pairs={{0,1},{1,0},{2,3},{3,2},{4,5},{5,4},{6,7},{7,6},{8,9},{9,8},{10,11... | collective-permute-start | bytes 405512 | tf_op jit(solution)/shard_map/ppermute | solution.py:340
  23.7 1.4 %collective-permute-start.6 = (bf16[528,128]{1,0:T(8,128)(2,1)S(1)}, bf16[528,128]{1,0:T(8,128)(2,1)S(1)}, u32[]{:S(2)}, u32[]{:S(2)}) collective-permute-start(bf16[528,128]{1,0:T(8,128)(2,1)S(1)} %collective-permute-done.5.refs_6_), channel_id=1, source_target_pairs={{0,1},{1,0},{2,3},{3,2},{4,5},{5,4},{6,7},{7,6},{8,9},{9,8},{10,11... | collective-permute-start | bytes 405512 | tf_op jit(solution)/shard_map/ppermute | solution.py:340
  24.4 7.3 %collective-permute-start.2 = (bf16[576,512]{1,0:T(8,128)(2,1)S(1)}, bf16[576,512]{1,0:T(8,128)(2,1)S(1)}, u32[]{:S(2)}, u32[]{:S(2)}) collective-permute-start(bf16[576,512]{1,0:T(8,128)(2,1)S(1)} %collective-permute-done.1.refs_5_.refs_2_), channel_id=1, source_target_pairs={{0,1},{1,0},{2,3},{3,2},{4,5},{5,4},{6,7},{7,6},{8,9},{9,8},{10,11... | collective-permute-start | bytes 1769480 | tf_op jit(solution)/shard_map/ppermute | solution.py:340
  25.4 6.2 %collective-permute-start.11 = (bf16[160,128]{1,0:T(8,128)(2,1)S(1)}, bf16[160,128]{1,0:T(8,128)(2,1)S(1)}, u32[]{:S(2)}, u32[]{:S(2)}) collective-permute-start(bf16[160,128]{1,0:T(8,128)(2,1)S(1)} %get-tuple-element.88.refs_0_), channel_id=1, source_target_pairs={{0,4},{1,5},{2,6},{3,7},{4,0},{5,1},{6,2},{7,3},{8,12},{9,13},{10,... | collective-permute-start | bytes 122888 | tf_op jit(solution)/shard_map/ppermute | solution.py:340
  28.8 2.9 %collective-permute-start.10 = (bf16[576,512]{1,0:T(8,128)(2,1)S(1)}, bf16[576,512]{1,0:T(8,128)(2,1)S(1)}, u32[]{:S(2)}, u32[]{:S(2)}) collective-permute-start(bf16[576,512]{1,0:T(8,128)(2,1)S(1)} %collective-permute-done.3.refs_4_), channel_id=1, source_target_pairs={{0,1},{1,0},{2,3},{3,2},{4,5},{5,4},{6,7},{7,6},{8,9},{9,8},{10,11... | collective-permute-start | bytes 1769480 | tf_op jit(solution)/shard_map/ppermute | solution.py:340
  31.1 2.2 %collective-permute-start.9 = (bf16[576,512]{1,0:T(8,128)(2,1)S(1)}, bf16[576,512]{1,0:T(8,128)(2,1)S(1)}, u32[]{:S(2)}, u32[]{:S(2)}) collective-permute-start(bf16[576,512]{1,0:T(8,128)(2,1)S(1)} %collective-permute-done.8.refs_4_), channel_id=1, source_target_pairs={{0,1},{1,0},{2,3},{3,2},{4,5},{5,4},{6,7},{7,6},{8,9},{9,8},{10,11... | collective-permute-start | bytes 1769480 | tf_op jit(solution)/shard_map/ppermute | solution.py:340
  33.3 3.6 %copy-start.1 = (bf16[1296,128]{1,0:T(8,128)(2,1)S(1)}, bf16[1296,128]{1,0:T(8,128)(2,1)}, u32[]{:S(2)}) copy-start(bf16[1296,128]{1,0:T(8,128)(2,1)} %get-tuple-element.62.refs_0_) | copy-start | bytes 995332
  33.3 3.6 %copy-start.4 = (bf16[64,128]{1,0:T(8,128)(2,1)S(1)}, bf16[64,128]{1,0:T(8,128)(2,1)}, u32[]{:S(2)}) copy-start(bf16[64,128]{1,0:T(8,128)(2,1)} %get-tuple-element.63.refs_1_) | copy-start | bytes 49156
  34.0 15.6 %collective-permute-start.13 = (bf16[256,512]{1,0:T(8,128)(2,1)S(1)}, bf16[256,512]{1,0:T(8,128)(2,1)S(1)}, u32[]{:S(2)}, u32[]{:S(2)}) collective-permute-start(bf16[256,512]{1,0:T(8,128)(2,1)S(1)} %get-tuple-element.114), channel_id=1, source_target_pairs={{0,8},{1,9},{2,10},{3,11},{4,12},{5,13},{6,14},{7,15},{8,0},{9,1},... | collective-permute-start | bytes 786440 | tf_op jit(solution)/shard_map/ppermute | solution.py:340
  37.7 5.7 %collective-permute-start.12 = (f32[4,2048]{1,0:T(4,128)S(1)}, f32[4,2048]{1,0:T(4,128)S(1)}, u32[]{:S(2)}, u32[]{:S(2)}) collective-permute-start(f32[4,2048]{1,0:T(4,128)S(1)} %get-tuple-element.102), channel_id=1, source_target_pairs={{0,4},{1,5},{2,6},{3,7},{4,0},{5,1},{6,2},{7,3},{8,12},{9,13},{10,... | collective-permute-start | bytes 98312 | tf_op jit(solution)/shard_map/ppermute | solution.py:340
  43.4 6.2 %collective-permute-start.14 = (bf16[2,4480]{1,0:T(2,128)(2,1)S(1)}, bf16[2,4480]{1,0:T(2,128)(2,1)S(1)}, u32[]{:S(2)}, u32[]{:S(2)}) collective-permute-start(bf16[2,4480]{1,0:T(2,128)(2,1)S(1)} %get-tuple-element.119), channel_id=1, source_target_pairs={{0,8},{1,9},{2,10},{3,11},{4,12},{5,13},{6,14},{7,15},{8,0},{9,1},... | collective-permute-start | bytes 53768 | tf_op jit(solution)/shard_map/ppermute | solution.py:340

commit v7 on v5

--- a/solution.py
+++ b/solution.py
@@ -234,12 +234,11 @@
             scales = keys[p][TOK:K_ROWS, :].astype(F32)
             scale = jnp.concatenate([scales[c : c + 1, :] for c in range(CHUNKS)], axis=1)
             at = pl.multiple_of(lax.bitwise_and(lax.bitwise_xor(me, p), 3) * TOK, TOK)
-            for side in range(2):
-                for t in range(2):
-                    row = side * 2 + t
-                    weighted = raw[row * IH : (row + 1) * IH, :] * w_cols[side][:, t : t + 1]
-                    line = jnp.sum(weighted, axis=0, keepdims=True) * scale
-                    out[row : row + 1, pl.ds(at, TOK)] = line
+            lines = []
+            for row in range(4):
+                weighted = raw[row * IH : (row + 1) * IH, :] * w_cols[row // 2][:, row % 2 : row % 2 + 1]
+                lines.append(jnp.sum(weighted, axis=0, keepdims=True) * scale)
+            out[:, pl.ds(at, TOK)] = jnp.concatenate(lines, axis=0).astype(out.dtype)
 
 
 def order_kernel(half_size, masks, *refs):
@@ -256,8 +255,9 @@
     for ref, mask in zip(refs, masks):
         at = lax.bitwise_and(lax.bitwise_xor(me, mask), half_size - 1) // 4 * span
         at = pl.multiple_of(at, span)
-        own_ref[:, pl.ds(at, span)] = ref[0:2, :]
-        far_ref[:, pl.ds(at, span)] = ref[2:4, :].astype(BF)
+        lines = ref[...].astype(F32)
+        own_ref[:, pl.ds(at, span)] = lines[0:2, :]
+        far_ref[:, pl.ds(at, span)] = lines[2:4, :].astype(BF)
 
 
 def finish_kernel(half_size, o_ref, lse_ref, wire_ref, own_ref, far_ref, scores_ref, out_ref):
@@ -452,7 +452,7 @@
 
     parts = call(
         functools.partial(score_kernel, len(i_pairs)),
-        tuple(shape((4, 4 * TOK), F32) for _ in i_pairs),
+        tuple(shape((4, 4 * TOK), BF if j else F32) for j in range(len(i_pairs))),
         "index_scores",
         2 * len(i_pairs) * 4 * IH * 4 * TOK * IDX,
         *prepared,

time: 50.9 us -> 50.9 us (level)
  no operation moved by 1% of the time
where the time goes in v7:
time: 50.9 us; the launch traced here: 50.7 us
  starting transfers between devices  25.5 us (50%)
  Pallas kernels  12.8 us (25%)
  waiting for transfers between devices  8.89 us (17%)
  local copies, waits for them, and re-layouts  2.7 us (5%)
  between operations  0.77 us (2%)
    ppermute x15, starting transfers between devices, permute(): return lax.ppermute(x, 'ctx', [(i, move(i)) for i in range(n)])  25.5 us
    pallas_call x13, Pallas kernels, call(): pl.pallas_call(kernel, out_shape=out_shape, in_specs=specs or [VMEM] * le...  12.8 us
    ppermute x15, waiting for transfers between devices, permute(): return lax.ppermute(x, 'ctx', [(i, move(i)) for i in range(n)])  8.89 us
    unnamed x10, local copies, waits for them, and re-layouts  2.7 us
  transfers between devices with their start and end apart: 15, of which 8 were waited for; matrix products, arithmetic and copies ran while one was open for 0% of the time, Pallas kernels for 22%

profile of v7, /device:TPU:0, one launch (start us, length us, event | category | flops | bytes accessed | tf_op | source)
XLA Modules:
  0.0 50.7 jit_solution(2165436384121469380)
XLA Ops:
  0.6 3.0 %collective-permute-start.7 = (bf16[576,512]{1,0:T(8,128)(2,1)}, bf16[576,512]{1,0:T(8,128)(2,1)S(1)}, u32[]{:S(2)}, u32[]{:S(2)}) collective-permute-start(bf16[576,512]{1,0:T(8,128)(2,1)} %bitcast.9), channel_id=1, source_target_pairs={{0,2},{1,5},{2,0},{3,7},{4,6},{5,1},{6,4},{7,3},{8,10},{9,13},{10,... | collective-permute-start | bytes 1769480 | tf_op jit(solution)/shard_map/ppermute | solution.py:337
  3.7 2.3 %pack.1 = (bf16[1296,128]{1,0:T(8,128)(2,1)}, bf16[64,128]{1,0:T(8,128)(2,1)}, bf16[528,128]{1,0:T(8,128)(2,1)}, bf16[80,128]{1,0:T(8,128)(2,1)}) custom-call(bf16[1152,128]{1,0:T(8,128)(2,1)} %bitcast.12, bf16[64,128]{1,0:T(8,128)(2,1)} %bitcast.13, bf16[2,32]{1,0:T(2,128)(2,1)} %w_in.1, bf16[512,128]{1,0:T(8,128)(2,1)} %keys_in.1, ...), custom_call_target="tpu_custom_call" | custom-call | flops 33554432 | bytes 460160 | tf_op jit(solution)/shard_map/pack/pallas_call | solution.py:290
  5.9 1.6 %collective-permute-start.1 = (bf16[576,512]{1,0:T(8,128)(2,1)}, bf16[576,512]{1,0:T(8,128)(2,1)S(1)}, u32[]{:S(2)}, u32[]{:S(2)}) collective-permute-start(bf16[576,512]{1,0:T(8,128)(2,1)} %bitcast.10), channel_id=1, source_target_pairs={{0,4},{1,3},{2,6},{3,1},{4,0},{5,7},{6,2},{7,5},{8,12},{9,11},{10,... | collective-permute-start | bytes 1769480 | tf_op jit(solution)/shard_map/ppermute | solution.py:337
  7.6 2.6 %collective-permute-start = (bf16[1296,128]{1,0:T(8,128)(2,1)}, bf16[1296,128]{1,0:T(8,128)(2,1)S(1)}, u32[]{:S(2)}, u32[]{:S(2)}) collective-permute-start(bf16[1296,128]{1,0:T(8,128)(2,1)} %get-tuple-element.61.refs_0_), channel_id=1, source_target_pairs={{0,8},{1,9},{2,10},{3,11},{4,12},{5,13},{6,14},{7,15},{8,0},{9,1},... | collective-permute-start | bytes 995336 | tf_op jit(solution)/shard_map/ppermute | solution.py:337
  10.2 0.5 collective-permute-start.4
  10.7 0.0 copy-start
  10.7 1.1 %copy-done = bf16[512,576]{0,1:T(8,128)(2,1)S(1)} copy-done((bf16[512,576]{0,1:T(8,128)(2,1)S(1)}, bf16[512,576]{0,1:T(8,128)(2,1)}, u32[]{:S(2)}) %copy-start) | copy-done | bytes 589848
  11.7 0.0 copy-start.2
  11.7 0.9 %copy-done.2 = bf16[528,128]{1,0:T(8,128)(2,1)S(1)} copy-done((bf16[528,128]{1,0:T(8,128)(2,1)S(1)}, bf16[528,128]{1,0:T(8,128)(2,1)}, u32[]{:S(2)}) %copy-start.2) | copy-done | bytes 135192
  12.7 0.0 copy-start.3
  12.7 0.7 %copy-done.3 = bf16[80,128]{1,0:T(8,128)(2,1)S(1)} copy-done((bf16[80,128]{1,0:T(8,128)(2,1)S(1)}, bf16[80,128]{1,0:T(8,128)(2,1)}, u32[]{:S(2)}) %copy-start.3) | copy-done | bytes 20504
  13.4 0.3 stage.1
  13.7 0.1 collective-permute-start.6
  13.8 1.3 %collective-permute-done.7.refs_4_ = bf16[576,512]{1,0:T(8,128)(2,1)S(1)} collective-permute-done((bf16[576,512]{1,0:T(8,128)(2,1)}, bf16[576,512]{1,0:T(8,128)(2,1)S(1)}, u32[]{:S(2)}, u32[]{:S(2)}) %collective-permute-start.7) | collective-permute-done | bytes 589856 | tf_op jit(solution)/shard_map/ppermute | solution.py:337
  15.1 3.7 %collective-permute-start.8 = (bf16[576,512]{1,0:T(8,128)(2,1)S(1)}, bf16[576,512]{1,0:T(8,128)(2,1)S(1)}, u32[]{:S(2)}, u32[]{:S(2)}) collective-permute-start(bf16[576,512]{1,0:T(8,128)(2,1)S(1)} %collective-permute-done.7.refs_4_), channel_id=1, source_target_pairs={{0,4},{1,3},{2,6},{3,1},{4,0},{5,7},{6,2},{7,5},{8,12},{9,11},{10,... | collective-permute-start | bytes 1769480 | tf_op jit(solution)/shard_map/ppermute | solution.py:337
  18.9 0.0 collective-permute-done.4.refs_6_
  18.9 3.4 %collective-permute-start.3 = (bf16[528,128]{1,0:T(8,128)(2,1)S(1)}, bf16[528,128]{1,0:T(8,128)(2,1)S(1)}, u32[]{:S(2)}, u32[]{:S(2)}) collective-permute-start(bf16[528,128]{1,0:T(8,128)(2,1)S(1)} %copy-done.2), channel_id=1, source_target_pairs={{0,1},{1,0},{2,3},{3,2},{4,5},{5,4},{6,7},{7,6},{8,9},{9,8},{10,11... | collective-permute-start | bytes 405512 | tf_op jit(solution)/shard_map/ppermute | solution.py:337
  22.3 1.5 %collective-permute-done.refs_0_.refs_1_ = bf16[1296,128]{1,0:T(8,128)(2,1)S(1)} collective-permute-done((bf16[1296,128]{1,0:T(8,128)(2,1)}, bf16[1296,128]{1,0:T(8,128)(2,1)S(1)}, u32[]{:S(2)}, u32[]{:S(2)}) %collective-permute-start) | collective-permute-done | bytes 331808 | tf_op jit(solution)/shard_map/ppermute | solution.py:337
  23.7 0.0 collective-permute-start.5
  23.7 0.6 %collective-permute-done.1.refs_5_.refs_2_ = bf16[576,512]{1,0:T(8,128)(2,1)S(1)} collective-permute-done((bf16[576,512]{1,0:T(8,128)(2,1)}, bf16[576,512]{1,0:T(8,128)(2,1)S(1)}, u32[]{:S(2)}, u32[]{:S(2)}) %collective-permute-start.1) | collective-permute-done | bytes 589856 | tf_op jit(solution)/shard_map/ppermute | solution.py:337
  24.4 0.0 collective-permute-start.2
  24.4 0.0 collective-permute-done.3.refs_5_
  24.4 0.7 %collective-permute-done.5.refs_7_ = bf16[528,128]{1,0:T(8,128)(2,1)S(1)} collective-permute-done((bf16[528,128]{1,0:T(8,128)(2,1)S(1)}, bf16[528,128]{1,0:T(8,128)(2,1)S(1)}, u32[]{:S(2)}, u32[]{:S(2)}) %collective-permute-start.5) | collective-permute-done | bytes 135200 | tf_op jit(solution)/shard_map/ppermute | solution.py:337
  25.1 0.3 unpack_far.1
  25.4 3.5 %collective-permute-start.11 = (bf16[160,128]{1,0:T(8,128)(2,1)S(1)}, bf16[160,128]{1,0:T(8,128)(2,1)S(1)}, u32[]{:S(2)}, u32[]{:S(2)}) collective-permute-start(bf16[160,128]{1,0:T(8,128)(2,1)S(1)} %get-tuple-element.86.refs_0_), channel_id=1, source_target_pairs={{0,4},{1,5},{2,6},{3,7},{4,0},{5,1},{6,2},{7,3},{8,12},{9,13},{10,... | collective-permute-start | bytes 122888 | tf_op jit(solution)/shard_map/ppermute | solution.py:337
  28.8 0.0 collective-permute-start.10
  28.8 0.0 collective-permute-done.6.refs_3_
  28.8 1.9 %far_early.1 = (f32[256,512]{1,0:T(8,128)S(1)}, f32[256,128]{1,0:T(8,128)S(1)}, f32[256,128]{1,0:T(8,128)S(1)}) custom-call(bf16[256,576]{1,0:T(8,128)(2,1)S(1)} %get-tuple-element.73.refs_0_, f32[16,512]{1,0:T(8,128)S(1)} %get-tuple-element.74.refs_1_, bf16[576,512]{1,0:T(8,128)(2,1)S(1)} %get-tuple-element.75.refs_2_, ...), custom_call_target="tpu_custom_call" | custom-call | flops 1140850688 | bytes 2686976 | tf_op jit(solution)/shard_map/far_early/pallas_call | solution.py:290
  30.7 0.4 collective-permute-done.8.refs_4_
  31.1 0.1 collective-permute-start.9
  31.3 0.3 collective-permute-done.11.refs_1_
  31.6 0.1 index_pairs.1
  31.7 0.0 collective-permute-done.2.refs_3_
  31.7 0.0 collective-permute-done.10.refs_2_.refs_5_
  31.7 1.6 %far_late_0.1 = (f32[256,512]{1,0:T(8,128)S(1)}, f32[256,128]{1,0:T(8,128)S(1)}, f32[256,128]{1,0:T(8,128)S(1)}) custom-call(bf16[256,576]{1,0:T(8,128)(2,1)S(1)} %get-tuple-element.73.refs_0_, f32[16,512]{1,0:T(8,128)S(1)} %get-tuple-element.74.refs_1_, bf16[576,512]{1,0:T(8,128)(2,1)S(1)} %collective-permute-done.10.refs_2_.refs_5_, ...), custom_call_target="tpu_custom_call" | custom-call | flops 855638016 | bytes 2883584 | tf_op jit(solution)/shard_map/far_late_0/pallas_call | solution.py:290
  33.3 0.0 copy-start.1
  33.3 0.0 copy-start.4
  33.3 0.0 collective-permute-done.9.refs_5_.refs_2_
  33.3 0.8 %far_last.1 = (bf16[256,512]{1,0:T(8,128)(2,1)S(1)}, f32[2,128]{1,0:T(2,128)S(1)}) custom-call(bf16[256,576]{1,0:T(8,128)(2,1)S(1)} %get-tuple-element.73.refs_0_, f32[16,512]{1,0:T(8,128)S(1)} %get-tuple-element.74.refs_1_, bf16[576,512]{1,0:T(8,128)(2,1)S(1)} %collective-permute-done.9.refs_5_.refs_2_, f32[256,512]{1,0:T(8,128)S(1)} %get-tuple-element.109.refs_3_, ...), custom_call_target="tpu_custom_call" | custom-call | flops 285212672 | bytes 1703936 | tf_op jit(solution)/shard_map/far_last/pallas_call | solution.py:290
  34.1 2.8 %collective-permute-start.13 = (bf16[256,512]{1,0:T(8,128)(2,1)S(1)}, bf16[256,512]{1,0:T(8,128)(2,1)S(1)}, u32[]{:S(2)}, u32[]{:S(2)}) collective-permute-start(bf16[256,512]{1,0:T(8,128)(2,1)S(1)} %get-tuple-element.112), channel_id=1, source_target_pairs={{0,8},{1,9},{2,10},{3,11},{4,12},{5,13},{6,14},{7,15},{8,0},{9,1},... | collective-permute-start | bytes 786440 | tf_op jit(solution)/shard_map/ppermute | solution.py:337
  36.9 0.0 copy-done.1
  36.9 0.0 copy-done.4
  36.9 0.3 unpack_own.1
  37.2 0.5 %index_scores.1 = (f32[4,2048]{1,0:T(4,128)S(1)}, bf16[4,2048]{1,0:T(4,128)(2,1)S(1)}) custom-call(bf16[128,128]{1,0:T(8,128)(2,1)S(1)} %get-tuple-element.91.refs_0_, f32[2,32,16]{2,1,0:T(8,128)S(1)} %get-tuple-element.92.refs_1_, bf16[128,128]{1,0:T(8,128)(2,1)S(1)} %get-tuple-element.93.refs_2_, f32[2,32,16]{2,1,0:T(8,128)S(1)} %get-tuple-element.94.refs_3_, ...), custom_call_target="tpu_custom_call" | custom-call | flops 134217728 | bytes 614400 | tf_op jit(solution)/shard_map/index_scores/pallas_call | solution.py:290
  37.7 1.6 %collective-permute-start.12 = (bf16[4,2048]{1,0:T(4,128)(2,1)S(1)}, bf16[4,2048]{1,0:T(4,128)(2,1)S(1)}, u32[]{:S(2)}, u32[]{:S(2)}) collective-permute-start(bf16[4,2048]{1,0:T(4,128)(2,1)S(1)} %get-tuple-element.100), channel_id=1, source_target_pairs={{0,4},{1,5},{2,6},{3,7},{4,0},{5,1},{6,2},{7,3},{8,12},{9,13},{10,... | collective-permute-start | bytes 49160 | tf_op jit(solution)/shard_map/ppermute | solution.py:337
  39.4 1.9 %own_first.1 = (f32[256,512]{1,0:T(8,128)S(1)}, f32[256,128]{1,0:T(8,128)S(1)}, f32[256,128]{1,0:T(8,128)S(1)}) custom-call(bf16[256,576]{1,0:T(8,128)(2,1)S(1)} %get-tuple-element.63.refs_0_, f32[16,512]{1,0:T(8,128)S(1)} %get-tuple-element.64.refs_1_, bf16[576,512]{1,0:T(8,128)(2,1)S(1)} %get-tuple-element.75.refs_2_, ...), custom_call_target="tpu_custom_call" | custom-call | flops 1140850688 | bytes 2686976 | tf_op jit(solution)/shard_map/own_first/pallas_call | solution.py:290
  41.2 1.9 %collective-permute-done.12.refs_1_ = bf16[4,2048]{1,0:T(4,128)(2,1)S(1)} collective-permute-done((bf16[4,2048]{1,0:T(4,128)(2,1)S(1)}, bf16[4,2048]{1,0:T(4,128)(2,1)S(1)}, u32[]{:S(2)}, u32[]{:S(2)}) %collective-permute-start.12) | collective-permute-done | bytes 16416 | tf_op jit(solution)/shard_map/ppermute | solution.py:337
  43.1 2.4 %collective-permute-start.14 = (bf16[2,4480]{1,0:T(2,128)(2,1)S(1)}, bf16[2,4480]{1,0:T(2,128)(2,1)S(1)}, u32[]{:S(2)}, u32[]{:S(2)}) collective-permute-start(bf16[2,4480]{1,0:T(2,128)(2,1)S(1)} %get-tuple-element.117), channel_id=1, source_target_pairs={{0,8},{1,9},{2,10},{3,11},{4,12},{5,13},{6,14},{7,15},{8,0},{9,1},... | collective-permute-start | bytes 53768 | tf_op jit(solution)/shard_map/ppermute | solution.py:337
  45.6 1.9 %own_late_0.1 = (f32[256,512]{1,0:T(8,128)S(1)}, f32[256,128]{1,0:T(8,128)S(1)}) custom-call(bf16[256,576]{1,0:T(8,128)(2,1)S(1)} %get-tuple-element.63.refs_0_, f32[16,512]{1,0:T(8,128)S(1)} %get-tuple-element.64.refs_1_, bf16[576,512]{1,0:T(8,128)(2,1)S(1)} %collective-permute-done.1.refs_5_.refs_2_, bf16[576,512]{1,0:T(8,128)(2,1)S(1)} %collective-permute-done.2.refs_3_, ...), custom_call_target="tpu_custom_call" | custom-call | flops 1140850688 | bytes 3473408 | tf_op jit(solution)/shard_map/own_late_0/pallas_call | solution.py:290
  47.5 2.1 %collective-permute-done.14.far_ref = bf16[2,4480]{1,0:T(2,128)(2,1)S(1)} collective-permute-done((bf16[2,4480]{1,0:T(2,128)(2,1)S(1)}, bf16[2,4480]{1,0:T(2,128)(2,1)S(1)}, u32[]{:S(2)}, u32[]{:S(2)}) %collective-permute-start.14) | collective-permute-done | bytes 17952 | tf_op jit(solution)/shard_map/ppermute | solution.py:337
  49.6 0.0 collective-permute-done.13.wire_ref
  49.7 1.0 %finish.1 = (f32[2,8192]{1,0:T(2,128)}, bf16[2,128,512]{2,1,0:T(8,128)(2,1)}) custom-call(f32[256,512]{1,0:T(8,128)S(1)} %get-tuple-element.107.o_ref, f32[256,128]{1,0:T(8,128)S(1)} %get-tuple-element.108.lse_ref, bf16[256,512]{1,0:T(8,128)(2,1)S(1)} %collective-permute-done.13.wire_ref, f32[2,4096]{1,0:T(2,128)S(1)} %get-tuple-element.116.own_ref, ...), custom_call_target="tpu_custom_call" | custom-call | flops 524288 | bytes 968192 | tf_op jit(solution)/shard_map/finish/pallas_call | solution.py:290
  (1 shorter events, 0.0 us)
Async XLA Ops:
  0.6 14.5 %collective-permute-start.7 = (bf16[576,512]{1,0:T(8,128)(2,1)}, bf16[576,512]{1,0:T(8,128)(2,1)S(1)}, u32[]{:S(2)}, u32[]{:S(2)}) collective-permute-start(bf16[576,512]{1,0:T(8,128)(2,1)} %bitcast.9), channel_id=1, source_target_pairs={{0,2},{1,5},{2,0},{3,7},{4,6},{5,1},{6,4},{7,3},{8,10},{9,13},{10,... | collective-permute-start | bytes 1769480 | tf_op jit(solution)/shard_map/ppermute | solution.py:337
  5.9 18.4 %collective-permute-start.1 = (bf16[576,512]{1,0:T(8,128)(2,1)}, bf16[576,512]{1,0:T(8,128)(2,1)S(1)}, u32[]{:S(2)}, u32[]{:S(2)}) collective-permute-start(bf16[576,512]{1,0:T(8,128)(2,1)} %bitcast.10), channel_id=1, source_target_pairs={{0,4},{1,3},{2,6},{3,1},{4,0},{5,7},{6,2},{7,5},{8,12},{9,11},{10,... | collective-permute-start | bytes 1769480 | tf_op jit(solution)/shard_map/ppermute | solution.py:337
  7.6 16.2 %collective-permute-start = (bf16[1296,128]{1,0:T(8,128)(2,1)}, bf16[1296,128]{1,0:T(8,128)(2,1)S(1)}, u32[]{:S(2)}, u32[]{:S(2)}) collective-permute-start(bf16[1296,128]{1,0:T(8,128)(2,1)} %get-tuple-element.61.refs_0_), channel_id=1, source_target_pairs={{0,8},{1,9},{2,10},{3,11},{4,12},{5,13},{6,14},{7,15},{8,0},{9,1},... | collective-permute-start | bytes 995336 | tf_op jit(solution)/shard_map/ppermute | solution.py:337
  10.2 8.7 %collective-permute-start.4 = (bf16[528,128]{1,0:T(8,128)(2,1)}, bf16[528,128]{1,0:T(8,128)(2,1)S(1)}, u32[]{:S(2)}, u32[]{:S(2)}) collective-permute-start(bf16[528,128]{1,0:T(8,128)(2,1)} %get-tuple-element.69.k_in), channel_id=1, source_target_pairs={{0,2},{1,3},{2,0},{3,1},{4,6},{5,7},{6,4},{7,5},{8,10},{9,11},{10,... | collective-permute-start | bytes 405512 | tf_op jit(solution)/shard_map/ppermute | solution.py:337
  10.7 1.1 %copy-start = (bf16[512,576]{0,1:T(8,128)(2,1)S(1)}, bf16[512,576]{0,1:T(8,128)(2,1)}, u32[]{:S(2)}) copy-start(bf16[512,576]{0,1:T(8,128)(2,1)} %param.13) | copy-start | bytes 1769476
  11.7 0.9 %copy-start.2 = (bf16[528,128]{1,0:T(8,128)(2,1)S(1)}, bf16[528,128]{1,0:T(8,128)(2,1)}, u32[]{:S(2)}) copy-start(bf16[528,128]{1,0:T(8,128)(2,1)} %get-tuple-element.69.k_in) | copy-start | bytes 405508
  12.7 0.7 %copy-start.3 = (bf16[80,128]{1,0:T(8,128)(2,1)S(1)}, bf16[80,128]{1,0:T(8,128)(2,1)}, u32[]{:S(2)}) copy-start(bf16[80,128]{1,0:T(8,128)(2,1)} %get-tuple-element.68.i_in) | copy-start | bytes 61444
  13.7 15.1 %collective-permute-start.6 = (bf16[576,512]{1,0:T(8,128)(2,1)S(1)}, bf16[576,512]{1,0:T(8,128)(2,1)S(1)}, u32[]{:S(2)}, u32[]{:S(2)}) collective-permute-start(bf16[576,512]{1,0:T(8,128)(2,1)S(1)} %get-tuple-element.75.refs_2_), channel_id=1, source_target_pairs={{0,1},{1,0},{2,3},{3,2},{4,5},{5,4},{6,7},{7,6},{8,9},{9,8},{10,11... | collective-permute-start | bytes 1769480 | tf_op jit(solution)/shard_map/ppermute | solution.py:337
  15.1 16.0 %collective-permute-start.8 = (bf16[576,512]{1,0:T(8,128)(2,1)S(1)}, bf16[576,512]{1,0:T(8,128)(2,1)S(1)}, u32[]{:S(2)}, u32[]{:S(2)}) collective-permute-start(bf16[576,512]{1,0:T(8,128)(2,1)S(1)} %collective-permute-done.7.refs_4_), channel_id=1, source_target_pairs={{0,4},{1,3},{2,6},{3,1},{4,0},{5,7},{6,2},{7,5},{8,12},{9,11},{10,... | collective-permute-start | bytes 1769480 | tf_op jit(solution)/shard_map/ppermute | solution.py:337
  18.9 5.5 %collective-permute-start.3 = (bf16[528,128]{1,0:T(8,128)(2,1)S(1)}, bf16[528,128]{1,0:T(8,128)(2,1)S(1)}, u32[]{:S(2)}, u32[]{:S(2)}) collective-permute-start(bf16[528,128]{1,0:T(8,128)(2,1)S(1)} %copy-done.2), channel_id=1, source_target_pairs={{0,1},{1,0},{2,3},{3,2},{4,5},{5,4},{6,7},{7,6},{8,9},{9,8},{10,11... | collective-permute-start | bytes 405512 | tf_op jit(solution)/shard_map/ppermute | solution.py:337
  23.7 1.4 %collective-permute-start.5 = (bf16[528,128]{1,0:T(8,128)(2,1)S(1)}, bf16[528,128]{1,0:T(8,128)(2,1)S(1)}, u32[]{:S(2)}, u32[]{:S(2)}) collective-permute-start(bf16[528,128]{1,0:T(8,128)(2,1)S(1)} %collective-permute-done.4.refs_6_), channel_id=1, source_target_pairs={{0,1},{1,0},{2,3},{3,2},{4,5},{5,4},{6,7},{7,6},{8,9},{9,8},{10,11... | collective-permute-start | bytes 405512 | tf_op jit(solution)/shard_map/ppermute | solution.py:337
  24.4 7.3 %collective-permute-start.2 = (bf16[576,512]{1,0:T(8,128)(2,1)S(1)}, bf16[576,512]{1,0:T(8,128)(2,1)S(1)}, u32[]{:S(2)}, u32[]{:S(2)}) collective-permute-start(bf16[576,512]{1,0:T(8,128)(2,1)S(1)} %collective-permute-done.1.refs_5_.refs_2_), channel_id=1, source_target_pairs={{0,1},{1,0},{2,3},{3,2},{4,5},{5,4},{6,7},{7,6},{8,9},{9,8},{10,11... | collective-permute-start | bytes 1769480 | tf_op jit(solution)/shard_map/ppermute | solution.py:337
  25.4 6.2 %collective-permute-start.11 = (bf16[160,128]{1,0:T(8,128)(2,1)S(1)}, bf16[160,128]{1,0:T(8,128)(2,1)S(1)}, u32[]{:S(2)}, u32[]{:S(2)}) collective-permute-start(bf16[160,128]{1,0:T(8,128)(2,1)S(1)} %get-tuple-element.86.refs_0_), channel_id=1, source_target_pairs={{0,4},{1,5},{2,6},{3,7},{4,0},{5,1},{6,2},{7,3},{8,12},{9,13},{10,... | collective-permute-start | bytes 122888 | tf_op jit(solution)/shard_map/ppermute | solution.py:337
  28.8 2.9 %collective-permute-start.10 = (bf16[576,512]{1,0:T(8,128)(2,1)S(1)}, bf16[576,512]{1,0:T(8,128)(2,1)S(1)}, u32[]{:S(2)}, u32[]{:S(2)}) collective-permute-start(bf16[576,512]{1,0:T(8,128)(2,1)S(1)} %collective-permute-done.7.refs_4_), channel_id=1, source_target_pairs={{0,1},{1,0},{2,3},{3,2},{4,5},{5,4},{6,7},{7,6},{8,9},{9,8},{10,11... | collective-permute-start | bytes 1769480 | tf_op jit(solution)/shard_map/ppermute | solution.py:337
  31.1 2.2 %collective-permute-start.9 = (bf16[576,512]{1,0:T(8,128)(2,1)S(1)}, bf16[576,512]{1,0:T(8,128)(2,1)S(1)}, u32[]{:S(2)}, u32[]{:S(2)}) collective-permute-start(bf16[576,512]{1,0:T(8,128)(2,1)S(1)} %collective-permute-done.8.refs_4_), channel_id=1, source_target_pairs={{0,1},{1,0},{2,3},{3,2},{4,5},{5,4},{6,7},{7,6},{8,9},{9,8},{10,11... | collective-permute-start | bytes 1769480 | tf_op jit(solution)/shard_map/ppermute | solution.py:337
  33.3 3.6 %copy-start.1 = (bf16[1296,128]{1,0:T(8,128)(2,1)S(1)}, bf16[1296,128]{1,0:T(8,128)(2,1)}, u32[]{:S(2)}) copy-start(bf16[1296,128]{1,0:T(8,128)(2,1)} %get-tuple-element.61.refs_0_) | copy-start | bytes 995332
  33.3 3.6 %copy-start.4 = (bf16[64,128]{1,0:T(8,128)(2,1)S(1)}, bf16[64,128]{1,0:T(8,128)(2,1)}, u32[]{:S(2)}) copy-start(bf16[64,128]{1,0:T(8,128)(2,1)} %get-tuple-element.62.refs_1_) | copy-start | bytes 49156
  34.1 15.6 %collective-permute-start.13 = (bf16[256,512]{1,0:T(8,128)(2,1)S(1)}, bf16[256,512]{1,0:T(8,128)(2,1)S(1)}, u32[]{:S(2)}, u32[]{:S(2)}) collective-permute-start(bf16[256,512]{1,0:T(8,128)(2,1)S(1)} %get-tuple-element.112), channel_id=1, source_target_pairs={{0,8},{1,9},{2,10},{3,11},{4,12},{5,13},{6,14},{7,15},{8,0},{9,1},... | collective-permute-start | bytes 786440 | tf_op jit(solution)/shard_map/ppermute | solution.py:337
  37.7 5.4 %collective-permute-start.12 = (bf16[4,2048]{1,0:T(4,128)(2,1)S(1)}, bf16[4,2048]{1,0:T(4,128)(2,1)S(1)}, u32[]{:S(2)}, u32[]{:S(2)}) collective-permute-start(bf16[4,2048]{1,0:T(4,128)(2,1)S(1)} %get-tuple-element.100), channel_id=1, source_target_pairs={{0,4},{1,5},{2,6},{3,7},{4,0},{5,1},{6,2},{7,3},{8,12},{9,13},{10,... | collective-permute-start | bytes 49160 | tf_op jit(solution)/shard_map/ppermute | solution.py:337
  43.1 6.5 %collective-permute-start.14 = (bf16[2,4480]{1,0:T(2,128)(2,1)S(1)}, bf16[2,4480]{1,0:T(2,128)(2,1)S(1)}, u32[]{:S(2)}, u32[]{:S(2)}) collective-permute-start(bf16[2,4480]{1,0:T(2,128)(2,1)S(1)} %get-tuple-element.117), channel_id=1, source_target_pairs={{0,8},{1,9},{2,10},{3,11},{4,12},{5,13},{6,14},{7,15},{8,0},{9,1},... | collective-permute-start | bytes 53768 | tf_op jit(solution)/shard_map/ppermute | solution.py:337
